TPU v7x, 32 devices: a whole 2x2x4 slice. The times are simulated.
32 devices in a mesh: req: 8 (over z, y), tp: 4 (over x, core).
Axes of the slice: x: 2, y: 2, z: 4, core: 2. Of those that a mesh axis runs over, the one named last changes fastest.
Arguments:
- drafts: bfloat16 [16, 64, 1536], P('req'), may hold values from -27 to 27, as said below
- gain_attn: float32 [1536], replicated, may hold values from 0.1 to 1.9
- w_query: bfloat16 [1536, 1536], P(None, 'tp'), may hold values from -0.15625 to 0.15625
- key_value_weight: bfloat16 [1536, 512], replicated, may hold values from -0.15625 to 0.15625
- w_output: bfloat16 [1536, 1536], P('tp'), may hold values from -0.5 to 0.5
- cache: bfloat16 [16, 2, 2, 3072, 128], P('req'), may hold values from -130 to 130, as said below
- lengths: int32 [16], P('req'), may hold values from 1 to 3072, 16384 in all
- tree_mask: int32 [16, 64, 64], P('req'), may hold values from 0 to 1, as said below
- depths: int32 [16, 64], P('req'), may hold values from 0 to 63, as said below
- gain_moe: float32 [1536], replicated, may hold values from 0.1 to 1.9
- w_router: bfloat16 [1536, 32], replicated, may hold values from -0.15625 to 0.15625
- expert_ids: int32 [16, 64, 4], P('req'), may hold values from 0 to 31, all different within a row; in each aligned block of 128 rows (0 to 127, 128 to 255, ..., all dimensions but the last counted through in order) at most 32 rows name the same one
- w_in: bfloat16 [64, 1536, 2, 384], P('req'), may hold values from -0.15625 to 0.15625
- w_out: bfloat16 [64, 384, 1536], P('req'), may hold values from -0.21875 to 0.21875
- slots: int32 [16, 64], P('req'), may hold values from -1 to 15, as said below
- order: int32 [16], P('req'), may hold values from 0 to 15, each once
Outputs:
- tree_out: bfloat16 [16, 64, 1536], P('req', None, 'tp')
- accepted: bfloat16 [16, 16, 1536], P('req', None, 'tp')
Inputs may be any that keep to these rules, and one draw needn't show every extreme that they name: `drafts`: values lie within this range. `cache`: values lie within this range. `tree_mask`: each request's tokens form a tree rooted at token 0, the parent of token t being one of tokens t - 4 to t - 1; entry [s, i, j] is 1 exactly when j is i or an ancestor of i. `depths`: depth of each token in its tree, agreeing with tree_mask; the root has depth 0. In every draw some request's tree is a single chain. In each request the tokens on the path from the root to one token of depth d carry slots 0 to d (their depths), with d + 1 <= 16; all other tokens carry -1. In every draw some request fills all 16 slots. `expert_ids`: each token names 4 different experts; among the tokens of one device no expert is named by more than 32 tokens. `order`: each request is served in exactly one serving slot.
All inputs are finite; a program needn't handle non-finite values. No bound on the sum of `lengths` on one device may be relied on, other than what follows from the above.
Results may differ from a plain program's by a relative error of at most 0.011.
Values may be sent and summed in bfloat16 or wider, within the bound.
No kernel may reach another device: no remote copies, remote signals or barrier semaphores. Data moves between devices by JAX's collectives and lax.ppermute only.
A program may use at most 128 MiB of HBM per device.

v0:
```python
import jax
import jax.numpy as jnp
from jax import lax
from jax.sharding import PartitionSpec as P

KEEP = 16
CAP = 32


EPSILON = 1e-06
THETA = 1000000.0


def rms_norm(values, gain_vec):
    return (
        values * lax.rsqrt(jnp.mean(values * values, axis=-1, keepdims=True) + EPSILON) * gain_vec
    )


def rotary(values, positions):
    half_dim = values.shape[-1] // 2
    freqs = jnp.exp(-jnp.log(THETA) * jnp.arange(half_dim, dtype=jnp.float32) / half_dim)
    angles = positions.astype(jnp.float32)[..., None] * freqs
    cosine = jnp.cos(angles)
    sine = jnp.sin(angles)
    first = values[..., :half_dim]
    second = values[..., half_dim:]
    return jnp.concatenate(
        [first * cosine - second * sine, second * cosine + first * sine], axis=-1
    )


def inner_rows(left, right):
    return lax.dot_general(
        left, right, (((1,), (1,)), ((), ())), preferred_element_type=jnp.float32
    )


def cache_block(cache, request, which, kv_head, offset, block_len):
    head_dim = cache.shape[-1]
    found = lax.dynamic_slice(
        cache, (request, which, kv_head, offset, 0), (1, 1, 1, block_len, head_dim)
    )
    return found.reshape(block_len, head_dim)


def block_scores(cache, queries, request, kv_head, offset, block_len, limit, scale):
    keys_blk = cache_block(cache, request, 0, kv_head, offset, block_len)
    scores = inner_rows(queries, keys_blk) * scale
    inside = offset + jnp.arange(block_len) < limit
    return jnp.where(inside[None, :], scores, -jnp.inf)


def attend_request(cache, queries, key_tree, val_tree, allowed, limit, request, kv_head, scale):
    block_len = min(512, cache.shape[3])
    tree_scores = jnp.where(allowed, inner_rows(queries, key_tree) * scale, -jnp.inf)
    count_blocks = (limit + block_len - 1) // block_len

    def max_step(blk_index, running):
        scores = block_scores(
            cache, queries, request, kv_head, blk_index * block_len, block_len, limit, scale
        )
        return jnp.maximum(running, jnp.max(scores, axis=1))

    peak = lax.fori_loop(0, count_blocks, max_step, jnp.max(tree_scores, axis=1))
    tree_weights = jnp.exp(tree_scores - peak[:, None])
    start_carry = (
        jnp.sum(tree_weights, axis=1),
        jnp.dot(tree_weights.astype(jnp.bfloat16), val_tree, preferred_element_type=jnp.float32),
    )

    def sum_step(blk_index, carry):
        weight_sum, accum = carry
        offset = blk_index * block_len
        scores = block_scores(cache, queries, request, kv_head, offset, block_len, limit, scale)
        weights = jnp.exp(scores - peak[:, None])
        vals_blk = cache_block(cache, request, 1, kv_head, offset, block_len)
        return (
            weight_sum + jnp.sum(weights, axis=1),
            accum
            + jnp.dot(weights.astype(jnp.bfloat16), vals_blk, preferred_element_type=jnp.float32),
        )

    weight_sum, accum = lax.fori_loop(0, count_blocks, sum_step, start_carry)
    return (accum / weight_sum[:, None]).astype(jnp.bfloat16)


def on_device(
    drafts,
    gain_attn,
    w_query,
    key_value_weight,
    w_output,
    cache,
    lengths,
    tree_mask,
    depths,
    gain_moe,
    w_router,
    expert_ids,
    w_in,
    w_out,
    slots,
    order,
):
    req_dev, draft_tree, width = drafts.shape
    head_dim = cache.shape[-1]
    kv_heads = cache.shape[2]
    local_heads = w_query.shape[1] // head_dim
    tp_count = lax.axis_size("tp")
    req_count = lax.axis_size("req")
    tp_rank = lax.axis_index("tp")
    head_group = local_heads * tp_count // kv_heads
    kv_head = tp_rank * local_heads // head_group
    scale = head_dim ** (-0.5)
    tokens = req_dev * draft_tree
    inputs = drafts.astype(jnp.float32).reshape(tokens, width)
    normalized_input = rms_norm(inputs, gain_attn).astype(jnp.bfloat16)
    positions = lengths[:, None] + depths
    query_rot = jnp.dot(normalized_input, w_query, preferred_element_type=jnp.float32).reshape(
        req_dev, draft_tree, local_heads, head_dim
    )
    query_rot = rotary(query_rot, positions[:, :, None]).astype(jnp.bfloat16)
    key_value = jnp.dot(
        normalized_input, key_value_weight, preferred_element_type=jnp.float32
    ).reshape(req_dev, draft_tree, 2, kv_heads, head_dim)
    keyval_own = lax.dynamic_index_in_dim(key_value, kv_head, 3, keepdims=False)
    key_new = rotary(keyval_own[:, :, 0], positions).astype(jnp.bfloat16)
    val_new = keyval_own[:, :, 1].astype(jnp.bfloat16)
    head_rows = []
    for request in range(req_dev):
        queries = query_rot[request].transpose(1, 0, 2).reshape(local_heads * draft_tree, head_dim)
        allowed = jnp.tile(tree_mask[request] > 0, (local_heads, 1))
        mixed = attend_request(
            cache,
            queries,
            key_new[request],
            val_new[request],
            allowed,
            lengths[request],
            request,
            kv_head,
            scale,
        )
        head_rows.append(
            mixed.reshape(local_heads, draft_tree, head_dim)
            .transpose(1, 0, 2)
            .reshape(draft_tree, local_heads * head_dim)
        )
    heads = jnp.concatenate(head_rows, axis=0)
    attn = lax.psum(
        jnp.dot(heads, w_output, preferred_element_type=jnp.float32).astype(jnp.bfloat16), "tp"
    ).astype(jnp.float32)
    resid = inputs + attn
    normed2 = rms_norm(resid, gain_moe).astype(jnp.bfloat16)
    experts = w_router.shape[1]
    logits = jnp.dot(normed2, w_router, preferred_element_type=jnp.float32)
    ids = expert_ids.reshape(tokens, -1)
    picks = ids[:, :, None] == jnp.arange(experts)[None, None, :]
    chosen = jax.nn.sigmoid(jnp.sum(jnp.where(picks, logits[:, None, :], 0.0), axis=-1))
    gates = (chosen / jnp.sum(chosen, axis=1, keepdims=True)).astype(jnp.bfloat16)
    counts = jnp.sum(picks.astype(jnp.int32), axis=1)
    slot_expert = jnp.cumsum(counts, axis=0) - counts
    slot_pick = jnp.sum(jnp.where(picks, slot_expert[:, None, :], 0), axis=-1)
    share = CAP // tp_count
    first_slot = tp_rank * share
    cap_index = first_slot + jnp.arange(share)
    dispatch_mat = (
        (counts.T[:, None, :] == 1) & (slot_expert.T[:, None, :] == cap_index[None, :, None])
    ).astype(jnp.bfloat16)
    sent = jnp.einsum(
        "ect,td->ecd", dispatch_mat, normed2, preferred_element_type=jnp.float32
    ).astype(jnp.bfloat16)
    pieces = w_in.shape[0]
    outgoing = jnp.repeat(sent, 2, axis=0).reshape(req_count, pieces, share, width)
    arrived = lax.all_to_all(outgoing, "req", split_axis=0, concat_axis=0, tiled=True)
    rows_in = arrived.transpose(1, 0, 2, 3).reshape(pieces, req_count * share, width)
    gate_up = jnp.einsum("prd,pdgf->prgf", rows_in, w_in, preferred_element_type=jnp.float32)
    act = (jax.nn.relu(gate_up[:, :, 0]) * gate_up[:, :, 1]).astype(jnp.bfloat16)
    produced = jnp.einsum("prf,pfd->prd", act, w_out, preferred_element_type=jnp.float32).astype(
        jnp.bfloat16
    )
    outbound = produced.reshape(pieces, req_count, share, width).transpose(1, 0, 2, 3)
    returned = lax.all_to_all(outbound, "req", split_axis=0, concat_axis=0, tiled=True)
    expert_rows = returned.reshape(experts * 2 * share, width)
    local_slot = slot_pick - first_slot
    owned = (local_slot >= 0) & (local_slot < share)
    target = jnp.where(owned, ids * share + local_slot, -1)
    combine_one = jnp.sum(
        jnp.where(
            target[:, :, None] == jnp.arange(experts * share)[None, None, :],
            gates[:, :, None],
            jnp.zeros((), jnp.bfloat16),
        ),
        axis=1,
    )
    combine = jnp.broadcast_to(
        combine_one.reshape(tokens, experts, 1, share), (tokens, experts, 2, share)
    ).reshape(tokens, experts * 2 * share)
    quarter = width // tp_count
    mixture = lax.psum_scatter(
        lax.dot_general(
            expert_rows, combine, (((0,), (1,)), ((), ())), preferred_element_type=jnp.float32
        ).astype(jnp.bfloat16),
        "tp",
        scatter_dimension=0,
        tiled=True,
    ).astype(jnp.float32)
    own_resid = lax.dynamic_slice_in_dim(resid, tp_rank * quarter, quarter, 1)
    tree_out = (own_resid + mixture.T).astype(jnp.bfloat16).reshape(req_dev, draft_tree, quarter)
    selector = (slots[:, None, :] == jnp.arange(KEEP)[None, :, None]).astype(jnp.bfloat16)
    kept_rows = jnp.einsum(
        "rkt,rtd->rkd", selector, tree_out, preferred_element_type=jnp.float32
    ).astype(jnp.bfloat16)
    destination = (order[:, None] == jnp.arange(req_count * req_dev)[None, :]).astype(jnp.bfloat16)
    posted = jnp.einsum(
        "rg,rkd->gkd", destination, kept_rows, preferred_element_type=jnp.float32
    ).astype(jnp.bfloat16)
    received = lax.all_to_all(
        posted.reshape(req_count, req_dev, KEEP, quarter),
        "req",
        split_axis=0,
        concat_axis=0,
        tiled=True,
    )
    accepted = jnp.sum(received.astype(jnp.float32), axis=0).astype(jnp.bfloat16)
    return (tree_out, accepted)


def solution(mesh):
    placed = (
        P("req", None, None),
        P(),
        P(None, "tp"),
        P(),
        P("tp", None),
        P("req", None, None, None, None),
        P("req"),
        P("req", None, None),
        P("req", None),
        P(),
        P(),
        P("req", None, None),
        P("req", None, None, None),
        P("req", None, None),
        P("req", None),
        P("req"),
    )
    return jax.shard_map(
        on_device,
        mesh=mesh,
        in_specs=placed,
        out_specs=(P("req", None, "tp"), P("req", None, "tp")),
        check_vma=False,
    )
```

profile of v0, /device:TPU:0, one launch (start us, length us, event | category | flops | bytes accessed | tf_op | source)
XLA Modules:
  0.0 238.1 jit_solution(9760772846952538633)
XLA Ops:
  7.3 1.4 fusion.95
  10.8 2.5 %copy.63 = bf16[1536,384]{0,1:T(8,128)(2,1)} copy(bf16[1536,384]{1,0:T(8,128)(2,1)} %param.26) | data formatting | bytes 2359296 | tf_op args[2]
  13.5 1.7 copy.86
  15.2 1.8 fusion.47
  17.0 1.3 fusion.45
  20.2 11.2 %while.54 = (s32[]{:T(128)}, f32[192]{0:T(256)S(1)}, s32[]{:T(128)}, s32[]{:T(128)}, bf16[2,2,2,3072,128]{4,3,2,1,0:T(8,128)(2,1)}, /*index=5*/s32[]{:T(128)}, b...) while((s32[]{:T(128)}, f32[192]{0:T(256)S(1)}, s32[]{:T(128)}, ...), condition=%wide.region_12.13_spmd, body=%wide.region_10.12_spmd.sunk | while | flops 25461764 | bytes 185007 | solution.py:65
  32.0 3.8 %while.52 = (s32[]{:T(128)}, f32[192]{0:T(256)S(1)}, s32[]{:T(128)}, s32[]{:T(128)}, bf16[2,2,2,3072,128]{4,3,2,1,0:T(8,128)(2,1)}, /*index=5*/s32[]{:T(128)}, b...) while((s32[]{:T(128)}, f32[192]{0:T(256)S(1)}, s32[]{:T(128)}, ...), condition=%wide.region_4.5_spmd, body=%wide.region_2.4_spmd.sunk | while | flops 25461764 | bytes 185007 | solution.py:65
  36.1 18.1 %while.55 = (s32[]{:T(128)}, f32[192]{0:T(256)S(1)}, f32[192,128]{1,0:T(8,128)S(1)}, s32[]{:T(128)}, s32[]{:T(128)}, /*index=5*/bf16[2,2,2,3072,128]{4,3,2,1,0:T...) while((s32[]{:T(128)}, f32[192]{0:T(256)S(1)}, ...), condition=%wide.region_16.17_spmd, body=%wide.region_14.16_spmd.sunk | while | flops 50848772 | bytes 907203 | solution.py:84
  36.7 1.3 fusion.142
  42.7 1.3 fusion.142
  48.8 1.3 fusion.142
  54.4 6.1 %while.53 = (s32[]{:T(128)}, f32[192]{0:T(256)S(1)}, f32[192,128]{1,0:T(8,128)S(1)}, s32[]{:T(128)}, s32[]{:T(128)}, /*index=5*/bf16[2,2,2,3072,128]{4,3,2,1,0:T...) while((s32[]{:T(128)}, f32[192]{0:T(256)S(1)}, ...), condition=%wide.region_8.9_spmd, body=%wide.region_6.8_spmd.sunk | while | flops 50848772 | bytes 907203 | solution.py:84
  55.0 1.3 fusion.135
  63.3 30.0 %all-reduce.2.cloned.1.call-done = bf16[128,1536]{1,0:T(8,128)(2,1)} async-done(((bf16[128,1536]{1,0:T(8,128)(2,1)}), bf16[128,1536]{1,0:T(8,128)(2,1)}) %all-reduce.2.cloned.1.call-update) | async-done | bytes 393232 | tf_op jit(solution)/shard_map/psum | solution.py:151
  95.1 41.5 %all_to_all.15 = bf16[8,8,8,1536]{3,2,1,0:T(8,128)(2,1)S(1)} all-to-all(bf16[8,8,8,1536]{3,2,1,0:T(8,128)(2,1)S(1)} %bitcast.181), channel_id=1, replica_groups=mesh['req'=8,'tp'=4] {'req'}, dimensions={0} | all-to-all | bytes 3145728 | tf_op jit(solution)/shard_map/all_to_all | solution.py:176
  136.6 12.3 %fusion.34 = f32[8,64,2,384]{3,1,2,0:T(8,128)} fusion(bf16[8,1536,2,384]{3,2,1,0:T(2,128)(2,1)} %param.36, bf16[8,8,8,1536]{3,2,1,0:T(8,128)(2,1)S(1)} %all_to_all.15), kind=kOutput, calls=%fused_computation.44 | convolution fusion | flops 1207959552 | bytes 22020096 | tf_op jit(solution)/shard_map/prd,pdgf->prgf/dot_general | solution.py:178
  149.0 3.2 %fusion.36 = bf16[8,8,8,1536]{3,2,1,0:T(8,128)(2,1)S(1)} fusion(bf16[8,384,1536]{2,1,0:T(8,128)(2,1)S(1)} %bitcast.177, f32[8,64,2,384]{3,1,2,0:T(8,128)} %fusion.34), kind=kOutput, calls=%fused_computation.47 | convolution fusion | flops 605356032 | bytes 12582912 | tf_op jit(solution)/shard_map/prf,pfd->prd/dot_general | solution.py:180
  152.2 1.3 copy.103
  153.4 3.6 %all-to-all-start.1 = ((bf16[8,8,8,1536]{3,2,1,0:T(8,128)(2,1)}), bf16[8,8,8,1536]{3,2,1,0:T(8,128)(2,1)S(1)}, u32[]{:S(2)}, u32[]{:S(2)}) async-start(bf16[8,8,8,1536]{3,2,1,0:T(8,128)(2,1)} %bitcast.179), calls=%async_computation.1 | async-start | bytes 3145728 | tf_op jit(solution)/shard_map/all_to_all | solution.py:184
  162.2 1.6 copy.77
  163.8 29.7 %all-to-all-done.1 = bf16[8,8,8,1536]{3,2,1,0:T(8,128)(2,1)S(1)} async-done(((bf16[8,8,8,1536]{3,2,1,0:T(8,128)(2,1)}), bf16[8,8,8,1536]{3,2,1,0:T(8,128)(2,1)S(1)}, u32[]{:S(2)}, u32[]{:S(2)}) %all-to-all-start.1) | async-done | bytes 1572896 | tf_op jit(solution)/shard_map/all_to_all | solution.py:184
  194.4 1.4 convolution_convert_fusion.2
  195.8 19.6 %reduce-scatter.4.cloned.1.call-done = bf16[384,128]{1,0:T(8,128)(2,1)} async-done(((bf16[1536,128]{1,0:T(8,128)(2,1)}), bf16[384,128]{1,0:T(8,128)(2,1)}) %reduce-scatter.4.cloned.1.call-update) | async-done | bytes 98320
  217.2 13.3 %all_to_all.16 = bf16[8,2,16,384]{3,1,2,0:T(2,128)(2,1)S(1)} all-to-all(bf16[8,2,16,384]{3,1,2,0:T(2,128)(2,1)S(1)} %copy.80), channel_id=1, replica_groups=mesh['req'=8,'tp'=4] {'req'}, dimensions={0} | all-to-all | bytes 393216 | tf_op jit(solution)/shard_map/all_to_all | solution.py:219
  (145 shorter events, 50.6 us)
Async XLA Ops:
  7.2 53.5 %copy-start = (bf16[384,1536]{1,0:T(8,128)(2,1)S(1)}, bf16[384,1536]{1,0:T(8,128)(2,1)}, u32[]{:S(2)}) copy-start(bf16[384,1536]{1,0:T(8,128)(2,1)} %param.28) | copy-start | bytes 3538948
  7.2 6.1 %copy-start.1 = (bf16[2,64,1536]{2,1,0:T(8,128)(2,1)S(1)}, bf16[2,64,1536]{2,1,0:T(8,128)(2,1)}, u32[]{:S(2)}) copy-start(bf16[2,64,1536]{2,1,0:T(8,128)(2,1)} %param.24) | copy-start | bytes 1179652
  7.2 86.1 %all-reduce.2.cloned.1.call-start = ((), (), s32[]{:S(2)}) async-start(), calls=%async_computation.4 | async-start | bytes 786432 | tf_op jit(solution)/shard_map/psum | solution.py:151
  13.5 1.7 copy-start.4
  17.0 2.3 copy-start.7
  17.0 2.3 copy-start.11
  60.5 1.4 copy-start.8
  61.8 32.7 %copy-start.6 = (f32[1536]{0:T(1024)S(1)}, f32[1536]{0:T(1024)}, u32[]{:S(2)}) copy-start(f32[1536]{0:T(1024)} %param.33) | copy-start | bytes 18436
  61.9 0.6 copy-start.5
  62.7 0.6 copy-start.2
  94.5 0.6 copy-start.9
  95.1 53.9 %slice-start = ((s8[9437184]{0:T(1024)(128)(4,1)}), s8[4194304]{0:T(1024)(128)(4,1)S(1)}, s32[]{:S(2)}) async-start(s8[9437184]{0:T(1024)(128)(4,1)} %bitcast.176), calls=%async_computation.6 | async-start | bytes 8388608
  136.6 12.4 %slice-start.1 = ((s8[9437184]{0:T(1024)(128)(4,1)}), s8[4194304]{0:T(1024)(128)(4,1)S(1)}, s32[]{:S(2)}) async-start(s8[9437184]{0:T(1024)(128)(4,1)} %bitcast.176), calls=%async_computation.7 | async-start | bytes 8388608
  136.6 12.4 %slice-start.2 = ((s8[9437184]{0:T(1024)(128)(4,1)}), s8[1048576]{0:T(1024)(128)(4,1)S(1)}, s32[]{:S(2)}) async-start(s8[9437184]{0:T(1024)(128)(4,1)} %bitcast.176), calls=%async_computation.8 | async-start | bytes 2097152
  153.4 40.1 %all-to-all-start.1 = ((bf16[8,8,8,1536]{3,2,1,0:T(8,128)(2,1)}), bf16[8,8,8,1536]{3,2,1,0:T(8,128)(2,1)S(1)}, u32[]{:S(2)}, u32[]{:S(2)}) async-start(bf16[8,8,8,1536]{3,2,1,0:T(8,128)(2,1)} %bitcast.179), calls=%async_computation.1 | async-start | bytes 3145728 | tf_op jit(solution)/shard_map/all_to_all | solution.py:184
  157.0 58.4 %reduce-scatter.4.cloned.1.call-start = ((), (), s32[]{:S(2)}) async-start(), calls=%async_computation.5 | async-start | bytes 491520
  194.4 22.1 %copy-start.10 = (s32[2,64]{1,0:T(2,128)S(1)}, s32[2,64]{1,0:T(2,128)}, u32[]{:S(2)}) copy-start(s32[2,64]{1,0:T(2,128)} %param.38) | copy-start | bytes 1540
  194.4 22.2 %copy-start.12 = (s32[2]{0:T(128)S(1)}, s32[2]{0:T(128)}, u32[]{:S(2)}) copy-start(s32[2]{0:T(128)} %param.39) | copy-start | bytes 28
  216.5 14.8 %copy-start.3 = (bf16[128,384]{1,0:T(8,128)(2,1)}, bf16[128,384]{1,0:T(8,128)(2,1)S(1)}, u32[]{:S(2)}) copy-start(bf16[128,384]{1,0:T(8,128)(2,1)S(1)} %fusion.52) | copy-start | bytes 294916
Sparse Core Ops, SparseCore 0:
  61.9 31.2 all-reduce.1
  195.9 19.4 reduce-scatter.3
where the time goes:
time: 238 us
  waiting for transfers between devices  79.3 us (33%)
  blocking collectives  54.8 us (23%)
  matrix products  52.7 us (22%)
  other arithmetic  17.4 us (7%)
  between operations  15.8 us (7%)
  local copies, waits for them, and re-layouts  13.8 us (6%)
  starting transfers between devices  3.66 us (2%)
    all_to_all x1, blocking collectives, on_device(): lax.all_to_all(outgoing, 'req', split_axis=0, concat_axis=0, tiled=True)  41.5 us
    psum x1, waiting for transfers between devices, on_device(): lax.psum(jnp.dot(heads, w_output, preferred_element_type=jnp.float32).ast...  30 us
    all_to_all x1, waiting for transfers between devices, on_device(): lax.all_to_all(outbound, 'req', split_axis=0, concat_axis=0, tiled=True)  29.7 us
    dot_general x18, matrix products, inner_rows(): lax.dot_general(left, right, (((1,), (1,)), ((), ())), preferred_element_...  20.2 us
    unnamed x3, waiting for transfers between devices  19.7 us
    all_to_all x1, blocking collectives, on_device(): lax.all_to_all(posted.reshape(req_count, req_dev, KEEP, quarter), 'req',...  13.3 us
    dot_general x1, matrix products, on_device(): jnp.einsum('prd,pdgf->prgf', rows_in, w_in, preferred_element_type=jnp.fl...  12.3 us
    lt x16, other arithmetic, block_scores(): inside = offset + jnp.arange(block_len) < limit  9.81 us
  transfers between devices with their start and end apart: 3, of which 3 were waited for; matrix products, arithmetic and copies ran while one was open for 3% of the time, Pallas kernels for 0%

commit v1 on v0

v1 whole, which is shorter than its diff:
```python
import functools

import jax
import jax.numpy as jnp
from jax import lax
from jax.experimental import pallas as pl
from jax.experimental.pallas import tpu as pltpu
from jax.sharding import PartitionSpec as P

KEEP = 16
CAP = 32


EPSILON = 1e-06
THETA = 1000000.0
LOG2E = 1.4426950408889634
BLOCK = 512


def rms_norm(values, gain_vec):
    return (
        values * lax.rsqrt(jnp.mean(values * values, axis=-1, keepdims=True) + EPSILON) * gain_vec
    )


def column_of(row):
    count = row.shape[1]
    at_row = lax.broadcasted_iota(jnp.int32, (count, count), 0)
    at_col = lax.broadcasted_iota(jnp.int32, (count, count), 1)
    return jnp.sum(jnp.where(at_row == at_col, row, 0.0), axis=1, keepdims=True)


def attention_kernel(
    lengths_ref,
    place_ref,
    drafts_ref,
    gain_ref,
    freqs_ref,
    depths_ref,
    mask_ref,
    wq_hbm,
    wkv_hbm,
    wo_hbm,
    cache_hbm,
    mine_ref,
    theirs_ref,
    wq,
    wk,
    wv,
    wo,
    keys,
    vals,
    scores,
    weight_sem,
    cache_sem,
):
    req_dev, tree, width = drafts_ref.shape
    head_dim = cache_hbm.shape[-1]
    kv_heads = cache_hbm.shape[2]
    local_heads = wq.shape[1] // head_dim
    block = scores.shape[2]
    kv_head = place_ref[0]
    first = place_ref[1]

    def column_copy(target, which, sem):
        start = pl.multiple_of((which * kv_heads + kv_head) * head_dim, head_dim)
        return pltpu.make_async_copy(wkv_hbm.at[:, pl.ds(start, head_dim)], target, sem)

    def cache_copy(request, which, index):
        rows = pl.ds(pl.multiple_of(index * block, block), block)
        target = vals if which else keys
        return pltpu.make_async_copy(
            cache_hbm.at[request, which, kv_head, rows],
            target.at[request, rows],
            cache_sem.at[request, which, index],
        )

    copy_q = pltpu.make_async_copy(wq_hbm, wq, weight_sem.at[0])
    copy_k = column_copy(wk, 0, weight_sem.at[1])
    copy_v = column_copy(wv, 1, weight_sem.at[2])
    copy_o = pltpu.make_async_copy(wo_hbm, wo, weight_sem.at[3])
    copy_q.start()
    copy_k.start()
    copy_v.start()
    limits = [lengths_ref[request] for request in range(req_dev)]
    counts = [(limit + block - 1) // block for limit in limits]
    for request in range(req_dev):
        for which in range(2):

            @pl.loop(0, counts[request])
            def _(index, request=request, which=which):
                cache_copy(request, which, index).start()

    copy_o.start()

    inputs = drafts_ref[...].astype(jnp.float32).reshape(req_dev * tree, width)
    normed = rms_norm(inputs, gain_ref[...]).astype(jnp.bfloat16)
    at = [
        column_of(depths_ref[request : request + 1, :].astype(jnp.float32))
        + limits[request].astype(jnp.float32)
        for request in range(req_dev)
    ]
    angles = jnp.concatenate(at, axis=0) * freqs_ref[...]
    cosine = jnp.cos(angles)
    lane = lax.broadcasted_iota(jnp.int32, angles.shape, 1)
    sine = jnp.sin(angles) * jnp.where(lane < head_dim // 2, -1.0, 1.0)

    def turned(vectors):
        return (vectors * cosine + pltpu.roll(vectors, head_dim // 2, 1) * sine).astype(jnp.bfloat16)

    copy_q.wait()
    query_all = jnp.dot(normed, wq[...], preferred_element_type=jnp.float32)
    queries = [
        turned(query_all[:, head * head_dim : (head + 1) * head_dim]) for head in range(local_heads)
    ]
    copy_k.wait()
    key_new = turned(jnp.dot(normed, wk[...], preferred_element_type=jnp.float32))
    copy_v.wait()
    val_new = jnp.dot(normed, wv[...], preferred_element_type=jnp.float32).astype(jnp.bfloat16)
    slope = LOG2E * head_dim ** (-0.5)
    rows = local_heads * tree
    contract = (((1,), (1,)), ((), ()))

    def lanes_down(values, step):
        parts = [values[:, i : i + 128] for i in range(0, values.shape[1], 128)]
        return functools.reduce(step, parts)

    mixed = []
    for request in range(req_dev):
        span = slice(request * tree, (request + 1) * tree)
        own = jnp.concatenate([q[span] for q in queries], axis=0)
        allowed = jnp.concatenate([mask_ref[request]] * local_heads, axis=0) > 0
        tree_scores = lax.dot_general(
            own, key_new[span], contract, preferred_element_type=jnp.float32
        )
        tree_scores = jnp.where(allowed, tree_scores, -jnp.inf)
        limit = limits[request]

        def score_step(index, best, request=request, own=own, limit=limit):
            cache_copy(request, 0, index).wait()
            offset = pl.multiple_of(index * block, block)
            found = lax.dot_general(
                own,
                keys[request, pl.ds(offset, block)],
                contract,
                preferred_element_type=jnp.float32,
            )
            inside = offset + lax.broadcasted_iota(jnp.int32, found.shape, 1) < limit
            found = jnp.where(inside, found, -jnp.inf)
            scores[index] = found
            return jnp.maximum(best, lanes_down(found, jnp.maximum))

        best = lax.fori_loop(
            0, counts[request], score_step, jnp.full((rows, 128), -jnp.inf, jnp.float32)
        )
        peak = jnp.maximum(
            jnp.max(best, axis=1, keepdims=True), jnp.max(tree_scores, axis=1, keepdims=True)
        )
        tree_weights = jnp.exp2((tree_scores - peak) * slope)
        start = (
            jnp.zeros((rows, 128), jnp.float32),
            jnp.dot(
                tree_weights.astype(jnp.bfloat16), val_new[span], preferred_element_type=jnp.float32
            ),
        )

        def sum_step(index, carry, request=request, peak=peak):
            total, accum = carry
            cache_copy(request, 1, index).wait()
            offset = pl.multiple_of(index * block, block)
            weights = jnp.exp2((scores[index] - peak) * slope)
            accum = accum + jnp.dot(
                weights.astype(jnp.bfloat16),
                vals[request, pl.ds(offset, block)],
                preferred_element_type=jnp.float32,
            )
            return total + lanes_down(weights, jnp.add), accum

        total, accum = lax.fori_loop(0, counts[request], sum_step, start)
        total = jnp.sum(total, axis=1, keepdims=True) + jnp.sum(tree_weights, axis=1, keepdims=True)
        mixed.append((accum / total).astype(jnp.bfloat16))

    copy_o.wait()
    for request in range(req_dev):
        heads = jnp.concatenate(
            [mixed[request][head * tree : (head + 1) * tree] for head in range(local_heads)], axis=1
        )
        part = jnp.dot(heads, wo[...], preferred_element_type=jnp.float32).astype(jnp.bfloat16)

        @pl.when(first == request)
        def _(part=part):
            mine_ref[...] = part

        @pl.when(first != request)
        def _(part=part):
            theirs_ref[...] = part


def attention_part(
    drafts, gain, w_query, key_value_weight, w_output, cache, lengths, tree_mask, depths, place
):
    req_dev, tree, width = drafts.shape
    head_dim = cache.shape[-1]
    longest = cache.shape[3]
    block = min(BLOCK, longest)
    local = w_query.shape[1]
    half_dim = head_dim // 2
    freqs = jnp.exp(-jnp.log(THETA) * jnp.arange(half_dim, dtype=jnp.float32) / half_dim)
    freqs = jnp.tile(freqs, 2).reshape(1, head_dim)
    whole = pl.BlockSpec(memory_space=pltpu.VMEM)
    scalar = pl.BlockSpec(memory_space=pltpu.SMEM)
    anywhere = pl.BlockSpec(memory_space=pl.ANY)
    bf16 = jnp.bfloat16
    return pl.pallas_call(
        attention_kernel,
        out_shape=[jax.ShapeDtypeStruct((tree, width), bf16)] * 2,
        in_specs=[scalar] * 2 + [whole] * 5 + [anywhere] * 4,
        out_specs=[whole] * 2,
        scratch_shapes=[
            pltpu.VMEM((width, local), bf16),
            pltpu.VMEM((width, head_dim), bf16),
            pltpu.VMEM((width, head_dim), bf16),
            pltpu.VMEM((local, width), bf16),
            pltpu.VMEM((req_dev, longest, head_dim), bf16),
            pltpu.VMEM((req_dev, longest, head_dim), bf16),
            pltpu.VMEM((longest // block, local // head_dim * tree, block), jnp.float32),
            pltpu.SemaphoreType.DMA((4,)),
            pltpu.SemaphoreType.DMA((req_dev, 2, longest // block)),
        ],
        compiler_params=pltpu.CompilerParams(vmem_limit_bytes=32 * 1024 * 1024),
        name="attention",
    )(
        lengths,
        place,
        drafts,
        gain.reshape(1, width),
        freqs,
        depths,
        tree_mask,
        w_query,
        key_value_weight,
        w_output,
        cache,
    )


def dispatch_kernel(
    place_ref, half_ref, other_ref, drafts_ref, gain_ref, matrix_ref, sent_ref, normed_ref, resid
):
    tree = half_ref.shape[0]
    first = place_ref[1]
    resid[pl.ds(first, 1)] = half_ref[...].astype(jnp.float32)[None]
    resid[pl.ds(1 - first, 1)] = other_ref[...].astype(jnp.float32)[None]
    values = drafts_ref[...].astype(jnp.float32) + resid[...]
    normed = rms_norm(values, gain_ref[...][None]).astype(jnp.bfloat16)
    normed = normed.reshape(normed_ref.shape)
    normed_ref[...] = normed
    sent_ref[...] = jnp.dot(
        matrix_ref[...], normed, preferred_element_type=jnp.float32
    ).astype(jnp.bfloat16)


def dispatch_rows(half, other, drafts, gain, matrix, place):
    req_dev, tree, width = drafts.shape
    whole = pl.BlockSpec(memory_space=pltpu.VMEM)
    scalar = pl.BlockSpec(memory_space=pltpu.SMEM)
    return pl.pallas_call(
        dispatch_kernel,
        out_shape=[
            jax.ShapeDtypeStruct((matrix.shape[0], width), jnp.bfloat16),
            jax.ShapeDtypeStruct((req_dev * tree, width), jnp.bfloat16),
        ],
        in_specs=[scalar] + [whole] * 5,
        out_specs=[whole] * 2,
        scratch_shapes=[pltpu.VMEM((req_dev, tree, width), jnp.float32)],
        compiler_params=pltpu.CompilerParams(vmem_limit_bytes=32 * 1024 * 1024),
        name="dispatch",
    )(place, half, other, drafts, gain.reshape(1, width), matrix)


def expert_kernel(place_ref, rows_ref, w_in_hbm, w_out_hbm, out_ref, wi, wo, in_sem, out_sem):
    halves = wi.shape[0]
    copies = []
    for half in range(halves):
        for which in range(2):
            copy = pltpu.make_async_copy(
                w_in_hbm.at[half, which], wi.at[half, which], in_sem.at[half, which]
            )
            copy.start()
            copies.append(copy)
    downs = []
    for half in range(halves):
        copy = pltpu.make_async_copy(
            w_out_hbm.at[place_ref[2] * halves + half], wo.at[half], out_sem.at[half]
        )
        copy.start()
        downs.append(copy)
    rows = rows_ref[...]
    acts = []
    for half in range(halves):
        copies[2 * half].wait()
        gate = jnp.dot(rows, wi[half, 0], preferred_element_type=jnp.float32)
        copies[2 * half + 1].wait()
        upper = jnp.dot(rows, wi[half, 1], preferred_element_type=jnp.float32)
        acts.append((jnp.maximum(gate, 0.0) * upper).astype(jnp.bfloat16))
    for half in range(halves):
        downs[half].wait()
    groups, ranks, share, quarter = out_ref.shape
    for rank in range(ranks):
        columns = slice(rank * quarter, (rank + 1) * quarter)
        made = jnp.dot(acts[0], wo[0, :, columns], preferred_element_type=jnp.float32)
        for half in range(1, halves):
            made = made + jnp.dot(
                acts[half], wo[half, :, columns], preferred_element_type=jnp.float32
            )
        out_ref[:, rank] = made.astype(jnp.bfloat16).reshape(groups, share, quarter)


def expert_rows(rows, w_in_own, w_out, place, groups, ranks):
    count, width = rows.shape
    halves, _, _, hidden = w_in_own.shape
    quarter = width // ranks
    whole = pl.BlockSpec(memory_space=pltpu.VMEM)
    scalar = pl.BlockSpec(memory_space=pltpu.SMEM)
    anywhere = pl.BlockSpec(memory_space=pl.ANY)
    return pl.pallas_call(
        expert_kernel,
        out_shape=jax.ShapeDtypeStruct((groups, ranks, count // groups, quarter), jnp.bfloat16),
        in_specs=[scalar, whole, anywhere, anywhere],
        out_specs=whole,
        scratch_shapes=[
            pltpu.VMEM((halves, 2, width, hidden), jnp.bfloat16),
            pltpu.VMEM((halves, hidden, width), jnp.bfloat16),
            pltpu.SemaphoreType.DMA((halves, 2)),
            pltpu.SemaphoreType.DMA((halves,)),
        ],
        compiler_params=pltpu.CompilerParams(vmem_limit_bytes=32 * 1024 * 1024),
        name="experts",
    )(place, rows, w_in_own, w_out)


def combine_kernel(
    order_ref, rows_ref, targets_ref, gates_ref, resid_ref, slots_ref, tree_ref, posted_ref
):
    req_dev, tree, quarter = tree_ref.shape
    keep = posted_ref.shape[1]
    tokens = req_dev * tree
    places = lax.broadcasted_iota(jnp.int32, (tokens, rows_ref.shape[0]), 1)
    matrix = jnp.zeros(places.shape, jnp.float32)
    for pick in range(targets_ref.shape[1]):
        matrix = matrix + jnp.where(
            places == targets_ref[:, pick : pick + 1], gates_ref[:, pick : pick + 1], 0.0
        )
    mixture = jnp.dot(
        matrix.astype(jnp.bfloat16), rows_ref[...], preferred_element_type=jnp.float32
    )
    done = (resid_ref[...] + mixture).astype(jnp.bfloat16)
    tree_ref[...] = done.reshape(tree_ref.shape)
    posted_ref[...] = jnp.zeros_like(posted_ref)
    for request in range(req_dev):
        wanted = lax.broadcasted_iota(jnp.int32, (keep, tree), 0)
        chosen = (slots_ref[request : request + 1, :] == wanted).astype(jnp.bfloat16)
        kept = jnp.dot(
            chosen, done[request * tree : (request + 1) * tree], preferred_element_type=jnp.float32
        )
        posted_ref[pl.ds(order_ref[request], 1)] = kept.astype(jnp.bfloat16)[None]


def combine_rows(rows, targets, gates, resid, slots, order, requests):
    tokens, quarter = resid.shape
    req_dev, tree = slots.shape
    whole = pl.BlockSpec(memory_space=pltpu.VMEM)
    scalar = pl.BlockSpec(memory_space=pltpu.SMEM)
    return pl.pallas_call(
        combine_kernel,
        out_shape=[
            jax.ShapeDtypeStruct((req_dev, tree, quarter), jnp.bfloat16),
            jax.ShapeDtypeStruct((requests, KEEP, quarter), jnp.bfloat16),
        ],
        in_specs=[scalar] + [whole] * 5,
        out_specs=[whole] * 2,
        compiler_params=pltpu.CompilerParams(vmem_limit_bytes=32 * 1024 * 1024),
        name="combine",
    )(order, rows, targets, gates, resid, slots)


def on_device(
    drafts,
    gain_attn,
    w_query,
    key_value_weight,
    w_output,
    cache,
    lengths,
    tree_mask,
    depths,
    gain_moe,
    w_router,
    expert_ids,
    w_in,
    w_out,
    slots,
    order,
):
    req_dev, draft_tree, width = drafts.shape
    head_dim = cache.shape[-1]
    kv_heads = cache.shape[2]
    local_heads = w_query.shape[1] // head_dim
    tp_count = lax.axis_size("tp")
    req_count = lax.axis_size("req")
    tp_rank = lax.axis_index("tp")
    head_group = local_heads * tp_count // kv_heads
    kv_head = tp_rank * local_heads // head_group
    tokens = req_dev * draft_tree
    experts = w_router.shape[1]
    pieces = w_in.shape[0]
    quarter = width // tp_count
    first = tp_rank % 2
    place = jnp.stack([kv_head, first, tp_rank]).astype(jnp.int32)

    ids = expert_ids.reshape(tokens, -1)
    picks = ids[:, :, None] == jnp.arange(experts)[None, None, :]
    counts = jnp.sum(picks.astype(jnp.int32), axis=1)
    slot_expert = jnp.cumsum(counts, axis=0) - counts
    slot_pick = jnp.sum(jnp.where(picks, slot_expert[:, None, :], 0), axis=-1)
    held = jnp.where(counts == 1, slot_expert, -1).T
    by_expert = pieces == 2 * tp_count
    if by_expert:
        share = CAP
        held = lax.dynamic_index_in_dim(
            held.reshape(req_count, tp_count, tokens), tp_rank, 1, keepdims=False
        )
        slot_ids = jnp.arange(share)
        targets = ids * CAP + slot_pick
    else:
        share = CAP // tp_count
        held = jnp.repeat(held, 2, axis=0)
        slot_ids = tp_rank * share + jnp.arange(share)
        piece = 2 * ids[:, :, None] + jnp.arange(2)
        lane = (piece // pieces) * tp_count + (slot_pick // share)[:, :, None]
        targets = (lane * pieces + piece % pieces) * share + (slot_pick % share)[:, :, None]
        targets = targets.reshape(tokens, -1)
    matrix = (held[:, None, :] == slot_ids[None, :, None]).astype(jnp.bfloat16)
    matrix = matrix.reshape(-1, tokens)

    mine, theirs = attention_part(
        drafts,
        gain_attn,
        w_query,
        key_value_weight,
        w_output,
        cache,
        lengths,
        tree_mask,
        depths,
        place,
    )
    near = [(i, i ^ 1) for i in range(tp_count)]
    far = [(i, i ^ 2) for i in range(tp_count)]

    def added(left, right):
        return (left.astype(jnp.float32) + right.astype(jnp.float32)).astype(jnp.bfloat16)

    chip = added(mine, lax.ppermute(theirs, "tp", near))
    half = added(chip, lax.ppermute(chip, "tp", far))
    other = lax.ppermute(half, "tp", near)

    sent, normed2 = dispatch_rows(half, other, drafts, gain_moe, matrix, place)
    arrived = lax.all_to_all(
        sent.reshape(req_count, -1, width), "req", split_axis=0, concat_axis=0, tiled=True
    )

    logits = jnp.dot(normed2, w_router, preferred_element_type=jnp.float32)
    chosen = jax.nn.sigmoid(jnp.sum(jnp.where(picks, logits[:, None, :], 0.0), axis=-1))
    gates = (chosen / jnp.sum(chosen, axis=1, keepdims=True)).astype(jnp.bfloat16)
    gates = gates.astype(jnp.float32)
    start = tp_rank * quarter
    own_attn = jnp.where(
        first == 0,
        jnp.concatenate([half, other], axis=0),
        jnp.concatenate([other, half], axis=0),
    )
    own_resid = lax.dynamic_slice_in_dim(
        drafts.reshape(tokens, width), start, quarter, 1
    ).astype(jnp.float32) + lax.dynamic_slice_in_dim(own_attn, start, quarter, 1).astype(
        jnp.float32
    )

    if by_expert:
        own_in = lax.dynamic_slice_in_dim(w_in, tp_rank * 2, 2, 0).transpose(0, 2, 1, 3)
        produced = expert_rows(
            arrived.reshape(-1, width), own_in, w_out, place, req_count, tp_count
        )
    else:
        gates = jnp.repeat(gates, 2, axis=1)
        rows_in = arrived.reshape(req_count, pieces, share, width)
        rows_in = rows_in.transpose(1, 0, 2, 3).reshape(pieces, req_count * share, width)
        gate_up = jnp.einsum("prd,pdgf->prgf", rows_in, w_in, preferred_element_type=jnp.float32)
        act = (jax.nn.relu(gate_up[:, :, 0]) * gate_up[:, :, 1]).astype(jnp.bfloat16)
        produced = jnp.einsum(
            "prf,pfd->prd", act, w_out, preferred_element_type=jnp.float32
        ).astype(jnp.bfloat16)
        produced = produced.reshape(pieces, req_count, share, tp_count, quarter)
        produced = produced.transpose(1, 3, 0, 2, 4)
    returned = lax.all_to_all(
        produced.reshape(req_count * tp_count, -1, quarter),
        ("req", "tp"),
        split_axis=0,
        concat_axis=0,
        tiled=True,
    )
    tree_out, posted = combine_rows(
        returned.reshape(-1, quarter),
        targets,
        gates,
        own_resid,
        slots,
        order,
        req_count * req_dev,
    )
    received = lax.all_to_all(
        posted.reshape(req_count, req_dev, KEEP, quarter),
        "req",
        split_axis=0,
        concat_axis=0,
        tiled=True,
    )
    accepted = jnp.sum(received.astype(jnp.float32), axis=0).astype(jnp.bfloat16)
    return (tree_out, accepted)


def solution(mesh):
    placed = (
        P("req", None, None),
        P(),
        P(None, "tp"),
        P(),
        P("tp", None),
        P("req", None, None, None, None),
        P("req"),
        P("req", None, None),
        P("req", None),
        P(),
        P(),
        P("req", None, None),
        P("req", None, None, None),
        P("req", None, None),
        P("req", None),
        P("req"),
    )
    return jax.shard_map(
        on_device,
        mesh=mesh,
        in_specs=placed,
        out_specs=(P("req", None, "tp"), P("req", None, "tp")),
        check_vma=False,
    )
```

time: 238 us -> 112 us (0.47)
  matrix products: 52.7 us -> 0.2 us
  blocking collectives: 54.8 us -> 11.6 us
  waiting for transfers between devices: 79.3 us -> 39.7 us
  Pallas kernels: 0 us -> 17 us
  other arithmetic: 17.4 us -> 1.51 us
  between operations: 15.8 us -> 0.85 us
  starting transfers between devices: 3.66 us -> 16.4 us
  local copies, waits for them, and re-layouts: 13.8 us -> 24.8 us
    dot_general x37 -> x0, matrix products: 51.5 us -> none  [the longest x18 20.2 us: inner_rows(): lax.dot_general(left, right, (((1,), (1,)), ((), ())), preferred_element_...]
    all_to_all x1 -> x0, blocking collectives: 41.5 us -> none  [on_device(): lax.all_to_all(outgoing, 'req', split_axis=0, concat_axis=0, tiled=True)]
    psum x1 -> x0, waiting for transfers between devices: 30 us -> none  [on_device(): lax.psum(jnp.dot(heads, w_output, preferred_element_type=jnp.float32).ast...]
    unnamed x3 -> x0, waiting for transfers between devices: 19.7 us -> none
    pallas_call x0 -> x4, Pallas kernels: none -> 17 us  [the longest x1 6.8 us: attention_part(): pl.pallas_call(attention_kernel, out_shape=[jax.ShapeDtypeStruct((tree, w...]
    unnamed x36 -> x34, local copies, waits for them, and re-layouts: 5.17 us -> 18.8 us
    lt x16 -> x0, other arithmetic: 9.81 us -> none  [block_scores(): inside = offset + jnp.arange(block_len) < limit]
    all_to_all x1 -> x2, starting transfers between devices: 3.58 us -> 12.9 us  [the longest x1 9.29 us: on_device(): lax.all_to_all(sent.reshape(req_count, -1, width), 'req', split_axis=0, c...]
  transfers between devices with their start and end apart: 3 -> 5, of which waited for: 3 -> 5; matrix products, arithmetic and copies ran while one was open for 3% -> 8% of each run, Pallas kernels for 0% -> 0%
where the time goes in v1:
time: 112 us
  waiting for transfers between devices  39.7 us (35%)
  local copies, waits for them, and re-layouts  24.8 us (22%)
  Pallas kernels  17 us (15%)
  starting transfers between devices  16.4 us (15%)
  blocking collectives  11.6 us (10%)
  other arithmetic  1.51 us (1%)
    all_to_all x1, waiting for transfers between devices, on_device(): lax.all_to_all(produced.reshape(req_count * tp_count, -1, quarter), ('req...  19.7 us
    unnamed x34, local copies, waits for them, and re-layouts  18.8 us
    all_to_all x1, waiting for transfers between devices, on_device(): lax.all_to_all(sent.reshape(req_count, -1, width), 'req', split_axis=0, c...  13.1 us
    all_to_all x1, blocking collectives, on_device(): lax.all_to_all(posted.reshape(req_count, req_dev, KEEP, quarter), 'req',...  11.6 us
    all_to_all x1, starting transfers between devices, on_device(): lax.all_to_all(sent.reshape(req_count, -1, width), 'req', split_axis=0, c...  9.29 us
    pallas_call x1, Pallas kernels, attention_part(): pl.pallas_call(attention_kernel, out_shape=[jax.ShapeDtypeStruct((tree, w...  6.8 us
    pallas_call x1, Pallas kernels, expert_rows(): pl.pallas_call(expert_kernel, out_shape=jax.ShapeDtypeStruct((groups, ran...  6.38 us
    ppermute x1, waiting for transfers between devices, on_device(): half = added(chip, lax.ppermute(chip, 'tp', far))  4.72 us
  transfers between devices with their start and end apart: 5, of which 5 were waited for; matrix products, arithmetic and copies ran while one was open for 8% of the time, Pallas kernels for 0%

profile of v1, /device:TPU:0, one launch (start us, length us, event | category | flops | bytes accessed | tf_op | source)
XLA Modules:
  0.0 112.1 jit_solution(13439671266764425578)
XLA Ops:
  0.8 0.7 reshape.48.gain_ref
  1.6 2.8 %copy-done.3 = bf16[2,2,2,3072,128]{4,3,2,1,0:T(8,128)(2,1)S(1)} copy-done((bf16[2,2,2,3072,128]{4,3,2,1,0:T(8,128)(2,1)S(1)}, bf16[2,2,2,3072,128]{4,3,2,1,0:T(8,128)(2,1)}, u32[]{:S(2)}) %copy-start.3) | copy-done | bytes 6291480
  4.4 1.0 copy-done.4
  5.3 1.4 %copy-done.6 = bf16[1536,512]{1,0:T(8,128)(2,1)S(1)} copy-done((bf16[1536,512]{1,0:T(8,128)(2,1)S(1)}, bf16[1536,512]{1,0:T(8,128)(2,1)}, u32[]{:S(2)}) %copy-start.6) | copy-done | bytes 1572888
  6.8 1.3 %copy-done.7 = bf16[1536,384]{1,0:T(8,128)(2,1)S(1)} copy-done((bf16[1536,384]{1,0:T(8,128)(2,1)S(1)}, bf16[1536,384]{1,0:T(8,128)(2,1)}, u32[]{:S(2)}) %copy-start.7) | copy-done | bytes 1179672
  8.0 1.3 %copy-done.8 = bf16[384,1536]{1,0:T(8,128)(2,1)S(1)} copy-done((bf16[384,1536]{1,0:T(8,128)(2,1)S(1)}, bf16[384,1536]{1,0:T(8,128)(2,1)}, u32[]{:S(2)}) %copy-start.8) | copy-done | bytes 1179672
  9.3 0.8 copy-done.9
  11.5 6.8 %attention.1 = (bf16[64,1536]{1,0:T(8,128)(2,1)S(1)}, bf16[64,1536]{1,0:T(8,128)(2,1)S(1)}) custom-call(s32[2]{0:T(128)S(1)} %copy-done.12, s32[3]{0:T(128)S(1)} %pad_add_fusion.place_ref, bf16[2,64,1536]{2,1,0:T(8,128)(2,1)S(1)} %copy-done.4, f32[1,1536]{1,0:T(1,128)S(1)} %reshape.48.gain_ref, f32[1,128]{1,0:T(1,128)S(1)} %reshape_tile.3.freqs_ref, ...), custom_call_target="tpu_custom_call" | custom-call | tf_op jit(solution)/shard_map/attention/pallas_call | solution.py:214
  18.8 1.1 collective-permute-done
  19.9 2.9 %collective-permute-start.1 = (bf16[64,1536]{1,0:T(8,128)(2,1)S(1)}, bf16[64,1536]{1,0:T(8,128)(2,1)S(1)}, u32[]{:S(2)}, u32[]{:S(2)}) collective-permute-start(bf16[64,1536]{1,0:T(8,128)(2,1)S(1)} %add_convert_fusion.1), channel_id=1, source_target_pairs={{0,2},{1,3},{2,0},{3,1},{4,6},{5,7},{6,4},{7,5},{8,10},{9,11},{10,... | collective-permute-start | bytes 589832 | tf_op jit(solution)/shard_map/ppermute | solution.py:465
  23.3 4.7 %collective-permute-done.1 = bf16[64,1536]{1,0:T(8,128)(2,1)S(1)} collective-permute-done((bf16[64,1536]{1,0:T(8,128)(2,1)S(1)}, bf16[64,1536]{1,0:T(8,128)(2,1)S(1)}, u32[]{:S(2)}, u32[]{:S(2)}) %collective-permute-start.1) | collective-permute-done | bytes 196640 | tf_op jit(solution)/shard_map/ppermute | solution.py:465
  28.5 1.1 collective-permute-done.2.other_ref
  29.6 2.0 %dispatch.1 = (bf16[256,1536]{1,0:T(8,128)(2,1)}, bf16[128,1536]{1,0:T(8,128)(2,1)S(1)}) custom-call(s32[3]{0:T(128)S(1)} %pad_add_fusion.place_ref, bf16[64,1536]{1,0:T(8,128)(2,1)S(1)} %add_convert_fusion.half_ref, bf16[64,1536]{1,0:T(8,128)(2,1)S(1)} %collective-permute-done.2.other_ref, bf16[2,64,1536]{2,1,0:T(8,128)(2,1)S(1)} %copy-done.5, ...), custom_call_target="tpu_custom_call" | custom-call | tf_op jit(solution)/shard_map/dispatch/pallas_call | solution.py:267
  31.7 9.3 %all-to-all-start = ((bf16[8,32,1536]{2,1,0:T(8,128)(2,1)}), bf16[8,32,1536]{2,1,0:T(8,128)(2,1)S(1)}, u32[]{:S(2)}, u32[]{:S(2)}) async-start(bf16[8,32,1536]{2,1,0:T(8,128)(2,1)} %bitcast.8), calls=%async_computation | async-start | bytes 1572864 | tf_op jit(solution)/shard_map/all_to_all | solution.py:469
  41.0 4.6 %constant_dynamic-slice_fusion = bf16[2,1536,2,384]{3,2,1,0:T(2,128)(2,1)S(1)} fusion(bf16[8,1536,2,384]{3,2,1,0:T(2,128)(2,1)} %param.28, s32[]{:T(128)S(6)} %select_n.51), kind=kLoop, calls=%fused_computation.23 | loop fusion | bytes 9437188 | tf_op jit(solution)/shard_map/dynamic_slice | solution.py:490
  45.5 2.8 %copy.50 = bf16[2,1536,2,384]{3,1,2,0:T(8,128)(2,1)} copy(bf16[2,1536,2,384]{3,2,1,0:T(2,128)(2,1)S(1)} %constant_dynamic-slice_fusion) | data formatting | bytes 9437184
  48.3 13.1 %all-to-all-done = bf16[8,32,1536]{2,1,0:T(8,128)(2,1)S(1)} async-done(((bf16[8,32,1536]{2,1,0:T(8,128)(2,1)}), bf16[8,32,1536]{2,1,0:T(8,128)(2,1)S(1)}, u32[]{:S(2)}, u32[]{:S(2)}) %all-to-all-start) | async-done | bytes 786464 | tf_op jit(solution)/shard_map/all_to_all | solution.py:469
  61.4 2.3 %copy-done.1 = bf16[2,1536,2,384]{3,1,2,0:T(8,128)(2,1)S(1)} copy-done((bf16[2,1536,2,384]{3,1,2,0:T(8,128)(2,1)S(1)}, bf16[2,1536,2,384]{3,1,2,0:T(8,128)(2,1)}, u32[]{:S(2)}) %copy-start.1) | copy-done | bytes 4718616
  63.8 3.7 %copy-done.2 = bf16[8,384,1536]{2,1,0:T(8,128)(2,1)S(1)} copy-done((bf16[8,384,1536]{2,1,0:T(8,128)(2,1)S(1)}, bf16[8,384,1536]{2,1,0:T(8,128)(2,1)}, u32[]{:S(2)}) %copy-start.2) | copy-done | bytes 9437208
  67.4 6.4 %experts.1 = bf16[8,4,32,384]{3,2,1,0:T(8,128)(2,1)} custom-call(s32[3]{0:T(128)S(1)} %pad_add_fusion.place_ref, bf16[256,1536]{1,0:T(8,128)(2,1)S(1)} %bitcast.25, bf16[2,2,1536,384]{3,2,1,0:T(8,128)(2,1)S(1)} %bitcast.24, bf16[8,384,1536]{2,1,0:T(8,128)(2,1)S(1)} %copy-done.2), custom_call_target="tpu_custom_call" | custom-call | tf_op jit(solution)/shard_map/experts/pallas_call | solution.py:326
  73.8 3.6 %all-to-all-start.1 = ((bf16[32,32,384]{2,1,0:T(8,128)(2,1)}), bf16[32,32,384]{2,1,0:T(8,128)(2,1)S(1)}, u32[]{:S(2)}, u32[]{:S(2)}) async-start(bf16[32,32,384]{2,1,0:T(8,128)(2,1)} %bitcast.11), calls=%async_computation.1 | async-start | bytes 1572864 | tf_op jit(solution)/shard_map/all_to_all | solution.py:505
  78.3 19.7 %all-to-all-done.1 = bf16[32,32,384]{2,1,0:T(8,128)(2,1)S(1)} async-done(((bf16[32,32,384]{2,1,0:T(8,128)(2,1)}), bf16[32,32,384]{2,1,0:T(8,128)(2,1)S(1)}, u32[]{:S(2)}, u32[]{:S(2)}) %all-to-all-start.1) | async-done | bytes 786464 | tf_op jit(solution)/shard_map/all_to_all | solution.py:505
  98.1 1.8 %combine.1 = (bf16[2,64,384]{2,1,0:T(8,128)(2,1)}, bf16[16,16,384]{2,1,0:T(8,128)(2,1)S(1)}) custom-call(s32[2]{0:T(128)S(1)} %copy-done.13, bf16[1024,384]{1,0:T(8,128)(2,1)S(1)} %bitcast.26, s32[128,4]{1,0:T(8,128)S(1)} %multiply_add_fusion.targets_ref, f32[128,4]{1,0:T(8,128)S(1)} %fusion.4.gates_ref, f32[128,384]{1,0:T(8,128)S(1)} %convert_add_fusion.resid_ref, ...), custom_call_target="tpu_custom_call" | custom-call | tf_op jit(solution)/shard_map/combine/pallas_call | solution.py:374
  99.8 11.6 %all_to_all.15 = bf16[8,2,16,384]{3,2,1,0:T(8,128)(2,1)S(1)} all-to-all(bf16[8,2,16,384]{3,2,1,0:T(8,128)(2,1)S(1)} %bitcast.28), channel_id=1, replica_groups=mesh['req'=8,'tp'=4] {'req'}, dimensions={0} | all-to-all | bytes 393216 | tf_op jit(solution)/shard_map/all_to_all | solution.py:521
  (55 shorter events, 4.5 us)
Async XLA Ops:
  0.6 77.1 %copy-start = (bf16[1536,32]{0,1:T(8,128)(2,1)S(1)}, bf16[1536,32]{0,1:T(8,128)(2,1)}, u32[]{:S(2)}) copy-start(bf16[1536,32]{0,1:T(8,128)(2,1)} %param.26) | copy-start | bytes 294916
  1.6 2.8 %copy-start.3 = (bf16[2,2,2,3072,128]{4,3,2,1,0:T(8,128)(2,1)S(1)}, bf16[2,2,2,3072,128]{4,3,2,1,0:T(8,128)(2,1)}, u32[]{:S(2)}) copy-start(bf16[2,2,2,3072,128]{4,3,2,1,0:T(8,128)(2,1)} %cache_hbm.1) | copy-start | bytes 18874372
  4.3 1.0 copy-start.4
  5.3 1.4 %copy-start.6 = (bf16[1536,512]{1,0:T(8,128)(2,1)S(1)}, bf16[1536,512]{1,0:T(8,128)(2,1)}, u32[]{:S(2)}) copy-start(bf16[1536,512]{1,0:T(8,128)(2,1)} %wkv_hbm.1) | copy-start | bytes 4718596
  6.8 1.3 %copy-start.7 = (bf16[1536,384]{1,0:T(8,128)(2,1)S(1)}, bf16[1536,384]{1,0:T(8,128)(2,1)}, u32[]{:S(2)}) copy-start(bf16[1536,384]{1,0:T(8,128)(2,1)} %wq_hbm.1) | copy-start | bytes 3538948
  8.0 1.3 %copy-start.8 = (bf16[384,1536]{1,0:T(8,128)(2,1)S(1)}, bf16[384,1536]{1,0:T(8,128)(2,1)}, u32[]{:S(2)}) copy-start(bf16[384,1536]{1,0:T(8,128)(2,1)} %wo_hbm.1) | copy-start | bytes 3538948
  9.3 0.8 copy-start.9
  10.1 0.7 copy-start.10
  10.8 0.7 copy-start.12
  11.5 11.4 %copy-start.15 = (s32[2,64,4]{1,2,0:T(4,128)S(1)}, s32[2,64,4]{1,2,0:T(4,128)}, u32[]{:S(2)}) copy-start(s32[2,64,4]{1,2,0:T(4,128)} %param.27) | copy-start | bytes 6148
  11.5 16.8 %copy-start.14 = (f32[1536]{0:T(1024)S(1)}, f32[1536]{0:T(1024)}, u32[]{:S(2)}) copy-start(f32[1536]{0:T(1024)} %param.25) | copy-start | bytes 18436
  11.5 18.2 %copy-start.5 = (bf16[2,64,1536]{2,1,0:T(8,128)(2,1)S(1)}, bf16[2,64,1536]{2,1,0:T(8,128)(2,1)}, u32[]{:S(2)}) copy-start(bf16[2,64,1536]{2,1,0:T(8,128)(2,1)} %drafts_ref.3) | copy-start | bytes 1179652
  18.3 1.6 %collective-permute-start = (bf16[64,1536]{1,0:T(8,128)(2,1)S(1)}, bf16[64,1536]{1,0:T(8,128)(2,1)S(1)}, u32[]{:S(2)}, u32[]{:S(2)}) collective-permute-start(bf16[64,1536]{1,0:T(8,128)(2,1)S(1)} %get-tuple-element.9), channel_id=1, source_target_pairs={{0,1},{1,0},{2,3},{3,2},{4,5},{5,4},{6,7},{7,6},{8,9},{9,8},{10,11... | collective-permute-start | bytes 589832 | tf_op jit(solution)/shard_map/ppermute | solution.py:464
  19.9 8.1 %collective-permute-start.1 = (bf16[64,1536]{1,0:T(8,128)(2,1)S(1)}, bf16[64,1536]{1,0:T(8,128)(2,1)S(1)}, u32[]{:S(2)}, u32[]{:S(2)}) collective-permute-start(bf16[64,1536]{1,0:T(8,128)(2,1)S(1)} %add_convert_fusion.1), channel_id=1, source_target_pairs={{0,2},{1,3},{2,0},{3,1},{4,6},{5,7},{6,4},{7,5},{8,10},{9,11},{10,... | collective-permute-start | bytes 589832 | tf_op jit(solution)/shard_map/ppermute | solution.py:465
  28.1 1.5 %collective-permute-start.2 = (bf16[64,1536]{1,0:T(8,128)(2,1)S(1)}, bf16[64,1536]{1,0:T(8,128)(2,1)S(1)}, u32[]{:S(2)}, u32[]{:S(2)}) collective-permute-start(bf16[64,1536]{1,0:T(8,128)(2,1)S(1)} %add_convert_fusion.half_ref), channel_id=1, source_target_pairs={{0,1},{1,0},{2,3},{3,2},{4,5},{5,4},{6,7},{7,6},{8,9},{9,8},{10,11... | collective-permute-start | bytes 589832 | tf_op jit(solution)/shard_map/ppermute | solution.py:466
  31.7 29.7 %all-to-all-start = ((bf16[8,32,1536]{2,1,0:T(8,128)(2,1)}), bf16[8,32,1536]{2,1,0:T(8,128)(2,1)S(1)}, u32[]{:S(2)}, u32[]{:S(2)}) async-start(bf16[8,32,1536]{2,1,0:T(8,128)(2,1)} %bitcast.8), calls=%async_computation | async-start | bytes 1572864 | tf_op jit(solution)/shard_map/all_to_all | solution.py:469
  61.4 2.3 %copy-start.1 = (bf16[2,1536,2,384]{3,1,2,0:T(8,128)(2,1)S(1)}, bf16[2,1536,2,384]{3,1,2,0:T(8,128)(2,1)}, u32[]{:S(2)}) copy-start(bf16[2,1536,2,384]{3,1,2,0:T(8,128)(2,1)} %copy.50) | copy-start | bytes 14155780
  63.8 3.7 %copy-start.2 = (bf16[8,384,1536]{2,1,0:T(8,128)(2,1)S(1)}, bf16[8,384,1536]{2,1,0:T(8,128)(2,1)}, u32[]{:S(2)}) copy-start(bf16[8,384,1536]{2,1,0:T(8,128)(2,1)} %w_out_hbm.1) | copy-start | bytes 28311556
  67.4 30.6 %copy-start.11 = (s32[2,64]{1,0:T(2,128)S(1)}, s32[2,64]{1,0:T(2,128)}, u32[]{:S(2)}) copy-start(s32[2,64]{1,0:T(2,128)} %slots_ref.1) | copy-start | bytes 1540
  67.4 30.6 %copy-start.13 = (s32[2]{0:T(128)S(1)}, s32[2]{0:T(128)}, u32[]{:S(2)}) copy-start(s32[2]{0:T(128)} %order_ref.1) | copy-start | bytes 28
  73.8 24.2 %all-to-all-start.1 = ((bf16[32,32,384]{2,1,0:T(8,128)(2,1)}), bf16[32,32,384]{2,1,0:T(8,128)(2,1)S(1)}, u32[]{:S(2)}, u32[]{:S(2)}) async-start(bf16[32,32,384]{2,1,0:T(8,128)(2,1)} %bitcast.11), calls=%async_computation.1 | async-start | bytes 1572864 | tf_op jit(solution)/shard_map/all_to_all | solution.py:505

commit v2 on v1

--- a/solution.py
+++ b/solution.py
@@ -15,6 +15,8 @@
 THETA = 1000000.0
 LOG2E = 1.4426950408889634
 BLOCK = 512
+WHOLE_VMEM = 60 * 1024 * 1024
+SOME_VMEM = 32 * 1024 * 1024
 
 
 def rms_norm(values, gain_vec):
@@ -33,17 +35,18 @@
 def attention_kernel(
     lengths_ref,
     place_ref,
-    drafts_ref,
     gain_ref,
     freqs_ref,
     depths_ref,
     mask_ref,
+    drafts_hbm,
     wq_hbm,
     wkv_hbm,
     wo_hbm,
     cache_hbm,
     mine_ref,
     theirs_ref,
+    drafts,
     wq,
     wk,
     wv,
@@ -54,7 +57,7 @@
     weight_sem,
     cache_sem,
 ):
-    req_dev, tree, width = drafts_ref.shape
+    req_dev, tree, width = drafts.shape
     head_dim = cache_hbm.shape[-1]
     kv_heads = cache_hbm.shape[2]
     local_heads = wq.shape[1] // head_dim
@@ -75,6 +78,8 @@
             cache_sem.at[request, which, index],
         )
 
+    copy_d = pltpu.make_async_copy(drafts_hbm, drafts, weight_sem.at[4])
+    copy_d.start()
     copy_q = pltpu.make_async_copy(wq_hbm, wq, weight_sem.at[0])
     copy_k = column_copy(wk, 0, weight_sem.at[1])
     copy_v = column_copy(wv, 1, weight_sem.at[2])
@@ -93,8 +98,9 @@
 
     copy_o.start()
 
-    inputs = drafts_ref[...].astype(jnp.float32).reshape(req_dev * tree, width)
-    normed = rms_norm(inputs, gain_ref[...]).astype(jnp.bfloat16)
+    copy_d.wait()
+    inputs = drafts[...].astype(jnp.float32).reshape(req_dev * tree, width)
+    normed = rms_norm(inputs, gain_ref[...][None, :]).astype(jnp.bfloat16)
     at = [
         column_of(depths_ref[request : request + 1, :].astype(jnp.float32))
         + limits[request].astype(jnp.float32)
@@ -214,9 +220,10 @@
     return pl.pallas_call(
         attention_kernel,
         out_shape=[jax.ShapeDtypeStruct((tree, width), bf16)] * 2,
-        in_specs=[scalar] * 2 + [whole] * 5 + [anywhere] * 4,
+        in_specs=[scalar] * 2 + [whole] * 4 + [anywhere] * 5,
         out_specs=[whole] * 2,
         scratch_shapes=[
+            pltpu.VMEM((req_dev, tree, width), bf16),
             pltpu.VMEM((width, local), bf16),
             pltpu.VMEM((width, head_dim), bf16),
             pltpu.VMEM((width, head_dim), bf16),
@@ -224,19 +231,19 @@
             pltpu.VMEM((req_dev, longest, head_dim), bf16),
             pltpu.VMEM((req_dev, longest, head_dim), bf16),
             pltpu.VMEM((longest // block, local // head_dim * tree, block), jnp.float32),
-            pltpu.SemaphoreType.DMA((4,)),
+            pltpu.SemaphoreType.DMA((5,)),
             pltpu.SemaphoreType.DMA((req_dev, 2, longest // block)),
         ],
-        compiler_params=pltpu.CompilerParams(vmem_limit_bytes=32 * 1024 * 1024),
+        compiler_params=pltpu.CompilerParams(vmem_limit_bytes=WHOLE_VMEM),
         name="attention",
     )(
         lengths,
         place,
-        drafts,
-        gain.reshape(1, width),
+        gain,
         freqs,
         depths,
         tree_mask,
+        drafts,
         w_query,
         key_value_weight,
         w_output,
@@ -245,67 +252,88 @@
 
 
 def dispatch_kernel(
-    place_ref, half_ref, other_ref, drafts_ref, gain_ref, matrix_ref, sent_ref, normed_ref, resid
+    place_ref,
+    half_ref,
+    other_ref,
+    drafts_ref,
+    gain_ref,
+    held_ref,
+    router_ref,
+    logits_ref,
+    *rest,
 ):
-    tree = half_ref.shape[0]
+    sent_refs, resid = rest[:-1], rest[-1]
     first = place_ref[1]
     resid[pl.ds(first, 1)] = half_ref[...].astype(jnp.float32)[None]
     resid[pl.ds(1 - first, 1)] = other_ref[...].astype(jnp.float32)[None]
     values = drafts_ref[...].astype(jnp.float32) + resid[...]
-    normed = rms_norm(values, gain_ref[...][None]).astype(jnp.bfloat16)
-    normed = normed.reshape(normed_ref.shape)
-    normed_ref[...] = normed
-    sent_ref[...] = jnp.dot(
-        matrix_ref[...], normed, preferred_element_type=jnp.float32
-    ).astype(jnp.bfloat16)
-
-
-def dispatch_rows(half, other, drafts, gain, matrix, place):
+    normed = rms_norm(values, gain_ref[...][None, None, :]).astype(jnp.bfloat16)
+    normed = normed.reshape(-1, normed.shape[-1])
+    for step, sent_ref in enumerate(sent_refs):
+        slots = lax.broadcasted_iota(
+            jnp.int32, (sent_ref.shape[0], held_ref.shape[1]), 0
+        )
+        row = held_ref[pl.ds(place_ref[3] ^ step, 1), :]
+        matrix = (row == slots).astype(jnp.bfloat16)
+        sent_ref[...] = jnp.dot(matrix, normed, preferred_element_type=jnp.float32).astype(
+            jnp.bfloat16
+        )
+    logits_ref[...] = lax.dot_general(
+        normed, router_ref[...], (((1,), (1,)), ((), ())), preferred_element_type=jnp.float32
+    )
+
+
+def dispatch_rows(half, other, drafts, gain, held, router, place):
     req_dev, tree, width = drafts.shape
+    tokens = req_dev * tree
     whole = pl.BlockSpec(memory_space=pltpu.VMEM)
     scalar = pl.BlockSpec(memory_space=pltpu.SMEM)
-    return pl.pallas_call(
+    logits, *sent = pl.pallas_call(
         dispatch_kernel,
-        out_shape=[
-            jax.ShapeDtypeStruct((matrix.shape[0], width), jnp.bfloat16),
-            jax.ShapeDtypeStruct((req_dev * tree, width), jnp.bfloat16),
-        ],
-        in_specs=[scalar] + [whole] * 5,
-        out_specs=[whole] * 2,
+        out_shape=[jax.ShapeDtypeStruct((tokens, router.shape[0]), jnp.float32)]
+        + [jax.ShapeDtypeStruct((CAP, width), jnp.bfloat16)] * held.shape[0],
+        in_specs=[scalar] + [whole] * 6,
+        out_specs=[whole] * (1 + held.shape[0]),
         scratch_shapes=[pltpu.VMEM((req_dev, tree, width), jnp.float32)],
-        compiler_params=pltpu.CompilerParams(vmem_limit_bytes=32 * 1024 * 1024),
+        compiler_params=pltpu.CompilerParams(vmem_limit_bytes=SOME_VMEM),
         name="dispatch",
-    )(place, half, other, drafts, gain.reshape(1, width), matrix)
-
-
-def expert_kernel(place_ref, rows_ref, w_in_hbm, w_out_hbm, out_ref, wi, wo, in_sem, out_sem):
+    )(place, half, other, drafts, gain, held, router)
+    return logits, sent
+
+
+def expert_kernel(place_ref, w_in_hbm, w_out_hbm, *rest):
+    *row_refs, out_ref, rows, wi, wo, in_sem, out_sem = rest
     halves = wi.shape[0]
-    copies = []
+    in_copies = []
     for half in range(halves):
         for which in range(2):
             copy = pltpu.make_async_copy(
                 w_in_hbm.at[half, which], wi.at[half, which], in_sem.at[half, which]
             )
             copy.start()
-            copies.append(copy)
-    downs = []
+            in_copies.append(copy)
+    out_copies = []
     for half in range(halves):
         copy = pltpu.make_async_copy(
             w_out_hbm.at[place_ref[2] * halves + half], wo.at[half], out_sem.at[half]
         )
         copy.start()
-        downs.append(copy)
-    rows = rows_ref[...]
+        out_copies.append(copy)
+    share = row_refs[0].shape[0]
+    for step, row_ref in enumerate(row_refs):
+        start = pl.multiple_of((place_ref[3] ^ step) * share, share)
+        rows[pl.ds(start, share)] = row_ref[...]
+    taken = rows[...]
     acts = []
     for half in range(halves):
-        copies[2 * half].wait()
-        gate = jnp.dot(rows, wi[half, 0], preferred_element_type=jnp.float32)
-        copies[2 * half + 1].wait()
-        upper = jnp.dot(rows, wi[half, 1], preferred_element_type=jnp.float32)
+        in_copies[2 * half].wait()
+        gate = jnp.dot(taken, wi[half, 0], preferred_element_type=jnp.float32)
+        in_copies[2 * half + 1].wait()
+        upper = jnp.dot(taken, wi[half, 1], preferred_element_type=jnp.float32)
         acts.append((jnp.maximum(gate, 0.0) * upper).astype(jnp.bfloat16))
-    for half in range(halves):
-        downs[half].wait()
-    groups, ranks, share, quarter = out_ref.shape
+    for copy in out_copies:
+        copy.wait()
+    groups, ranks, _, quarter = out_ref.shape
     for rank in range(ranks):
         columns = slice(rank * quarter, (rank + 1) * quarter)
         made = jnp.dot(acts[0], wo[0, :, columns], preferred_element_type=jnp.float32)
@@ -316,8 +344,9 @@
         out_ref[:, rank] = made.astype(jnp.bfloat16).reshape(groups, share, quarter)
 
 
-def expert_rows(rows, w_in_own, w_out, place, groups, ranks):
-    count, width = rows.shape
+def expert_rows(rows, w_in_own, w_out, place, ranks):
+    share, width = rows[0].shape
+    groups = len(rows)
     halves, _, _, hidden = w_in_own.shape
     quarter = width // ranks
     whole = pl.BlockSpec(memory_space=pltpu.VMEM)
@@ -325,18 +354,19 @@
     anywhere = pl.BlockSpec(memory_space=pl.ANY)
     return pl.pallas_call(
         expert_kernel,
-        out_shape=jax.ShapeDtypeStruct((groups, ranks, count // groups, quarter), jnp.bfloat16),
-        in_specs=[scalar, whole, anywhere, anywhere],
+        out_shape=jax.ShapeDtypeStruct((groups, ranks, share, quarter), jnp.bfloat16),
+        in_specs=[scalar] + [anywhere] * 2 + [whole] * groups,
         out_specs=whole,
         scratch_shapes=[
+            pltpu.VMEM((groups * share, width), jnp.bfloat16),
             pltpu.VMEM((halves, 2, width, hidden), jnp.bfloat16),
             pltpu.VMEM((halves, hidden, width), jnp.bfloat16),
             pltpu.SemaphoreType.DMA((halves, 2)),
             pltpu.SemaphoreType.DMA((halves,)),
         ],
-        compiler_params=pltpu.CompilerParams(vmem_limit_bytes=32 * 1024 * 1024),
+        compiler_params=pltpu.CompilerParams(vmem_limit_bytes=WHOLE_VMEM),
         name="experts",
-    )(place, rows, w_in_own, w_out)
+    )(place, w_in_own, w_out, *rows)
 
 
 def combine_kernel(
@@ -379,7 +409,7 @@
         ],
         in_specs=[scalar] + [whole] * 5,
         out_specs=[whole] * 2,
-        compiler_params=pltpu.CompilerParams(vmem_limit_bytes=32 * 1024 * 1024),
+        compiler_params=pltpu.CompilerParams(vmem_limit_bytes=SOME_VMEM),
         name="combine",
     )(order, rows, targets, gates, resid, slots)
 
@@ -416,7 +446,7 @@
     pieces = w_in.shape[0]
     quarter = width // tp_count
     first = tp_rank % 2
-    place = jnp.stack([kv_head, first, tp_rank]).astype(jnp.int32)
+    place = jnp.stack([kv_head, first, tp_rank, lax.axis_index("req")]).astype(jnp.int32)
 
     ids = expert_ids.reshape(tokens, -1)
     picks = ids[:, :, None] == jnp.arange(experts)[None, None, :]
@@ -430,7 +460,6 @@
         held = lax.dynamic_index_in_dim(
             held.reshape(req_count, tp_count, tokens), tp_rank, 1, keepdims=False
         )
-        slot_ids = jnp.arange(share)
         targets = ids * CAP + slot_pick
     else:
         share = CAP // tp_count
@@ -440,8 +469,8 @@
         lane = (piece // pieces) * tp_count + (slot_pick // share)[:, :, None]
         targets = (lane * pieces + piece % pieces) * share + (slot_pick % share)[:, :, None]
         targets = targets.reshape(tokens, -1)
-    matrix = (held[:, None, :] == slot_ids[None, :, None]).astype(jnp.bfloat16)
-    matrix = matrix.reshape(-1, tokens)
+        matrix = (held[:, None, :] == slot_ids[None, :, None]).astype(jnp.bfloat16)
+        matrix = matrix.reshape(-1, tokens)
 
     mine, theirs = attention_part(
         drafts,
@@ -465,12 +494,24 @@
     half = added(chip, lax.ppermute(chip, "tp", far))
     other = lax.ppermute(half, "tp", near)
 
-    sent, normed2 = dispatch_rows(half, other, drafts, gain_moe, matrix, place)
-    arrived = lax.all_to_all(
-        sent.reshape(req_count, -1, width), "req", split_axis=0, concat_axis=0, tiled=True
-    )
-
-    logits = jnp.dot(normed2, w_router, preferred_element_type=jnp.float32)
+    if by_expert:
+        logits, sent = dispatch_rows(
+            half, other, drafts, gain_moe, held, w_router.T, place
+        )
+        arrived = [sent[0]] + [
+            lax.ppermute(sent[step], "req", [(i, i ^ step) for i in range(req_count)])
+            for step in range(1, req_count)
+        ]
+    else:
+        resid = jnp.where(first == 0, jnp.stack([half, other]), jnp.stack([other, half]))
+        resid = (drafts.astype(jnp.float32) + resid.astype(jnp.float32)).reshape(tokens, width)
+        normed2 = rms_norm(resid, gain_moe).astype(jnp.bfloat16)
+        logits = jnp.dot(normed2, w_router, preferred_element_type=jnp.float32)
+        sent = jnp.dot(matrix, normed2, preferred_element_type=jnp.float32).astype(jnp.bfloat16)
+        arrived = lax.all_to_all(
+            sent.reshape(req_count, -1, width), "req", split_axis=0, concat_axis=0, tiled=True
+        )
+
     chosen = jax.nn.sigmoid(jnp.sum(jnp.where(picks, logits[:, None, :], 0.0), axis=-1))
     gates = (chosen / jnp.sum(chosen, axis=1, keepdims=True)).astype(jnp.bfloat16)
     gates = gates.astype(jnp.float32)
@@ -488,9 +529,7 @@
 
     if by_expert:
         own_in = lax.dynamic_slice_in_dim(w_in, tp_rank * 2, 2, 0).transpose(0, 2, 1, 3)
-        produced = expert_rows(
-            arrived.reshape(-1, width), own_in, w_out, place, req_count, tp_count
-        )
+        produced = expert_rows(arrived, own_in, w_out, place, tp_count)
     else:
         gates = jnp.repeat(gates, 2, axis=1)
         rows_in = arrived.reshape(req_count, pieces, share, width)

time: 112 us -> 96.3 us (0.86)
  local copies, waits for them, and re-layouts: 24.8 us -> 9.99 us
  waiting for transfers between devices: 39.7 us -> 28.5 us
  starting transfers between devices: 16.4 us -> 24.9 us
  other arithmetic: 1.51 us -> 2.85 us
    unnamed x34 -> x32, local copies, waits for them, and re-layouts: 18.8 us -> 4.2 us
    ppermute x0 -> x7, starting transfers between devices: none -> 14.2 us  [on_device(): lax.ppermute(sent[step], 'req', [(i, i ^ step) for i in range(req_count)])]
    all_to_all x1 -> x0, waiting for transfers between devices: 13.1 us -> none  [on_device(): lax.all_to_all(sent.reshape(req_count, -1, width), 'req', split_axis=0, c...]
    all_to_all x1 -> x0, starting transfers between devices: 9.29 us -> none  [on_device(): lax.all_to_all(sent.reshape(req_count, -1, width), 'req', split_axis=0, c...]
    all_to_all x1, starting transfers between devices: 3.6 us -> 7.1 us  [on_device(): lax.all_to_all(produced.reshape(req_count * tp_count, -1, quarter), ('req...]
    ppermute x0 -> x7, waiting for transfers between devices: none -> 1.27 us  [on_device(): lax.ppermute(sent[step], 'req', [(i, i ^ step) for i in range(req_count)])]
  transfers between devices with their start and end apart: 5 -> 11, of which waited for: 5 -> 5; matrix products, arithmetic and copies ran while one was open for 8% -> 9% of each run, Pallas kernels for 0% -> 0%
where the time goes in v2:
time: 96.3 us; the launch traced here: 96.1 us
  waiting for transfers between devices  28.5 us (30%)
  starting transfers between devices  24.9 us (26%)
  Pallas kernels  17.3 us (18%)
  blocking collectives  11.6 us (12%)
  local copies, waits for them, and re-layouts  9.99 us (10%)
  other arithmetic  2.85 us (3%)
    all_to_all x1, waiting for transfers between devices, on_device(): lax.all_to_all(produced.reshape(req_count * tp_count, -1, quarter), ('req...  19.9 us
    ppermute x7, starting transfers between devices, on_device(): lax.ppermute(sent[step], 'req', [(i, i ^ step) for i in range(req_count)])  14.2 us
    all_to_all x1, blocking collectives, on_device(): lax.all_to_all(posted.reshape(req_count, req_dev, KEEP, quarter), 'req',...  11.6 us
    pallas_call x1, Pallas kernels, attention_part(): pl.pallas_call(attention_kernel, out_shape=[jax.ShapeDtypeStruct((tree, w...  7.26 us
    all_to_all x1, starting transfers between devices, on_device(): lax.all_to_all(produced.reshape(req_count * tp_count, -1, quarter), ('req...  7.1 us
    pallas_call x1, Pallas kernels, expert_rows(): pl.pallas_call(expert_kernel, out_shape=jax.ShapeDtypeStruct((groups, ran...  6.88 us
    ppermute x1, waiting for transfers between devices, on_device(): half = added(chip, lax.ppermute(chip, 'tp', far))  4.72 us
    dynamic_slice x1, local copies, waits for them, and re-layouts, on_device(): lax.dynamic_slice_in_dim(w_in, tp_rank * 2, 2, 0).transpose(0, 2, 1, 3)  4.55 us
  transfers between devices with their start and end apart: 11, of which 5 were waited for; matrix products, arithmetic and copies ran while one was open for 9% of the time, Pallas kernels for 0%

profile of v2, /device:TPU:0, one launch (start us, length us, event | category | flops | bytes accessed | tf_op | source)
XLA Modules:
  0.0 96.1 jit_solution(8823269407560093557)
XLA Ops:
  0.7 0.7 reshape_tile.3.freqs_ref
  1.3 0.6 pad_add_fusion.place_ref
  2.0 7.3 %attention.1 = (bf16[64,1536]{1,0:T(8,128)(2,1)}, bf16[64,1536]{1,0:T(8,128)(2,1)}) custom-call(s32[2]{0:T(128)} %lengths_ref.1, s32[4]{0:T(128)} %pad_add_fusion.place_ref, f32[1536]{0:T(1024)} %gain_ref.2, f32[1,128]{1,0:T(1,128)} %reshape_tile.3.freqs_ref, s32[2,64]{1,0:T(2,128)} %depths_ref.1, s32[2,64,64]{2,1,0:T(8,128)} %mask_ref.1, ...), custom_call_target="tpu_custom_call" | custom-call | tf_op jit(solution)/shard_map/attention/pallas_call | solution.py:220
  9.8 1.3 %collective-permute-done = bf16[64,1536]{1,0:T(8,128)(2,1)S(1)} collective-permute-done((bf16[64,1536]{1,0:T(8,128)(2,1)}, bf16[64,1536]{1,0:T(8,128)(2,1)S(1)}, u32[]{:S(2)}, u32[]{:S(2)}) %collective-permute-start) | collective-permute-done | bytes 196640 | tf_op jit(solution)/shard_map/ppermute | solution.py:493
  11.1 1.0 %add_convert_fusion.1 = bf16[64,1536]{1,0:T(8,128)(2,1)S(1)} fusion(bf16[64,1536]{1,0:T(8,128)(2,1)S(1)} %collective-permute-done, bf16[64,1536]{1,0:T(8,128)(2,1)} %get-tuple-element.15), kind=kLoop, calls=%fused_computation.6 | loop fusion | flops 393216 | bytes 589824 | tf_op jit(solution)/shard_map/convert_element_type | solution.py:491
  12.0 2.9 %collective-permute-start.1 = (bf16[64,1536]{1,0:T(8,128)(2,1)S(1)}, bf16[64,1536]{1,0:T(8,128)(2,1)S(1)}, u32[]{:S(2)}, u32[]{:S(2)}) collective-permute-start(bf16[64,1536]{1,0:T(8,128)(2,1)S(1)} %add_convert_fusion.1), channel_id=1, source_target_pairs={{0,2},{1,3},{2,0},{3,1},{4,6},{5,7},{6,4},{7,5},{8,10},{9,11},{10,... | collective-permute-start | bytes 589832 | tf_op jit(solution)/shard_map/ppermute | solution.py:494
  15.4 4.7 %collective-permute-done.1 = bf16[64,1536]{1,0:T(8,128)(2,1)S(1)} collective-permute-done((bf16[64,1536]{1,0:T(8,128)(2,1)S(1)}, bf16[64,1536]{1,0:T(8,128)(2,1)S(1)}, u32[]{:S(2)}, u32[]{:S(2)}) %collective-permute-start.1) | collective-permute-done | bytes 196640 | tf_op jit(solution)/shard_map/ppermute | solution.py:494
  20.4 1.3 %collective-permute-done.2.other_ref = bf16[64,1536]{1,0:T(8,128)(2,1)S(1)} collective-permute-done((bf16[64,1536]{1,0:T(8,128)(2,1)S(1)}, bf16[64,1536]{1,0:T(8,128)(2,1)S(1)}, u32[]{:S(2)}, u32[]{:S(2)}) %collective-permute-start.2) | collective-permute-done | bytes 196640 | tf_op jit(solution)/shard_map/ppermute | solution.py:495
  21.7 1.4 %dispatch.1 = (f32[128,32]{1,0:T(8,128)S(1)}, bf16[32,1536]{1,0:T(8,128)(2,1)S(1)}, bf16[32,1536]{1,0:T(8,128)(2,1)S(1)}, bf16[32,1536]{1,0:T(8,128)(2,1)S(1)}, ...) custom-call(s32[4]{0:T(128)S(1)} %copy-done.3, ...), custom_call_target="tpu_custom_call" | custom-call | tf_op jit(solution)/shard_map/dispatch/pallas_call | solution.py:291
  23.2 0.6 copy-done.1
  23.8 2.6 %collective-permute-start.3 = (bf16[32,1536]{1,0:T(8,128)(2,1)S(1)}, bf16[32,1536]{1,0:T(8,128)(2,1)S(1)}, u32[]{:S(2)}, u32[]{:S(2)}) collective-permute-start(bf16[32,1536]{1,0:T(8,128)(2,1)S(1)} %get-tuple-element.18), channel_id=1, source_target_pairs={{0,4},{4,0},{8,12},{12,8},{16,20},{20,16},{24,28},{28,24},{1,5},{5... | collective-permute-start | bytes 294920 | tf_op jit(solution)/shard_map/ppermute | solution.py:502
  27.0 1.5 %collective-permute-start.5 = (bf16[32,1536]{1,0:T(8,128)(2,1)S(1)}, bf16[32,1536]{1,0:T(8,128)(2,1)S(1)}, u32[]{:S(2)}, u32[]{:S(2)}) collective-permute-start(bf16[32,1536]{1,0:T(8,128)(2,1)S(1)} %get-tuple-element.20), channel_id=1, source_target_pairs={{0,12},{4,8},{8,4},{12,0},{16,28},{20,24},{24,20},{28,16},{1,13},{... | collective-permute-start | bytes 294920 | tf_op jit(solution)/shard_map/ppermute | solution.py:502
  28.4 3.5 %collective-permute-start.6 = (bf16[32,1536]{1,0:T(8,128)(2,1)S(1)}, bf16[32,1536]{1,0:T(8,128)(2,1)S(1)}, u32[]{:S(2)}, u32[]{:S(2)}) collective-permute-start(bf16[32,1536]{1,0:T(8,128)(2,1)S(1)} %get-tuple-element.21), channel_id=1, source_target_pairs={{0,16},{4,20},{8,24},{12,28},{16,0},{20,4},{24,8},{28,12},{1,17},{... | collective-permute-start | bytes 294920 | tf_op jit(solution)/shard_map/ppermute | solution.py:502
  32.4 2.9 %collective-permute-start.8 = (bf16[32,1536]{1,0:T(8,128)(2,1)S(1)}, bf16[32,1536]{1,0:T(8,128)(2,1)S(1)}, u32[]{:S(2)}, u32[]{:S(2)}) collective-permute-start(bf16[32,1536]{1,0:T(8,128)(2,1)S(1)} %get-tuple-element.23), channel_id=1, source_target_pairs={{0,24},{4,28},{8,16},{12,20},{16,8},{20,12},{24,0},{28,4},{1,25},{... | collective-permute-start | bytes 294920 | tf_op jit(solution)/shard_map/ppermute | solution.py:502
  35.3 2.8 %collective-permute-start.9 = (bf16[32,1536]{1,0:T(8,128)(2,1)S(1)}, bf16[32,1536]{1,0:T(8,128)(2,1)S(1)}, u32[]{:S(2)}, u32[]{:S(2)}) collective-permute-start(bf16[32,1536]{1,0:T(8,128)(2,1)S(1)} %get-tuple-element.24), channel_id=1, source_target_pairs={{0,28},{4,24},{8,20},{12,16},{16,12},{20,8},{24,4},{28,0},{1,29},{... | collective-permute-start | bytes 294920 | tf_op jit(solution)/shard_map/ppermute | solution.py:502
  38.1 4.6 %constant_dynamic-slice_fusion.1 = bf16[2,1536,2,384]{3,2,1,0:T(2,128)(2,1)S(1)} fusion(bf16[8,1536,2,384]{3,2,1,0:T(2,128)(2,1)} %param.28, s32[]{:T(128)S(6)} %select_n.48), kind=kLoop, calls=%fused_computation.22 | loop fusion | bytes 9437188 | tf_op jit(solution)/shard_map/dynamic_slice | solution.py:531
  42.7 2.8 %copy.51 = bf16[2,1536,2,384]{3,1,2,0:T(8,128)(2,1)} copy(bf16[2,1536,2,384]{3,2,1,0:T(2,128)(2,1)S(1)} %constant_dynamic-slice_fusion.1) | data formatting | bytes 9437184
  45.4 1.3 %collective-permute-done.7.rest_5_ = bf16[32,1536]{1,0:T(8,128)(2,1)S(1)} collective-permute-done((bf16[32,1536]{1,0:T(8,128)(2,1)S(1)}, bf16[32,1536]{1,0:T(8,128)(2,1)S(1)}, u32[]{:S(2)}, u32[]{:S(2)}) %collective-permute-start.7) | collective-permute-done | bytes 98336 | tf_op jit(solution)/shard_map/ppermute | solution.py:502
  47.4 6.9 %experts.1 = bf16[8,4,32,384]{3,2,1,0:T(8,128)(2,1)} custom-call(s32[4]{0:T(128)} %pad_add_fusion.place_ref, bf16[2,2,1536,384]{3,2,1,0:T(8,128)(2,1)} %bitcast.23, bf16[8,384,1536]{2,1,0:T(8,128)(2,1)} %w_out_hbm.1, bf16[32,1536]{1,0:T(8,128)(2,1)} %copy-done.1, bf16[32,1536]{1,0:T(8,128)(2,1)} %copy-done.7, bf16[32,1536]{1,0:T(8,128)(2,1)} %copy-done.8, ...), custom_call_target="tpu_custom_call" | custom-call | tf_op jit(solution)/shard_map/experts/pallas_call | solution.py:355
  54.3 7.1 %all-to-all-start = ((bf16[32,32,384]{2,1,0:T(8,128)(2,1)}), bf16[32,32,384]{2,1,0:T(8,128)(2,1)S(1)}, u32[]{:S(2)}, u32[]{:S(2)}) async-start(bf16[32,32,384]{2,1,0:T(8,128)(2,1)} %bitcast.24), calls=%async_computation | async-start | bytes 1572864 | tf_op jit(solution)/shard_map/all_to_all | solution.py:544
  62.1 19.9 %all-to-all-done = bf16[32,32,384]{2,1,0:T(8,128)(2,1)S(1)} async-done(((bf16[32,32,384]{2,1,0:T(8,128)(2,1)}), bf16[32,32,384]{2,1,0:T(8,128)(2,1)S(1)}, u32[]{:S(2)}, u32[]{:S(2)}) %all-to-all-start) | async-done | bytes 786464 | tf_op jit(solution)/shard_map/all_to_all | solution.py:544
  82.0 1.8 %combine.1 = (bf16[2,64,384]{2,1,0:T(8,128)(2,1)}, bf16[16,16,384]{2,1,0:T(8,128)(2,1)S(1)}) custom-call(s32[2]{0:T(128)S(1)} %copy-done.6, bf16[1024,384]{1,0:T(8,128)(2,1)S(1)} %bitcast.18, s32[128,4]{1,0:T(8,128)S(1)} %multiply_add_fusion.targets_ref, f32[128,4]{1,0:T(8,128)S(1)} %fusion.3.gates_ref, f32[128,384]{1,0:T(8,128)S(1)} %convert_add_fusion.resid_ref, ...), custom_call_target="tpu_custom_call" | custom-call | tf_op jit(solution)/shard_map/combine/pallas_call | solution.py:404
  83.8 11.6 %all_to_all.10 = bf16[8,2,16,384]{3,2,1,0:T(8,128)(2,1)S(1)} all-to-all(bf16[8,2,16,384]{3,2,1,0:T(8,128)(2,1)S(1)} %bitcast.20), channel_id=1, replica_groups=mesh['req'=8,'tp'=4] {'req'}, dimensions={0} | all-to-all | bytes 393216 | tf_op jit(solution)/shard_map/all_to_all | solution.py:560
  95.4 0.6 reduce_sum.52
  (60 shorter events, 3.6 us)
Async XLA Ops:
  2.0 13.0 %copy-start.14 = (s32[2,64,4]{1,2,0:T(4,128)S(1)}, s32[2,64,4]{1,2,0:T(4,128)}, u32[]{:S(2)}) copy-start(s32[2,64,4]{1,2,0:T(4,128)} %param.27) | copy-start | bytes 6148
  2.0 19.8 %copy-start = (bf16[2,64,1536]{2,1,0:T(8,128)(2,1)S(1)}, bf16[2,64,1536]{2,1,0:T(8,128)(2,1)}, u32[]{:S(2)}) copy-start(bf16[2,64,1536]{2,1,0:T(8,128)(2,1)} %drafts_ref.1) | copy-start | bytes 1179652
  2.0 19.8 %copy-start.2 = (bf16[1536,32]{0,1:T(8,128)(2,1)S(1)}, bf16[1536,32]{0,1:T(8,128)(2,1)}, u32[]{:S(2)}) copy-start(bf16[1536,32]{0,1:T(8,128)(2,1)} %param.26) | copy-start | bytes 294916
  2.0 19.8 %copy-start.3 = (s32[4]{0:T(128)S(1)}, s32[4]{0:T(128)}, u32[]{:S(2)}) copy-start(s32[4]{0:T(128)} %pad_add_fusion.place_ref) | copy-start | bytes 52
  2.0 19.8 %copy-start.4 = (f32[1536]{0:T(1024)S(1)}, f32[1536]{0:T(1024)}, u32[]{:S(2)}) copy-start(f32[1536]{0:T(1024)} %gain_ref.3) | copy-start | bytes 18436
  9.2 1.8 %collective-permute-start = (bf16[64,1536]{1,0:T(8,128)(2,1)}, bf16[64,1536]{1,0:T(8,128)(2,1)S(1)}, u32[]{:S(2)}, u32[]{:S(2)}) collective-permute-start(bf16[64,1536]{1,0:T(8,128)(2,1)} %get-tuple-element.16), channel_id=1, source_target_pairs={{0,1},{1,0},{2,3},{3,2},{4,5},{5,4},{6,7},{7,6},{8,9},{9,8},{10,11... | collective-permute-start | bytes 589832 | tf_op jit(solution)/shard_map/ppermute | solution.py:493
  12.0 8.1 %collective-permute-start.1 = (bf16[64,1536]{1,0:T(8,128)(2,1)S(1)}, bf16[64,1536]{1,0:T(8,128)(2,1)S(1)}, u32[]{:S(2)}, u32[]{:S(2)}) collective-permute-start(bf16[64,1536]{1,0:T(8,128)(2,1)S(1)} %add_convert_fusion.1), channel_id=1, source_target_pairs={{0,2},{1,3},{2,0},{3,1},{4,6},{5,7},{6,4},{7,5},{8,10},{9,11},{10,... | collective-permute-start | bytes 589832 | tf_op jit(solution)/shard_map/ppermute | solution.py:494
  20.2 1.5 %collective-permute-start.2 = (bf16[64,1536]{1,0:T(8,128)(2,1)S(1)}, bf16[64,1536]{1,0:T(8,128)(2,1)S(1)}, u32[]{:S(2)}, u32[]{:S(2)}) collective-permute-start(bf16[64,1536]{1,0:T(8,128)(2,1)S(1)} %add_convert_fusion.half_ref), channel_id=1, source_target_pairs={{0,1},{1,0},{2,3},{3,2},{4,5},{5,4},{6,7},{7,6},{8,9},{9,8},{10,11... | collective-permute-start | bytes 589832 | tf_op jit(solution)/shard_map/ppermute | solution.py:495
  23.8 8.6 %collective-permute-start.3 = (bf16[32,1536]{1,0:T(8,128)(2,1)S(1)}, bf16[32,1536]{1,0:T(8,128)(2,1)S(1)}, u32[]{:S(2)}, u32[]{:S(2)}) collective-permute-start(bf16[32,1536]{1,0:T(8,128)(2,1)S(1)} %get-tuple-element.18), channel_id=1, source_target_pairs={{0,4},{4,0},{8,12},{12,8},{16,20},{20,16},{24,28},{28,24},{1,5},{5... | collective-permute-start | bytes 294920 | tf_op jit(solution)/shard_map/ppermute | solution.py:502
  26.5 8.8 %collective-permute-start.4 = (bf16[32,1536]{1,0:T(8,128)(2,1)S(1)}, bf16[32,1536]{1,0:T(8,128)(2,1)S(1)}, u32[]{:S(2)}, u32[]{:S(2)}) collective-permute-start(bf16[32,1536]{1,0:T(8,128)(2,1)S(1)} %get-tuple-element.19), channel_id=1, source_target_pairs={{0,8},{4,12},{8,0},{12,4},{16,24},{20,28},{24,16},{28,20},{1,9},{5... | collective-permute-start | bytes 294920 | tf_op jit(solution)/shard_map/ppermute | solution.py:502
  27.0 18.4 %collective-permute-start.5 = (bf16[32,1536]{1,0:T(8,128)(2,1)S(1)}, bf16[32,1536]{1,0:T(8,128)(2,1)S(1)}, u32[]{:S(2)}, u32[]{:S(2)}) collective-permute-start(bf16[32,1536]{1,0:T(8,128)(2,1)S(1)} %get-tuple-element.20), channel_id=1, source_target_pairs={{0,12},{4,8},{8,4},{12,0},{16,28},{20,24},{24,20},{28,16},{1,13},{... | collective-permute-start | bytes 294920 | tf_op jit(solution)/shard_map/ppermute | solution.py:502
  28.4 17.0 %collective-permute-start.6 = (bf16[32,1536]{1,0:T(8,128)(2,1)S(1)}, bf16[32,1536]{1,0:T(8,128)(2,1)S(1)}, u32[]{:S(2)}, u32[]{:S(2)}) collective-permute-start(bf16[32,1536]{1,0:T(8,128)(2,1)S(1)} %get-tuple-element.21), channel_id=1, source_target_pairs={{0,16},{4,20},{8,24},{12,28},{16,0},{20,4},{24,8},{28,12},{1,17},{... | collective-permute-start | bytes 294920 | tf_op jit(solution)/shard_map/ppermute | solution.py:502
  31.9 14.8 %collective-permute-start.7 = (bf16[32,1536]{1,0:T(8,128)(2,1)S(1)}, bf16[32,1536]{1,0:T(8,128)(2,1)S(1)}, u32[]{:S(2)}, u32[]{:S(2)}) collective-permute-start(bf16[32,1536]{1,0:T(8,128)(2,1)S(1)} %get-tuple-element.22), channel_id=1, source_target_pairs={{0,20},{4,16},{8,28},{12,24},{16,4},{20,0},{24,12},{28,8},{1,21},{... | collective-permute-start | bytes 294920 | tf_op jit(solution)/shard_map/ppermute | solution.py:502
  32.4 10.2 %copy-start.7 = (bf16[32,1536]{1,0:T(8,128)(2,1)}, bf16[32,1536]{1,0:T(8,128)(2,1)S(1)}, u32[]{:S(2)}) copy-start(bf16[32,1536]{1,0:T(8,128)(2,1)S(1)} %collective-permute-done.3.rest_1_) | copy-start | bytes 294916
  32.4 14.2 %collective-permute-start.8 = (bf16[32,1536]{1,0:T(8,128)(2,1)S(1)}, bf16[32,1536]{1,0:T(8,128)(2,1)S(1)}, u32[]{:S(2)}, u32[]{:S(2)}) collective-permute-start(bf16[32,1536]{1,0:T(8,128)(2,1)S(1)} %get-tuple-element.23), channel_id=1, source_target_pairs={{0,24},{4,28},{8,16},{12,20},{16,8},{20,12},{24,0},{28,4},{1,25},{... | collective-permute-start | bytes 294920 | tf_op jit(solution)/shard_map/ppermute | solution.py:502
  35.3 7.3 %copy-start.8 = (bf16[32,1536]{1,0:T(8,128)(2,1)}, bf16[32,1536]{1,0:T(8,128)(2,1)S(1)}, u32[]{:S(2)}) copy-start(bf16[32,1536]{1,0:T(8,128)(2,1)S(1)} %collective-permute-done.4.rest_2_) | copy-start | bytes 294916
  35.3 11.4 %collective-permute-start.9 = (bf16[32,1536]{1,0:T(8,128)(2,1)S(1)}, bf16[32,1536]{1,0:T(8,128)(2,1)S(1)}, u32[]{:S(2)}, u32[]{:S(2)}) collective-permute-start(bf16[32,1536]{1,0:T(8,128)(2,1)S(1)} %get-tuple-element.24), channel_id=1, source_target_pairs={{0,28},{4,24},{8,20},{12,16},{16,12},{20,8},{24,4},{28,0},{1,29},{... | collective-permute-start | bytes 294920 | tf_op jit(solution)/shard_map/ppermute | solution.py:502
  45.4 1.3 %copy-start.9 = (bf16[32,1536]{1,0:T(8,128)(2,1)}, bf16[32,1536]{1,0:T(8,128)(2,1)S(1)}, u32[]{:S(2)}) copy-start(bf16[32,1536]{1,0:T(8,128)(2,1)S(1)} %collective-permute-done.5.rest_3_) | copy-start | bytes 294916
  45.4 1.3 %copy-start.10 = (bf16[32,1536]{1,0:T(8,128)(2,1)}, bf16[32,1536]{1,0:T(8,128)(2,1)S(1)}, u32[]{:S(2)}) copy-start(bf16[32,1536]{1,0:T(8,128)(2,1)S(1)} %collective-permute-done.6.rest_4_) | copy-start | bytes 294916
  46.7 0.7 copy-start.12
  46.7 0.7 copy-start.13
  47.4 34.6 %copy-start.5 = (s32[2,64]{1,0:T(2,128)S(1)}, s32[2,64]{1,0:T(2,128)}, u32[]{:S(2)}) copy-start(s32[2,64]{1,0:T(2,128)} %slots_ref.1) | copy-start | bytes 1540
  47.4 34.6 %copy-start.6 = (s32[2]{0:T(128)S(1)}, s32[2]{0:T(128)}, u32[]{:S(2)}) copy-start(s32[2]{0:T(128)} %order_ref.1) | copy-start | bytes 28
  54.3 27.7 %all-to-all-start = ((bf16[32,32,384]{2,1,0:T(8,128)(2,1)}), bf16[32,32,384]{2,1,0:T(8,128)(2,1)S(1)}, u32[]{:S(2)}, u32[]{:S(2)}) async-start(bf16[32,32,384]{2,1,0:T(8,128)(2,1)} %bitcast.24), calls=%async_computation | async-start | bytes 1572864 | tf_op jit(solution)/shard_map/all_to_all | solution.py:544
  (2 other events, 1.3 us)

commit v3 on v2

--- a/solution.py
+++ b/solution.py
@@ -14,9 +14,9 @@
 EPSILON = 1e-06
 THETA = 1000000.0
 LOG2E = 1.4426950408889634
-BLOCK = 512
+BLOCK = 1536
 WHOLE_VMEM = 60 * 1024 * 1024
-SOME_VMEM = 32 * 1024 * 1024
+SOME_VMEM = 20 * 1024 * 1024
 
 
 def rms_norm(values, gain_vec):
@@ -33,12 +33,11 @@
 
 
 def attention_kernel(
+    tp_count,
     lengths_ref,
-    place_ref,
-    gain_ref,
-    freqs_ref,
-    depths_ref,
-    mask_ref,
+    gain_hbm,
+    depths_hbm,
+    mask_hbm,
     drafts_hbm,
     wq_hbm,
     wkv_hbm,
@@ -46,6 +45,9 @@
     cache_hbm,
     mine_ref,
     theirs_ref,
+    gain_ref,
+    depths_ref,
+    mask_ref,
     drafts,
     wq,
     wk,
@@ -62,8 +64,9 @@
     kv_heads = cache_hbm.shape[2]
     local_heads = wq.shape[1] // head_dim
     block = scores.shape[2]
-    kv_head = place_ref[0]
-    first = place_ref[1]
+    tp_rank = lax.axis_index("tp")
+    kv_head = tp_rank * local_heads // (local_heads * tp_count // kv_heads)
+    first = lax.rem(tp_rank, 2)
 
     def column_copy(target, which, sem):
         start = pl.multiple_of((which * kv_heads + kv_head) * head_dim, head_dim)
@@ -80,6 +83,13 @@
 
     copy_d = pltpu.make_async_copy(drafts_hbm, drafts, weight_sem.at[4])
     copy_d.start()
+    small = [
+        pltpu.make_async_copy(gain_hbm, gain_ref, weight_sem.at[5]),
+        pltpu.make_async_copy(depths_hbm, depths_ref, weight_sem.at[6]),
+        pltpu.make_async_copy(mask_hbm, mask_ref, weight_sem.at[7]),
+    ]
+    for copy in small:
+        copy.start()
     copy_q = pltpu.make_async_copy(wq_hbm, wq, weight_sem.at[0])
     copy_k = column_copy(wk, 0, weight_sem.at[1])
     copy_v = column_copy(wv, 1, weight_sem.at[2])
@@ -99,16 +109,23 @@
     copy_o.start()
 
     copy_d.wait()
+    small[0].wait()
     inputs = drafts[...].astype(jnp.float32).reshape(req_dev * tree, width)
     normed = rms_norm(inputs, gain_ref[...][None, :]).astype(jnp.bfloat16)
+    small[1].wait()
+    small[2].wait()
     at = [
         column_of(depths_ref[request : request + 1, :].astype(jnp.float32))
         + limits[request].astype(jnp.float32)
         for request in range(req_dev)
     ]
-    angles = jnp.concatenate(at, axis=0) * freqs_ref[...]
+    lane = lax.broadcasted_iota(jnp.int32, (req_dev * tree, head_dim), 1)
+    half_dim = head_dim // 2
+    freqs = jnp.exp(
+        -jnp.log(THETA) * lax.rem(lane, half_dim).astype(jnp.float32) / half_dim
+    )
+    angles = jnp.concatenate(at, axis=0) * freqs
     cosine = jnp.cos(angles)
-    lane = lax.broadcasted_iota(jnp.int32, angles.shape, 1)
     sine = jnp.sin(angles) * jnp.where(lane < head_dim // 2, -1.0, 1.0)
 
     def turned(vectors):
@@ -203,26 +220,26 @@
 
 
 def attention_part(
-    drafts, gain, w_query, key_value_weight, w_output, cache, lengths, tree_mask, depths, place
+    drafts, gain, w_query, key_value_weight, w_output, cache, lengths, tree_mask, depths, tp_count
 ):
     req_dev, tree, width = drafts.shape
     head_dim = cache.shape[-1]
     longest = cache.shape[3]
     block = min(BLOCK, longest)
     local = w_query.shape[1]
-    half_dim = head_dim // 2
-    freqs = jnp.exp(-jnp.log(THETA) * jnp.arange(half_dim, dtype=jnp.float32) / half_dim)
-    freqs = jnp.tile(freqs, 2).reshape(1, head_dim)
     whole = pl.BlockSpec(memory_space=pltpu.VMEM)
     scalar = pl.BlockSpec(memory_space=pltpu.SMEM)
     anywhere = pl.BlockSpec(memory_space=pl.ANY)
     bf16 = jnp.bfloat16
     return pl.pallas_call(
-        attention_kernel,
+        functools.partial(attention_kernel, tp_count),
         out_shape=[jax.ShapeDtypeStruct((tree, width), bf16)] * 2,
-        in_specs=[scalar] * 2 + [whole] * 4 + [anywhere] * 5,
+        in_specs=[scalar] + [anywhere] * 8,
         out_specs=[whole] * 2,
         scratch_shapes=[
+            pltpu.VMEM((width,), jnp.float32),
+            pltpu.VMEM((req_dev, tree), jnp.int32),
+            pltpu.VMEM((req_dev, tree, tree), jnp.int32),
             pltpu.VMEM((req_dev, tree, width), bf16),
             pltpu.VMEM((width, local), bf16),
             pltpu.VMEM((width, head_dim), bf16),
@@ -231,16 +248,14 @@
             pltpu.VMEM((req_dev, longest, head_dim), bf16),
             pltpu.VMEM((req_dev, longest, head_dim), bf16),
             pltpu.VMEM((longest // block, local // head_dim * tree, block), jnp.float32),
-            pltpu.SemaphoreType.DMA((5,)),
+            pltpu.SemaphoreType.DMA((8,)),
             pltpu.SemaphoreType.DMA((req_dev, 2, longest // block)),
         ],
         compiler_params=pltpu.CompilerParams(vmem_limit_bytes=WHOLE_VMEM),
         name="attention",
     )(
         lengths,
-        place,
         gain,
-        freqs,
         depths,
         tree_mask,
         drafts,
@@ -301,72 +316,71 @@
     return logits, sent
 
 
-def expert_kernel(place_ref, w_in_hbm, w_out_hbm, *rest):
-    *row_refs, out_ref, rows, wi, wo, in_sem, out_sem = rest
+def fetch_kernel(place_ref, w_in_hbm, w_out_hbm, wi, wo, in_sem, out_sem):
     halves = wi.shape[0]
-    in_copies = []
-    for half in range(halves):
-        for which in range(2):
-            copy = pltpu.make_async_copy(
-                w_in_hbm.at[half, which], wi.at[half, which], in_sem.at[half, which]
-            )
-            copy.start()
-            in_copies.append(copy)
-    out_copies = []
-    for half in range(halves):
-        copy = pltpu.make_async_copy(
-            w_out_hbm.at[place_ref[2] * halves + half], wo.at[half], out_sem.at[half]
-        )
-        copy.start()
-        out_copies.append(copy)
+    inward = pltpu.make_async_copy(w_in_hbm, wi, in_sem)
+    outward = pltpu.make_async_copy(
+        w_out_hbm.at[pl.ds(place_ref[2] * halves, halves)], wo, out_sem
+    )
+    inward.start()
+    outward.start()
+    inward.wait()
+    outward.wait()
+
+
+def fetched(w_in_own, w_out, place):
+    halves = w_in_own.shape[0]
+    whole = pl.BlockSpec(memory_space=pltpu.VMEM)
+    scalar = pl.BlockSpec(memory_space=pltpu.SMEM)
+    anywhere = pl.BlockSpec(memory_space=pl.ANY)
+    return pl.pallas_call(
+        fetch_kernel,
+        out_shape=[
+            jax.ShapeDtypeStruct(w_in_own.shape, w_in_own.dtype),
+            jax.ShapeDtypeStruct((halves,) + w_out.shape[1:], w_out.dtype),
+        ],
+        in_specs=[scalar, anywhere, anywhere],
+        out_specs=[whole] * 2,
+        scratch_shapes=[pltpu.SemaphoreType.DMA, pltpu.SemaphoreType.DMA],
+        compiler_params=pltpu.CompilerParams(vmem_limit_bytes=SOME_VMEM),
+        name="fetch",
+    )(place, w_in_own, w_out)
+
+
+def expert_kernel(place_ref, wi, wo, *rest):
+    *row_refs, out_ref, rows = rest
     share = row_refs[0].shape[0]
     for step, row_ref in enumerate(row_refs):
         start = pl.multiple_of((place_ref[3] ^ step) * share, share)
         rows[pl.ds(start, share)] = row_ref[...]
     taken = rows[...]
     acts = []
-    for half in range(halves):
-        in_copies[2 * half].wait()
+    for half in range(wi.shape[0]):
         gate = jnp.dot(taken, wi[half, 0], preferred_element_type=jnp.float32)
-        in_copies[2 * half + 1].wait()
         upper = jnp.dot(taken, wi[half, 1], preferred_element_type=jnp.float32)
         acts.append((jnp.maximum(gate, 0.0) * upper).astype(jnp.bfloat16))
-    for copy in out_copies:
-        copy.wait()
+    acts = jnp.concatenate(acts, axis=1)
     groups, ranks, _, quarter = out_ref.shape
     for rank in range(ranks):
         columns = slice(rank * quarter, (rank + 1) * quarter)
-        made = jnp.dot(acts[0], wo[0, :, columns], preferred_element_type=jnp.float32)
-        for half in range(1, halves):
-            made = made + jnp.dot(
-                acts[half], wo[half, :, columns], preferred_element_type=jnp.float32
-            )
+        made = jnp.dot(acts, wo[:, columns], preferred_element_type=jnp.float32)
         out_ref[:, rank] = made.astype(jnp.bfloat16).reshape(groups, share, quarter)
 
 
-def expert_rows(rows, w_in_own, w_out, place, ranks):
+def expert_rows(rows, w_in_own, w_out_own, place, ranks):
     share, width = rows[0].shape
     groups = len(rows)
-    halves, _, _, hidden = w_in_own.shape
-    quarter = width // ranks
     whole = pl.BlockSpec(memory_space=pltpu.VMEM)
     scalar = pl.BlockSpec(memory_space=pltpu.SMEM)
-    anywhere = pl.BlockSpec(memory_space=pl.ANY)
     return pl.pallas_call(
         expert_kernel,
-        out_shape=jax.ShapeDtypeStruct((groups, ranks, share, quarter), jnp.bfloat16),
-        in_specs=[scalar] + [anywhere] * 2 + [whole] * groups,
+        out_shape=jax.ShapeDtypeStruct((groups, ranks, share, width // ranks), jnp.bfloat16),
+        in_specs=[scalar] + [whole] * (2 + groups),
         out_specs=whole,
-        scratch_shapes=[
-            pltpu.VMEM((groups * share, width), jnp.bfloat16),
-            pltpu.VMEM((halves, 2, width, hidden), jnp.bfloat16),
-            pltpu.VMEM((halves, hidden, width), jnp.bfloat16),
-            pltpu.SemaphoreType.DMA((halves, 2)),
-            pltpu.SemaphoreType.DMA((halves,)),
-        ],
-        compiler_params=pltpu.CompilerParams(vmem_limit_bytes=WHOLE_VMEM),
+        scratch_shapes=[pltpu.VMEM((groups * share, width), jnp.bfloat16)],
+        compiler_params=pltpu.CompilerParams(vmem_limit_bytes=SOME_VMEM),
         name="experts",
-    )(place, w_in_own, w_out, *rows)
+    )(place, w_in_own, w_out_own, *rows)
 
 
 def combine_kernel(
@@ -482,7 +496,7 @@
         lengths,
         tree_mask,
         depths,
-        place,
+        tp_count,
     )
     near = [(i, i ^ 1) for i in range(tp_count)]
     far = [(i, i ^ 2) for i in range(tp_count)]
@@ -529,7 +543,8 @@
 
     if by_expert:
         own_in = lax.dynamic_slice_in_dim(w_in, tp_rank * 2, 2, 0).transpose(0, 2, 1, 3)
-        produced = expert_rows(arrived, own_in, w_out, place, tp_count)
+        own_in, own_out = fetched(own_in, w_out, place)
+        produced = expert_rows(arrived, own_in, own_out.reshape(-1, width), place, tp_count)
     else:
         gates = jnp.repeat(gates, 2, axis=1)
         rows_in = arrived.reshape(req_count, pieces, share, width)

time: 96.3 us -> 90 us (0.935)
  starting transfers between devices: 24.9 us -> 22.4 us
  local copies, waits for them, and re-layouts: 9.99 us -> 7.63 us
  Pallas kernels: 17.3 us -> 16.3 us
    unnamed x32 -> x20, local copies, waits for them, and re-layouts: 4.2 us -> 1.33 us
    pallas_call x1, Pallas kernels: 6.88 us -> 4.1 us  [expert_rows(): pl.pallas_call(expert_kernel, out_shape=jax.ShapeDtypeStruct((groups, ran...]
    ppermute x7, starting transfers between devices: 14.2 us -> 11.9 us  [on_device(): lax.ppermute(sent[step], 'req', [(i, i ^ step) for i in range(req_count)])]
    pallas_call x1 -> x2, Pallas kernels: 7.26 us -> 8.98 us  [the longest x1 7.94 us: attention_part(): pl.pallas_call(functools.partial(attention_kernel, tp_count), out_shape=[...]
    dynamic_slice x1, local copies, waits for them, and re-layouts: 4.55 us -> 5.75 us  [on_device(): lax.dynamic_slice_in_dim(w_in, tp_rank * 2, 2, 0).transpose(0, 2, 1, 3)]
  transfers between devices with their start and end apart: 11 -> 11, of which waited for: 5 -> 5; matrix products, arithmetic and copies ran while one was open for 9% -> 9% of each run, Pallas kernels for 0% -> 1%
where the time goes in v3:
time: 90 us; the launch traced here: 89.7 us
  waiting for transfers between devices  28.6 us (32%)
  starting transfers between devices  22.4 us (25%)
  Pallas kernels  16.3 us (18%)
  blocking collectives  11.6 us (13%)
  local copies, waits for them, and re-layouts  7.63 us (8%)
  other arithmetic  2.32 us (3%)
    all_to_all x1, waiting for transfers between devices, on_device(): lax.all_to_all(produced.reshape(req_count * tp_count, -1, quarter), ('req...  19.9 us
    ppermute x7, starting transfers between devices, on_device(): lax.ppermute(sent[step], 'req', [(i, i ^ step) for i in range(req_count)])  11.9 us
    all_to_all x1, blocking collectives, on_device(): lax.all_to_all(posted.reshape(req_count, req_dev, KEEP, quarter), 'req',...  11.6 us
    pallas_call x1, Pallas kernels, attention_part(): pl.pallas_call(functools.partial(attention_kernel, tp_count), out_shape=[...  7.94 us
    all_to_all x1, starting transfers between devices, on_device(): lax.all_to_all(produced.reshape(req_count * tp_count, -1, quarter), ('req...  6.92 us
    dynamic_slice x1, local copies, waits for them, and re-layouts, on_device(): lax.dynamic_slice_in_dim(w_in, tp_rank * 2, 2, 0).transpose(0, 2, 1, 3)  5.75 us
    ppermute x1, waiting for transfers between devices, on_device(): half = added(chip, lax.ppermute(chip, 'tp', far))  5.14 us
    pallas_call x1, Pallas kernels, expert_rows(): pl.pallas_call(expert_kernel, out_shape=jax.ShapeDtypeStruct((groups, ran...  4.1 us
  transfers between devices with their start and end apart: 11, of which 5 were waited for; matrix products, arithmetic and copies ran while one was open for 9% of the time, Pallas kernels for 1%

profile of v3, /device:TPU:0, one launch (start us, length us, event | category | flops | bytes accessed | tf_op | source)
XLA Modules:
  0.0 89.7 jit_solution(7885367890655245383)
XLA Ops:
  0.7 7.9 %attention.1 = (bf16[64,1536]{1,0:T(8,128)(2,1)}, bf16[64,1536]{1,0:T(8,128)(2,1)}) custom-call(s32[2]{0:T(128)} %lengths_ref.1, f32[1536]{0:T(1024)} %gain_hbm.1, s32[2,64]{1,0:T(2,128)} %depths_hbm.1, s32[2,64,64]{2,1,0:T(8,128)} %mask_hbm.1, bf16[2,64,1536]{2,1,0:T(8,128)(2,1)} %drafts_ref.1, bf16[1536,384]{1,0:T(8,128)(2,1)} %wq_hbm.1, ...), custom_call_target="tpu_custom_call" | custom-call | tf_op jit(solution)/shard_map/attention/pallas_call | solution.py:234
  9.6 0.8 collective-permute-done
  10.4 1.0 %add_convert_fusion.1 = bf16[64,1536]{1,0:T(8,128)(2,1)S(1)} fusion(bf16[64,1536]{1,0:T(8,128)(2,1)S(1)} %collective-permute-done, bf16[64,1536]{1,0:T(8,128)(2,1)} %get-tuple-element.19), kind=kLoop, calls=%fused_computation.6 | loop fusion | flops 393216 | bytes 589824 | tf_op jit(solution)/shard_map/convert_element_type | solution.py:505
  11.4 2.9 %collective-permute-start.1 = (bf16[64,1536]{1,0:T(8,128)(2,1)S(1)}, bf16[64,1536]{1,0:T(8,128)(2,1)S(1)}, u32[]{:S(2)}, u32[]{:S(2)}) collective-permute-start(bf16[64,1536]{1,0:T(8,128)(2,1)S(1)} %add_convert_fusion.1), channel_id=1, source_target_pairs={{0,2},{1,3},{2,0},{3,1},{4,6},{5,7},{6,4},{7,5},{8,10},{9,11},{10,... | collective-permute-start | bytes 589832 | tf_op jit(solution)/shard_map/ppermute | solution.py:508
  14.4 5.1 %collective-permute-done.1 = bf16[64,1536]{1,0:T(8,128)(2,1)S(1)} collective-permute-done((bf16[64,1536]{1,0:T(8,128)(2,1)S(1)}, bf16[64,1536]{1,0:T(8,128)(2,1)S(1)}, u32[]{:S(2)}, u32[]{:S(2)}) %collective-permute-start.1) | collective-permute-done | bytes 196640 | tf_op jit(solution)/shard_map/ppermute | solution.py:508
  19.8 1.3 %collective-permute-done.2.other_ref = bf16[64,1536]{1,0:T(8,128)(2,1)S(1)} collective-permute-done((bf16[64,1536]{1,0:T(8,128)(2,1)S(1)}, bf16[64,1536]{1,0:T(8,128)(2,1)S(1)}, u32[]{:S(2)}, u32[]{:S(2)}) %collective-permute-start.2) | collective-permute-done | bytes 196640 | tf_op jit(solution)/shard_map/ppermute | solution.py:509
  21.1 1.4 %dispatch.1 = (f32[128,32]{1,0:T(8,128)S(1)}, bf16[32,1536]{1,0:T(8,128)(2,1)S(1)}, bf16[32,1536]{1,0:T(8,128)(2,1)S(1)}, bf16[32,1536]{1,0:T(8,128)(2,1)S(1)}, ...) custom-call(s32[4]{0:T(128)S(1)} %pad_add_fusion.place_ref, ...), custom_call_target="tpu_custom_call" | custom-call | tf_op jit(solution)/shard_map/dispatch/pallas_call | solution.py:306
  22.5 1.8 %collective-permute-start.3 = (bf16[32,1536]{1,0:T(8,128)(2,1)S(1)}, bf16[32,1536]{1,0:T(8,128)(2,1)S(1)}, u32[]{:S(2)}, u32[]{:S(2)}) collective-permute-start(bf16[32,1536]{1,0:T(8,128)(2,1)S(1)} %get-tuple-element.22), channel_id=1, source_target_pairs={{0,4},{4,0},{8,12},{12,8},{16,20},{20,16},{24,28},{28,24},{1,5},{5... | collective-permute-start | bytes 294920 | tf_op jit(solution)/shard_map/ppermute | solution.py:516
  24.4 1.6 %collective-permute-start.4 = (bf16[32,1536]{1,0:T(8,128)(2,1)S(1)}, bf16[32,1536]{1,0:T(8,128)(2,1)S(1)}, u32[]{:S(2)}, u32[]{:S(2)}) collective-permute-start(bf16[32,1536]{1,0:T(8,128)(2,1)S(1)} %get-tuple-element.23), channel_id=1, source_target_pairs={{0,8},{4,12},{8,0},{12,4},{16,24},{20,28},{24,16},{28,20},{1,9},{5... | collective-permute-start | bytes 294920 | tf_op jit(solution)/shard_map/ppermute | solution.py:516
  26.1 2.8 %collective-permute-start.6 = (bf16[32,1536]{1,0:T(8,128)(2,1)S(1)}, bf16[32,1536]{1,0:T(8,128)(2,1)S(1)}, u32[]{:S(2)}, u32[]{:S(2)}) collective-permute-start(bf16[32,1536]{1,0:T(8,128)(2,1)S(1)} %get-tuple-element.25), channel_id=1, source_target_pairs={{0,16},{4,20},{8,24},{12,28},{16,0},{20,4},{24,8},{28,12},{1,17},{... | collective-permute-start | bytes 294920 | tf_op jit(solution)/shard_map/ppermute | solution.py:516
  28.9 1.3 %collective-permute-start.7 = (bf16[32,1536]{1,0:T(8,128)(2,1)S(1)}, bf16[32,1536]{1,0:T(8,128)(2,1)S(1)}, u32[]{:S(2)}, u32[]{:S(2)}) collective-permute-start(bf16[32,1536]{1,0:T(8,128)(2,1)S(1)} %get-tuple-element.26), channel_id=1, source_target_pairs={{0,20},{4,16},{8,28},{12,24},{16,4},{20,0},{24,12},{28,8},{1,21},{... | collective-permute-start | bytes 294920 | tf_op jit(solution)/shard_map/ppermute | solution.py:516
  30.2 2.9 %collective-permute-start.8 = (bf16[32,1536]{1,0:T(8,128)(2,1)S(1)}, bf16[32,1536]{1,0:T(8,128)(2,1)S(1)}, u32[]{:S(2)}, u32[]{:S(2)}) collective-permute-start(bf16[32,1536]{1,0:T(8,128)(2,1)S(1)} %get-tuple-element.27), channel_id=1, source_target_pairs={{0,24},{4,28},{8,16},{12,20},{16,8},{20,12},{24,0},{28,4},{1,25},{... | collective-permute-start | bytes 294920 | tf_op jit(solution)/shard_map/ppermute | solution.py:516
  33.1 1.3 %collective-permute-start.9 = (bf16[32,1536]{1,0:T(8,128)(2,1)S(1)}, bf16[32,1536]{1,0:T(8,128)(2,1)S(1)}, u32[]{:S(2)}, u32[]{:S(2)}) collective-permute-start(bf16[32,1536]{1,0:T(8,128)(2,1)S(1)} %get-tuple-element.28), channel_id=1, source_target_pairs={{0,28},{4,24},{8,20},{12,16},{16,12},{20,8},{24,4},{28,0},{1,29},{... | collective-permute-start | bytes 294920 | tf_op jit(solution)/shard_map/ppermute | solution.py:516
  34.5 5.7 %constant_dynamic-slice_fusion.1 = bf16[2,1536,2,384]{3,2,1,0:T(2,128)(2,1)S(1)} fusion(bf16[8,1536,2,384]{3,2,1,0:T(2,128)(2,1)} %param.28, s32[]{:T(128)S(6)} %select_n.48), kind=kLoop, calls=%fused_computation.22 | loop fusion | bytes 9437188 | tf_op jit(solution)/shard_map/dynamic_slice | solution.py:545
  40.2 0.6 copy.51
  40.9 0.6 slice-done.2
  41.5 1.0 %fetch.1 = (bf16[2,2,1536,384]{3,2,1,0:T(8,128)(2,1)S(1)}, bf16[2,384,1536]{2,1,0:T(8,128)(2,1)S(1)}) custom-call(s32[4]{0:T(128)S(1)} %pad_add_fusion.place_ref, bf16[2,2,1536,384]{3,2,1,0:T(8,128)(2,1)S(1)} %bitcast.19, bf16[8,384,1536]{2,1,0:T(8,128)(2,1)S(1)} %bitcast.21), custom_call_target="tpu_custom_call" | custom-call | tf_op jit(solution)/shard_map/fetch/pallas_call | solution.py:336
  42.5 1.4 %collective-permute-done.7.rest_5_ = bf16[32,1536]{1,0:T(8,128)(2,1)S(1)} collective-permute-done((bf16[32,1536]{1,0:T(8,128)(2,1)S(1)}, bf16[32,1536]{1,0:T(8,128)(2,1)S(1)}, u32[]{:S(2)}, u32[]{:S(2)}) %collective-permute-start.7) | collective-permute-done | bytes 98336 | tf_op jit(solution)/shard_map/ppermute | solution.py:516
  44.0 4.1 %experts.1 = bf16[8,4,32,384]{3,2,1,0:T(8,128)(2,1)} custom-call(s32[4]{0:T(128)S(1)} %pad_add_fusion.place_ref, bf16[2,2,1536,384]{3,2,1,0:T(8,128)(2,1)S(1)} %get-tuple-element.17.wi, bf16[768,1536]{1,0:T(8,128)(2,1)S(1)} %bitcast.23, bf16[32,1536]{1,0:T(8,128)(2,1)S(1)} %get-tuple-element.21.rest_0_, bf16[32,1536]{1,0:T(8,128)(2,1)S(1)} %collective-permute-done.3.rest_1_, ...), custom_call_target="tpu_custom_call" | custom-call | tf_op jit(solution)/shard_map/experts/pallas_call | solution.py:375
  48.1 6.9 %all-to-all-start = ((bf16[32,32,384]{2,1,0:T(8,128)(2,1)}), bf16[32,32,384]{2,1,0:T(8,128)(2,1)S(1)}, u32[]{:S(2)}, u32[]{:S(2)}) async-start(bf16[32,32,384]{2,1,0:T(8,128)(2,1)} %bitcast.11), calls=%async_computation | async-start | bytes 1572864 | tf_op jit(solution)/shard_map/all_to_all | solution.py:559
  55.7 19.9 %all-to-all-done = bf16[32,32,384]{2,1,0:T(8,128)(2,1)S(1)} async-done(((bf16[32,32,384]{2,1,0:T(8,128)(2,1)}), bf16[32,32,384]{2,1,0:T(8,128)(2,1)S(1)}, u32[]{:S(2)}, u32[]{:S(2)}) %all-to-all-start) | async-done | bytes 786464 | tf_op jit(solution)/shard_map/all_to_all | solution.py:559
  75.6 1.8 %combine.1 = (bf16[2,64,384]{2,1,0:T(8,128)(2,1)}, bf16[16,16,384]{2,1,0:T(8,128)(2,1)S(1)}) custom-call(s32[2]{0:T(128)S(1)} %copy-done.4, bf16[1024,384]{1,0:T(8,128)(2,1)S(1)} %bitcast.22, s32[128,4]{1,0:T(8,128)S(1)} %multiply_add_fusion.targets_ref, f32[128,4]{1,0:T(8,128)S(1)} %fusion.3.gates_ref, f32[128,384]{1,0:T(8,128)S(1)} %convert_add_fusion.resid_ref, ...), custom_call_target="tpu_custom_call" | custom-call | tf_op jit(solution)/shard_map/combine/pallas_call | solution.py:418
  77.4 11.6 %all_to_all.10 = bf16[8,2,16,384]{3,2,1,0:T(8,128)(2,1)S(1)} all-to-all(bf16[8,2,16,384]{3,2,1,0:T(8,128)(2,1)S(1)} %bitcast.25), channel_id=1, replica_groups=mesh['req'=8,'tp'=4] {'req'}, dimensions={0} | all-to-all | bytes 393216 | tf_op jit(solution)/shard_map/all_to_all | solution.py:575
  89.0 0.6 reduce_sum.52
  (47 shorter events, 2.2 us)
Async XLA Ops:
  0.6 20.5 %copy-start = (bf16[2,64,1536]{2,1,0:T(8,128)(2,1)S(1)}, bf16[2,64,1536]{2,1,0:T(8,128)(2,1)}, u32[]{:S(2)}) copy-start(bf16[2,64,1536]{2,1,0:T(8,128)(2,1)} %drafts_ref.1) | copy-start | bytes 1179652
  0.6 8.5 %copy-start.5 = (s32[2,64,4]{1,2,0:T(4,128)S(1)}, s32[2,64,4]{1,2,0:T(4,128)}, u32[]{:S(2)}) copy-start(s32[2,64,4]{1,2,0:T(4,128)} %param.27) | copy-start | bytes 6148
  0.7 20.5 %copy-start.1 = (bf16[1536,32]{0,1:T(8,128)(2,1)S(1)}, bf16[1536,32]{0,1:T(8,128)(2,1)}, u32[]{:S(2)}) copy-start(bf16[1536,32]{0,1:T(8,128)(2,1)} %param.26) | copy-start | bytes 294916
  0.7 20.5 %copy-start.2 = (f32[1536]{0:T(1024)S(1)}, f32[1536]{0:T(1024)}, u32[]{:S(2)}) copy-start(f32[1536]{0:T(1024)} %gain_ref.1) | copy-start | bytes 18436
  8.6 1.8 %collective-permute-start = (bf16[64,1536]{1,0:T(8,128)(2,1)}, bf16[64,1536]{1,0:T(8,128)(2,1)S(1)}, u32[]{:S(2)}, u32[]{:S(2)}) collective-permute-start(bf16[64,1536]{1,0:T(8,128)(2,1)} %get-tuple-element.20), channel_id=1, source_target_pairs={{0,1},{1,0},{2,3},{3,2},{4,5},{5,4},{6,7},{7,6},{8,9},{9,8},{10,11... | collective-permute-start | bytes 589832 | tf_op jit(solution)/shard_map/ppermute | solution.py:507
  11.4 8.1 %collective-permute-start.1 = (bf16[64,1536]{1,0:T(8,128)(2,1)S(1)}, bf16[64,1536]{1,0:T(8,128)(2,1)S(1)}, u32[]{:S(2)}, u32[]{:S(2)}) collective-permute-start(bf16[64,1536]{1,0:T(8,128)(2,1)S(1)} %add_convert_fusion.1), channel_id=1, source_target_pairs={{0,2},{1,3},{2,0},{3,1},{4,6},{5,7},{6,4},{7,5},{8,10},{9,11},{10,... | collective-permute-start | bytes 589832 | tf_op jit(solution)/shard_map/ppermute | solution.py:508
  19.6 1.5 %collective-permute-start.2 = (bf16[64,1536]{1,0:T(8,128)(2,1)S(1)}, bf16[64,1536]{1,0:T(8,128)(2,1)S(1)}, u32[]{:S(2)}, u32[]{:S(2)}) collective-permute-start(bf16[64,1536]{1,0:T(8,128)(2,1)S(1)} %add_convert_fusion.half_ref), channel_id=1, source_target_pairs={{0,1},{1,0},{2,3},{3,2},{4,5},{5,4},{6,7},{7,6},{8,9},{9,8},{10,11... | collective-permute-start | bytes 589832 | tf_op jit(solution)/shard_map/ppermute | solution.py:509
  22.5 7.7 %collective-permute-start.3 = (bf16[32,1536]{1,0:T(8,128)(2,1)S(1)}, bf16[32,1536]{1,0:T(8,128)(2,1)S(1)}, u32[]{:S(2)}, u32[]{:S(2)}) collective-permute-start(bf16[32,1536]{1,0:T(8,128)(2,1)S(1)} %get-tuple-element.22), channel_id=1, source_target_pairs={{0,4},{4,0},{8,12},{12,8},{16,20},{20,16},{24,28},{28,24},{1,5},{5... | collective-permute-start | bytes 294920 | tf_op jit(solution)/shard_map/ppermute | solution.py:516
  24.4 8.8 %collective-permute-start.4 = (bf16[32,1536]{1,0:T(8,128)(2,1)S(1)}, bf16[32,1536]{1,0:T(8,128)(2,1)S(1)}, u32[]{:S(2)}, u32[]{:S(2)}) collective-permute-start(bf16[32,1536]{1,0:T(8,128)(2,1)S(1)} %get-tuple-element.23), channel_id=1, source_target_pairs={{0,8},{4,12},{8,0},{12,4},{16,24},{20,28},{24,16},{28,20},{1,9},{5... | collective-permute-start | bytes 294920 | tf_op jit(solution)/shard_map/ppermute | solution.py:516
  25.9 16.6 %collective-permute-start.5 = (bf16[32,1536]{1,0:T(8,128)(2,1)S(1)}, bf16[32,1536]{1,0:T(8,128)(2,1)S(1)}, u32[]{:S(2)}, u32[]{:S(2)}) collective-permute-start(bf16[32,1536]{1,0:T(8,128)(2,1)S(1)} %get-tuple-element.24), channel_id=1, source_target_pairs={{0,12},{4,8},{8,4},{12,0},{16,28},{20,24},{24,20},{28,16},{1,13},{... | collective-permute-start | bytes 294920 | tf_op jit(solution)/shard_map/ppermute | solution.py:516
  26.1 16.4 %collective-permute-start.6 = (bf16[32,1536]{1,0:T(8,128)(2,1)S(1)}, bf16[32,1536]{1,0:T(8,128)(2,1)S(1)}, u32[]{:S(2)}, u32[]{:S(2)}) collective-permute-start(bf16[32,1536]{1,0:T(8,128)(2,1)S(1)} %get-tuple-element.25), channel_id=1, source_target_pairs={{0,16},{4,20},{8,24},{12,28},{16,0},{20,4},{24,8},{28,12},{1,17},{... | collective-permute-start | bytes 294920 | tf_op jit(solution)/shard_map/ppermute | solution.py:516
  28.9 15.0 %collective-permute-start.7 = (bf16[32,1536]{1,0:T(8,128)(2,1)S(1)}, bf16[32,1536]{1,0:T(8,128)(2,1)S(1)}, u32[]{:S(2)}, u32[]{:S(2)}) collective-permute-start(bf16[32,1536]{1,0:T(8,128)(2,1)S(1)} %get-tuple-element.26), channel_id=1, source_target_pairs={{0,20},{4,16},{8,28},{12,24},{16,4},{20,0},{24,12},{28,8},{1,21},{... | collective-permute-start | bytes 294920 | tf_op jit(solution)/shard_map/ppermute | solution.py:516
  30.2 13.7 %collective-permute-start.8 = (bf16[32,1536]{1,0:T(8,128)(2,1)S(1)}, bf16[32,1536]{1,0:T(8,128)(2,1)S(1)}, u32[]{:S(2)}, u32[]{:S(2)}) collective-permute-start(bf16[32,1536]{1,0:T(8,128)(2,1)S(1)} %get-tuple-element.27), channel_id=1, source_target_pairs={{0,24},{4,28},{8,16},{12,20},{16,8},{20,12},{24,0},{28,4},{1,25},{... | collective-permute-start | bytes 294920 | tf_op jit(solution)/shard_map/ppermute | solution.py:516
  33.1 10.8 %collective-permute-start.9 = (bf16[32,1536]{1,0:T(8,128)(2,1)S(1)}, bf16[32,1536]{1,0:T(8,128)(2,1)S(1)}, u32[]{:S(2)}, u32[]{:S(2)}) collective-permute-start(bf16[32,1536]{1,0:T(8,128)(2,1)S(1)} %get-tuple-element.28), channel_id=1, source_target_pairs={{0,28},{4,24},{8,20},{12,16},{16,12},{20,8},{24,4},{28,0},{1,29},{... | collective-permute-start | bytes 294920 | tf_op jit(solution)/shard_map/ppermute | solution.py:516
  34.5 6.4 %slice-start = ((s8[9437184]{0:T(1024)(128)(4,1)}), s8[4194304]{0:T(1024)(128)(4,1)S(1)}, s32[]{:S(2)}) async-start(s8[9437184]{0:T(1024)(128)(4,1)} %bitcast.20), calls=%async_computation.2 | async-start | bytes 8388608
  34.5 6.4 %slice-start.1 = ((s8[9437184]{0:T(1024)(128)(4,1)}), s8[4194304]{0:T(1024)(128)(4,1)S(1)}, s32[]{:S(2)}) async-start(s8[9437184]{0:T(1024)(128)(4,1)} %bitcast.20), calls=%async_computation.3 | async-start | bytes 8388608
  40.2 1.2 %slice-start.2 = ((s8[9437184]{0:T(1024)(128)(4,1)}), s8[1048576]{0:T(1024)(128)(4,1)S(1)}, s32[]{:S(2)}) async-start(s8[9437184]{0:T(1024)(128)(4,1)} %bitcast.20), calls=%async_computation.4 | async-start | bytes 2097152
  43.9 31.7 %copy-start.3 = (s32[2,64]{1,0:T(2,128)S(1)}, s32[2,64]{1,0:T(2,128)}, u32[]{:S(2)}) copy-start(s32[2,64]{1,0:T(2,128)} %slots_ref.1) | copy-start | bytes 1540
  43.9 31.7 %copy-start.4 = (s32[2]{0:T(128)S(1)}, s32[2]{0:T(128)}, u32[]{:S(2)}) copy-start(s32[2]{0:T(128)} %order_ref.1) | copy-start | bytes 28
  48.1 27.5 %all-to-all-start = ((bf16[32,32,384]{2,1,0:T(8,128)(2,1)}), bf16[32,32,384]{2,1,0:T(8,128)(2,1)S(1)}, u32[]{:S(2)}, u32[]{:S(2)}) async-start(bf16[32,32,384]{2,1,0:T(8,128)(2,1)} %bitcast.11), calls=%async_computation | async-start | bytes 1572864 | tf_op jit(solution)/shard_map/all_to_all | solution.py:559

commit v4 on v3

--- a/solution.py
+++ b/solution.py
@@ -9,6 +9,8 @@
 
 KEEP = 16
 CAP = 32
+REQ_DEV = 2
+TOPK = 4
 
 
 EPSILON = 1e-06
@@ -351,7 +353,7 @@
     *row_refs, out_ref, rows = rest
     share = row_refs[0].shape[0]
     for step, row_ref in enumerate(row_refs):
-        start = pl.multiple_of((place_ref[3] ^ step) * share, share)
+        start = pl.multiple_of((place_ref[4] ^ step) * share, share)
         rows[pl.ds(start, share)] = row_ref[...]
     taken = rows[...]
     acts = []
@@ -360,11 +362,13 @@
         upper = jnp.dot(taken, wi[half, 1], preferred_element_type=jnp.float32)
         acts.append((jnp.maximum(gate, 0.0) * upper).astype(jnp.bfloat16))
     acts = jnp.concatenate(acts, axis=1)
-    groups, ranks, _, quarter = out_ref.shape
+    groups, ranks, sides, _, quarter = out_ref.shape
     for rank in range(ranks):
         columns = slice(rank * quarter, (rank + 1) * quarter)
         made = jnp.dot(acts, wo[:, columns], preferred_element_type=jnp.float32)
-        out_ref[:, rank] = made.astype(jnp.bfloat16).reshape(groups, share, quarter)
+        made = made.astype(jnp.bfloat16).reshape(sides, groups, share, quarter)
+        for side in range(sides):
+            out_ref[:, rank, side] = made[side]
 
 
 def expert_rows(rows, w_in_own, w_out_own, place, ranks):
@@ -374,7 +378,9 @@
     scalar = pl.BlockSpec(memory_space=pltpu.SMEM)
     return pl.pallas_call(
         expert_kernel,
-        out_shape=jax.ShapeDtypeStruct((groups, ranks, share, width // ranks), jnp.bfloat16),
+        out_shape=jax.ShapeDtypeStruct(
+            (groups // 2, ranks, 2, share, width // ranks), jnp.bfloat16
+        ),
         in_specs=[scalar] + [whole] * (2 + groups),
         out_specs=whole,
         scratch_shapes=[pltpu.VMEM((groups * share, width), jnp.bfloat16)],
@@ -426,6 +432,109 @@
         compiler_params=pltpu.CompilerParams(vmem_limit_bytes=SOME_VMEM),
         name="combine",
     )(order, rows, targets, gates, resid, slots)
+
+
+def mixture(place_ref, rows_ref, pack_ref, side):
+    experts, _, quarter = rows_ref.shape
+    pack = jnp.transpose(pack_ref[...])
+    first = place_ref[5] * (experts * CAP)
+    places = lax.broadcasted_iota(jnp.int32, (pack.shape[0], experts * CAP), 1) + first
+    matrix = jnp.zeros(places.shape, jnp.float32)
+    for pick in range(TOPK):
+        target = pack[:, pick : pick + 1].astype(jnp.int32)
+        gate = pack[:, TOPK + pick : TOPK + pick + 1]
+        matrix = matrix + jnp.where(places == target, gate, 0.0)
+    rows = rows_ref[:, side * CAP : (side + 1) * CAP].reshape(experts * CAP, quarter)
+    return jnp.dot(matrix.astype(jnp.bfloat16), rows, preferred_element_type=jnp.float32)
+
+
+def relay_kernel(place_ref, rows_ref, partner_ref, relay_ref):
+    relay_ref[...] = mixture(place_ref, rows_ref, partner_ref, 1).astype(jnp.bfloat16)
+
+
+def relayed(place, rows, partner):
+    whole = pl.BlockSpec(memory_space=pltpu.VMEM)
+    scalar = pl.BlockSpec(memory_space=pltpu.SMEM)
+    return pl.pallas_call(
+        relay_kernel,
+        out_shape=jax.ShapeDtypeStruct((partner.shape[1], rows.shape[2]), jnp.bfloat16),
+        in_specs=[scalar] + [whole] * 2,
+        out_specs=whole,
+        compiler_params=pltpu.CompilerParams(vmem_limit_bytes=SOME_VMEM),
+        name="relay",
+    )(place, rows, partner)
+
+
+def gather_kernel(
+    place_ref, rows_ref, own_ref, partner_ref, resid_ref, relay_ref, sum_ref, posted_ref
+):
+    requests, keep, quarter = posted_ref.shape
+    tokens = own_ref.shape[1]
+    tree = tokens // REQ_DEV
+    own_sum = resid_ref[...] + mixture(place_ref, rows_ref, own_ref, 0)
+    sum_ref[...] = own_sum
+    posted = [jnp.zeros((keep, quarter), jnp.float32)] * requests
+    for pack_ref, done in (
+        (own_ref, own_sum.astype(jnp.bfloat16)),
+        (partner_ref, relay_ref[...]),
+    ):
+        slots = pack_ref[2 * TOPK : 2 * TOPK + 1, :].astype(jnp.int32)
+        chosen = lax.broadcasted_iota(jnp.int32, (keep, tokens), 0) == slots
+        homes = pack_ref[2 * TOPK + 1 : 2 * TOPK + 2, :].astype(jnp.int32)
+        for request in range(REQ_DEV):
+            start = request * tree
+            rows = jnp.dot(
+                chosen[:, start : start + tree].astype(jnp.bfloat16),
+                done[start : start + tree],
+                preferred_element_type=jnp.float32,
+            )
+            home = homes[:, start : start + 1]
+            posted = [jnp.where(home == place, rows, held) for place, held in enumerate(posted)]
+    for place in range(requests):
+        posted_ref[place] = posted[place].astype(jnp.bfloat16)
+
+
+def gathered(place, rows, own, partner, resid, relay, requests):
+    tokens, quarter = resid.shape
+    whole = pl.BlockSpec(memory_space=pltpu.VMEM)
+    scalar = pl.BlockSpec(memory_space=pltpu.SMEM)
+    return pl.pallas_call(
+        gather_kernel,
+        out_shape=[
+            jax.ShapeDtypeStruct((tokens, quarter), jnp.float32),
+            jax.ShapeDtypeStruct((requests, KEEP, quarter), jnp.bfloat16),
+        ],
+        in_specs=[scalar] + [whole] * 5,
+        out_specs=[whole] * 2,
+        compiler_params=pltpu.CompilerParams(vmem_limit_bytes=SOME_VMEM),
+        name="gather",
+    )(place, rows, own, partner, resid, relay)
+
+
+def finish_kernel(sum_ref, other_ref, received_ref, tree_ref, accepted_ref):
+    done = (sum_ref[...] + other_ref[...].astype(jnp.float32)).astype(jnp.bfloat16)
+    tree_ref[...] = done.reshape(tree_ref.shape)
+    total = received_ref[0].astype(jnp.float32)
+    for source in range(1, received_ref.shape[0]):
+        total = total + received_ref[source].astype(jnp.float32)
+    accepted_ref[...] = total.astype(jnp.bfloat16)
+
+
+def finished(own_sum, other_sum, received):
+    tokens, quarter = own_sum.shape
+    req_dev = received.shape[1]
+    whole = pl.BlockSpec(memory_space=pltpu.VMEM)
+    return pl.pallas_call(
+        finish_kernel,
+        out_shape=[
+            jax.ShapeDtypeStruct((req_dev, tokens // req_dev, quarter), jnp.bfloat16),
+            jax.ShapeDtypeStruct(received.shape[1:], jnp.bfloat16),
+        ],
+        in_specs=[whole] * 3,
+        out_specs=[whole] * 2,
+        compiler_params=pltpu.CompilerParams(vmem_limit_bytes=SOME_VMEM),
+        name="finish",
+    )(own_sum, other_sum, received)
 
 
 def on_device(
@@ -460,7 +569,11 @@
     pieces = w_in.shape[0]
     quarter = width // tp_count
     first = tp_rank % 2
-    place = jnp.stack([kv_head, first, tp_rank, lax.axis_index("req")]).astype(jnp.int32)
+    req_rank = lax.axis_index("req")
+    side = req_count // 2
+    place = jnp.stack(
+        [kv_head, first, tp_rank, req_rank, req_rank % side, req_rank // side]
+    ).astype(jnp.int32)
 
     ids = expert_ids.reshape(tokens, -1)
     picks = ids[:, :, None] == jnp.arange(experts)[None, None, :]
@@ -468,7 +581,7 @@
     slot_expert = jnp.cumsum(counts, axis=0) - counts
     slot_pick = jnp.sum(jnp.where(picks, slot_expert[:, None, :], 0), axis=-1)
     held = jnp.where(counts == 1, slot_expert, -1).T
-    by_expert = pieces == 2 * tp_count
+    by_expert = pieces == 2 * tp_count and req_count == 8 and req_dev == REQ_DEV
     if by_expert:
         share = CAP
         held = lax.dynamic_index_in_dim(
@@ -556,22 +669,52 @@
         ).astype(jnp.bfloat16)
         produced = produced.reshape(pieces, req_count, share, tp_count, quarter)
         produced = produced.transpose(1, 3, 0, 2, 4)
-    returned = lax.all_to_all(
-        produced.reshape(req_count * tp_count, -1, quarter),
-        ("req", "tp"),
-        split_axis=0,
-        concat_axis=0,
-        tiled=True,
-    )
-    tree_out, posted = combine_rows(
-        returned.reshape(-1, quarter),
-        targets,
-        gates,
-        own_resid,
-        slots,
-        order,
-        req_count * req_dev,
-    )
+    if by_expert:
+        across = [(i, i ^ side) for i in range(req_count)]
+        halves = [
+            list(range(i * side * tp_count, (i + 1) * side * tp_count)) for i in range(2)
+        ]
+        own = jnp.concatenate(
+            [
+                targets.astype(jnp.float32).T,
+                gates.T,
+                slots.reshape(1, tokens).astype(jnp.float32),
+                jnp.repeat(order, draft_tree).reshape(1, tokens).astype(jnp.float32),
+                jnp.zeros((6, tokens), jnp.float32),
+            ],
+            axis=0,
+        )
+        partner = lax.ppermute(own, "req", across)
+        returned = lax.all_to_all(
+            produced.reshape(side * tp_count, -1, quarter),
+            ("req", "tp"),
+            split_axis=0,
+            concat_axis=0,
+            axis_index_groups=halves,
+            tiled=True,
+        )
+        relay = relayed(place, returned, partner)
+        other_sum = lax.ppermute(relay, "req", across)
+        own_sum, posted = gathered(
+            place, returned, own, partner, own_resid, relay, req_count * req_dev
+        )
+    else:
+        returned = lax.all_to_all(
+            produced.reshape(req_count * tp_count, -1, quarter),
+            ("req", "tp"),
+            split_axis=0,
+            concat_axis=0,
+            tiled=True,
+        )
+        tree_out, posted = combine_rows(
+            returned.reshape(-1, quarter),
+            targets,
+            gates,
+            own_resid,
+            slots,
+            order,
+            req_count * req_dev,
+        )
     received = lax.all_to_all(
         posted.reshape(req_count, req_dev, KEEP, quarter),
         "req",
@@ -579,7 +722,10 @@
         concat_axis=0,
         tiled=True,
     )
-    accepted = jnp.sum(received.astype(jnp.float32), axis=0).astype(jnp.bfloat16)
+    if by_expert:
+        tree_out, accepted = finished(own_sum, other_sum, received)
+    else:
+        accepted = jnp.sum(received.astype(jnp.float32), axis=0).astype(jnp.bfloat16)
     return (tree_out, accepted)
 
 

time: 90 us -> 87.6 us (0.973)
  blocking collectives: 11.6 us -> 0 us
  starting transfers between devices: 22.4 us -> 30.3 us
  Pallas kernels: 16.3 us -> 17.5 us
  other arithmetic: 2.32 us -> 1.38 us
    all_to_all x1 -> x2, waiting for transfers between devices: 19.9 us -> 3.91 us  [the longest x1 3.91 us: on_device(): lax.all_to_all(produced.reshape(side * tp_count, -1, quarter), ('req', 't...]
    ppermute x0 -> x2, waiting for transfers between devices: none -> 16 us  [the longest x1 8.88 us: on_device(): other_sum = lax.ppermute(relay, 'req', across)]
    all_to_all x1 -> x0, blocking collectives: 11.6 us -> none  [on_device(): lax.all_to_all(posted.reshape(req_count, req_dev, KEEP, quarter), 'req',...]
    ppermute x0 -> x2, starting transfers between devices: none -> 4.78 us  [the longest x1 2.84 us: on_device(): other_sum = lax.ppermute(relay, 'req', across)]
    all_to_all x1 -> x2, starting transfers between devices: 6.92 us -> 10.1 us  [the longest x1 6.72 us: on_device(): lax.all_to_all(produced.reshape(side * tp_count, -1, quarter), ('req', 't...]
    pallas_call x2 -> x4, Pallas kernels: 5.86 us -> 7.81 us  [the longest x1 4.09 us: expert_rows(): pl.pallas_call(expert_kernel, out_shape=jax.ShapeDtypeStruct((groups // 2...]
  transfers between devices with their start and end apart: 11 -> 14, of which waited for: 5 -> 7; matrix products, arithmetic and copies ran while one was open for 9% -> 9% of each run, Pallas kernels for 1% -> 1%
where the time goes in v4:
time: 87.6 us; the launch traced here: 87.2 us
  starting transfers between devices  30.3 us (35%)
  waiting for transfers between devices  29.4 us (34%)
  Pallas kernels  17.5 us (20%)
  local copies, waits for them, and re-layouts  7.72 us (9%)
  other arithmetic  1.38 us (2%)
  between operations  0.92 us (1%)
    ppermute x7, starting transfers between devices, on_device(): lax.ppermute(sent[step], 'req', [(i, i ^ step) for i in range(req_count)])  11.9 us
    ppermute x1, waiting for transfers between devices, on_device(): other_sum = lax.ppermute(relay, 'req', across)  8.88 us
    pallas_call x1, Pallas kernels, attention_part(): pl.pallas_call(functools.partial(attention_kernel, tp_count), out_shape=[...  7.25 us
    ppermute x1, waiting for transfers between devices, on_device(): partner = lax.ppermute(own, 'req', across)  7.09 us
    all_to_all x1, starting transfers between devices, on_device(): lax.all_to_all(produced.reshape(side * tp_count, -1, quarter), ('req', 't...  6.72 us
    dynamic_slice x1, local copies, waits for them, and re-layouts, on_device(): lax.dynamic_slice_in_dim(w_in, tp_rank * 2, 2, 0).transpose(0, 2, 1, 3)  5.75 us
    ppermute x1, waiting for transfers between devices, on_device(): half = added(chip, lax.ppermute(chip, 'tp', far))  4.83 us
    pallas_call x1, Pallas kernels, expert_rows(): pl.pallas_call(expert_kernel, out_shape=jax.ShapeDtypeStruct((groups // 2...  4.09 us
  transfers between devices with their start and end apart: 14, of which 7 were waited for; matrix products, arithmetic and copies ran while one was open for 9% of the time, Pallas kernels for 1%

profile of v4, /device:TPU:0, one launch (start us, length us, event | category | flops | bytes accessed | tf_op | source)
XLA Modules:
  0.0 87.2 jit_solution(14617800474109785427)
XLA Ops:
  0.7 7.3 %attention.1 = (bf16[64,1536]{1,0:T(8,128)(2,1)}, bf16[64,1536]{1,0:T(8,128)(2,1)}) custom-call(s32[2]{0:T(128)} %lengths_ref.1, f32[1536]{0:T(1024)} %gain_hbm.1, s32[2,64]{1,0:T(2,128)} %depths_hbm.1, s32[2,64,64]{2,1,0:T(8,128)} %mask_hbm.1, bf16[2,64,1536]{2,1,0:T(8,128)(2,1)} %drafts_ref.1, bf16[1536,384]{1,0:T(8,128)(2,1)} %wq_hbm.1, ...), custom_call_target="tpu_custom_call" | custom-call | tf_op jit(solution)/shard_map/attention/pallas_call | solution.py:236
  8.5 1.3 %collective-permute-done = bf16[64,1536]{1,0:T(8,128)(2,1)S(1)} collective-permute-done((bf16[64,1536]{1,0:T(8,128)(2,1)}, bf16[64,1536]{1,0:T(8,128)(2,1)S(1)}, u32[]{:S(2)}, u32[]{:S(2)}) %collective-permute-start) | collective-permute-done | bytes 196640 | tf_op jit(solution)/shard_map/ppermute | solution.py:620
  9.7 1.0 %add_convert_fusion.1 = bf16[64,1536]{1,0:T(8,128)(2,1)S(1)} fusion(bf16[64,1536]{1,0:T(8,128)(2,1)S(1)} %collective-permute-done, bf16[64,1536]{1,0:T(8,128)(2,1)} %get-tuple-element.19), kind=kLoop, calls=%fused_computation.6 | loop fusion | flops 393216 | bytes 589824 | tf_op jit(solution)/shard_map/convert_element_type | solution.py:618
  10.7 2.9 %collective-permute-start.1 = (bf16[64,1536]{1,0:T(8,128)(2,1)S(1)}, bf16[64,1536]{1,0:T(8,128)(2,1)S(1)}, u32[]{:S(2)}, u32[]{:S(2)}) collective-permute-start(bf16[64,1536]{1,0:T(8,128)(2,1)S(1)} %add_convert_fusion.1), channel_id=1, source_target_pairs={{0,2},{1,3},{2,0},{3,1},{4,6},{5,7},{6,4},{7,5},{8,10},{9,11},{10,... | collective-permute-start | bytes 589832 | tf_op jit(solution)/shard_map/ppermute | solution.py:621
  14.0 4.8 %collective-permute-done.1 = bf16[64,1536]{1,0:T(8,128)(2,1)S(1)} collective-permute-done((bf16[64,1536]{1,0:T(8,128)(2,1)S(1)}, bf16[64,1536]{1,0:T(8,128)(2,1)S(1)}, u32[]{:S(2)}, u32[]{:S(2)}) %collective-permute-start.1) | collective-permute-done | bytes 196640 | tf_op jit(solution)/shard_map/ppermute | solution.py:621
  19.2 1.2 %collective-permute-done.2.other_ref = bf16[64,1536]{1,0:T(8,128)(2,1)S(1)} collective-permute-done((bf16[64,1536]{1,0:T(8,128)(2,1)S(1)}, bf16[64,1536]{1,0:T(8,128)(2,1)S(1)}, u32[]{:S(2)}, u32[]{:S(2)}) %collective-permute-start.2) | collective-permute-done | bytes 196640 | tf_op jit(solution)/shard_map/ppermute | solution.py:622
  20.4 1.4 %dispatch.1 = (f32[128,32]{1,0:T(8,128)S(1)}, bf16[32,1536]{1,0:T(8,128)(2,1)S(1)}, bf16[32,1536]{1,0:T(8,128)(2,1)S(1)}, bf16[32,1536]{1,0:T(8,128)(2,1)S(1)}, ...) custom-call(s32[6]{0:T(128)S(1)} %stack.27.place_ref, ...), custom_call_target="tpu_custom_call" | custom-call | tf_op jit(solution)/shard_map/dispatch/pallas_call | solution.py:308
  21.9 2.5 %collective-permute-start.3 = (bf16[32,1536]{1,0:T(8,128)(2,1)S(1)}, bf16[32,1536]{1,0:T(8,128)(2,1)S(1)}, u32[]{:S(2)}, u32[]{:S(2)}) collective-permute-start(bf16[32,1536]{1,0:T(8,128)(2,1)S(1)} %get-tuple-element.22), channel_id=1, source_target_pairs={{0,4},{4,0},{8,12},{12,8},{16,20},{20,16},{24,28},{28,24},{1,5},{5... | collective-permute-start | bytes 294920 | tf_op jit(solution)/shard_map/ppermute | solution.py:629
  25.9 3.0 %collective-permute-start.6 = (bf16[32,1536]{1,0:T(8,128)(2,1)S(1)}, bf16[32,1536]{1,0:T(8,128)(2,1)S(1)}, u32[]{:S(2)}, u32[]{:S(2)}) collective-permute-start(bf16[32,1536]{1,0:T(8,128)(2,1)S(1)} %get-tuple-element.25), channel_id=1, source_target_pairs={{0,16},{4,20},{8,24},{12,28},{16,0},{20,4},{24,8},{28,12},{1,17},{... | collective-permute-start | bytes 294920 | tf_op jit(solution)/shard_map/ppermute | solution.py:629
  28.9 1.3 %collective-permute-start.7 = (bf16[32,1536]{1,0:T(8,128)(2,1)S(1)}, bf16[32,1536]{1,0:T(8,128)(2,1)S(1)}, u32[]{:S(2)}, u32[]{:S(2)}) collective-permute-start(bf16[32,1536]{1,0:T(8,128)(2,1)S(1)} %get-tuple-element.26), channel_id=1, source_target_pairs={{0,20},{4,16},{8,28},{12,24},{16,4},{20,0},{24,12},{28,8},{1,21},{... | collective-permute-start | bytes 294920 | tf_op jit(solution)/shard_map/ppermute | solution.py:629
  30.2 2.9 %collective-permute-start.8 = (bf16[32,1536]{1,0:T(8,128)(2,1)S(1)}, bf16[32,1536]{1,0:T(8,128)(2,1)S(1)}, u32[]{:S(2)}, u32[]{:S(2)}) collective-permute-start(bf16[32,1536]{1,0:T(8,128)(2,1)S(1)} %get-tuple-element.27), channel_id=1, source_target_pairs={{0,24},{4,28},{8,16},{12,20},{16,8},{20,12},{24,0},{28,4},{1,25},{... | collective-permute-start | bytes 294920 | tf_op jit(solution)/shard_map/ppermute | solution.py:629
  33.7 5.7 %constant_dynamic-slice_fusion.1 = bf16[2,1536,2,384]{3,2,1,0:T(2,128)(2,1)S(1)} fusion(bf16[8,1536,2,384]{3,2,1,0:T(2,128)(2,1)} %param.28, s32[]{:T(128)S(6)} %select_n.57), kind=kLoop, calls=%fused_computation.23 | loop fusion | bytes 9437188 | tf_op jit(solution)/shard_map/dynamic_slice | solution.py:658
  40.7 1.0 %fetch.1 = (bf16[2,2,1536,384]{3,2,1,0:T(8,128)(2,1)S(1)}, bf16[2,384,1536]{2,1,0:T(8,128)(2,1)S(1)}) custom-call(s32[6]{0:T(128)S(1)} %stack.27.place_ref, bf16[2,2,1536,384]{3,2,1,0:T(8,128)(2,1)S(1)} %bitcast.24, bf16[8,384,1536]{2,1,0:T(8,128)(2,1)S(1)} %bitcast.26), custom_call_target="tpu_custom_call" | custom-call | tf_op jit(solution)/shard_map/fetch/pallas_call | solution.py:338
  41.8 2.2 %collective-permute-done.7.rest_5_ = bf16[32,1536]{1,0:T(8,128)(2,1)S(1)} collective-permute-done((bf16[32,1536]{1,0:T(8,128)(2,1)S(1)}, bf16[32,1536]{1,0:T(8,128)(2,1)S(1)}, u32[]{:S(2)}, u32[]{:S(2)}) %collective-permute-start.7) | collective-permute-done | bytes 98336 | tf_op jit(solution)/shard_map/ppermute | solution.py:629
  44.0 4.1 %experts.1 = bf16[4,4,2,32,384]{4,3,2,1,0:T(8,128)(2,1)} custom-call(s32[6]{0:T(128)S(1)} %stack.27.place_ref, bf16[2,2,1536,384]{3,2,1,0:T(8,128)(2,1)S(1)} %get-tuple-element.17.wi, bf16[768,1536]{1,0:T(8,128)(2,1)S(1)} %bitcast.27, bf16[32,1536]{1,0:T(8,128)(2,1)S(1)} %get-tuple-element.21.rest_0_, bf16[32,1536]{1,0:T(8,128)(2,1)S(1)} %collective-permute-done.3.rest_1_, ...), custom_call_target="tpu_custom_call" | custom-call | tf_op jit(solution)/shard_map/experts/pallas_call | solution.py:379
  48.1 6.7 %all-to-all-start = ((bf16[16,64,384]{2,1,0:T(8,128)(2,1)}), bf16[16,64,384]{2,1,0:T(8,128)(2,1)S(1)}, u32[]{:S(2)}, u32[]{:S(2)}) async-start(bf16[16,64,384]{2,1,0:T(8,128)(2,1)} %bitcast.12), calls=%async_computation | async-start | bytes 1572864 | tf_op jit(solution)/shard_map/all_to_all | solution.py:688
  55.4 1.9 %collective-permute-start.10 = (f32[16,128]{1,0:T(8,128)S(1)}, f32[16,128]{1,0:T(8,128)S(1)}, u32[]{:S(2)}, u32[]{:S(2)}) collective-permute-start(f32[16,128]{1,0:T(8,128)S(1)} %concatenate.9.own_ref), channel_id=1, source_target_pairs={{0,16},{4,20},{8,24},{12,28},{16,0},{20,4},{24,8},{28,12},{1,17},{... | collective-permute-start | bytes 24584 | tf_op jit(solution)/shard_map/ppermute | solution.py:687
  57.3 7.1 %collective-permute-done.10.partner_ref = f32[16,128]{1,0:T(8,128)S(1)} collective-permute-done((f32[16,128]{1,0:T(8,128)S(1)}, f32[16,128]{1,0:T(8,128)S(1)}, u32[]{:S(2)}, u32[]{:S(2)}) %collective-permute-start.10) | collective-permute-done | bytes 8224 | tf_op jit(solution)/shard_map/ppermute | solution.py:687
  64.4 3.9 %all-to-all-done.rows_ref = bf16[16,64,384]{2,1,0:T(8,128)(2,1)S(1)} async-done(((bf16[16,64,384]{2,1,0:T(8,128)(2,1)}), bf16[16,64,384]{2,1,0:T(8,128)(2,1)S(1)}, u32[]{:S(2)}, u32[]{:S(2)}) %all-to-all-start) | async-done | bytes 786464 | tf_op jit(solution)/shard_map/all_to_all | solution.py:688
  68.3 1.1 %relay.1.relay_ref = bf16[128,384]{1,0:T(8,128)(2,1)S(1)} custom-call(s32[6]{0:T(128)S(1)} %stack.27.place_ref, bf16[16,64,384]{2,1,0:T(8,128)(2,1)S(1)} %all-to-all-done.rows_ref, f32[16,128]{1,0:T(8,128)S(1)} %collective-permute-done.10.partner_ref), custom_call_target="tpu_custom_call" | custom-call | tf_op jit(solution)/shard_map/relay/pallas_call | solution.py:458
  69.4 2.0 %gather.1 = (f32[128,384]{1,0:T(8,128)S(1)}, bf16[16,16,384]{2,1,0:T(8,128)(2,1)}) custom-call(s32[6]{0:T(128)S(1)} %stack.27.place_ref, bf16[16,64,384]{2,1,0:T(8,128)(2,1)S(1)} %all-to-all-done.rows_ref, f32[16,128]{1,0:T(8,128)S(1)} %concatenate.9.own_ref, f32[16,128]{1,0:T(8,128)S(1)} %collective-permute-done.10.partner_ref, ...), custom_call_target="tpu_custom_call" | custom-call | tf_op jit(solution)/shard_map/gather/pallas_call | solution.py:501
  71.4 3.4 %all-to-all-start.1 = ((bf16[8,2,16,384]{3,2,1,0:T(8,128)(2,1)}), bf16[8,2,16,384]{3,2,1,0:T(8,128)(2,1)S(1)}, u32[]{:S(2)}, u32[]{:S(2)}) async-start(bf16[8,2,16,384]{3,2,1,0:T(8,128)(2,1)} %bitcast.16), calls=%async_computation.1 | async-start | bytes 393216 | tf_op jit(solution)/shard_map/all_to_all | solution.py:718
  74.8 2.8 %collective-permute-start.11 = (bf16[128,384]{1,0:T(8,128)(2,1)S(1)}, bf16[128,384]{1,0:T(8,128)(2,1)S(1)}, u32[]{:S(2)}, u32[]{:S(2)}) collective-permute-start(bf16[128,384]{1,0:T(8,128)(2,1)S(1)} %relay.1.relay_ref), channel_id=1, source_target_pairs={{0,16},{4,20},{8,24},{12,28},{16,0},{20,4},{24,8},{28,12},{1,17},{... | collective-permute-start | bytes 294920 | tf_op jit(solution)/shard_map/ppermute | solution.py:697
  77.6 8.9 %collective-permute-done.11.other_ref = bf16[128,384]{1,0:T(8,128)(2,1)S(1)} collective-permute-done((bf16[128,384]{1,0:T(8,128)(2,1)S(1)}, bf16[128,384]{1,0:T(8,128)(2,1)S(1)}, u32[]{:S(2)}, u32[]{:S(2)}) %collective-permute-start.11) | collective-permute-done | bytes 98336 | tf_op jit(solution)/shard_map/ppermute | solution.py:697
  (58 shorter events, 5.8 us)
Async XLA Ops:
  0.6 19.8 %copy-start = (bf16[2,64,1536]{2,1,0:T(8,128)(2,1)S(1)}, bf16[2,64,1536]{2,1,0:T(8,128)(2,1)}, u32[]{:S(2)}) copy-start(bf16[2,64,1536]{2,1,0:T(8,128)(2,1)} %drafts_ref.1) | copy-start | bytes 1179652
  0.6 13.0 %copy-start.3 = (s32[2,64,4]{1,2,0:T(4,128)S(1)}, s32[2,64,4]{1,2,0:T(4,128)}, u32[]{:S(2)}) copy-start(s32[2,64,4]{1,2,0:T(4,128)} %param.27) | copy-start | bytes 6148
  0.7 19.8 %copy-start.1 = (bf16[1536,32]{0,1:T(8,128)(2,1)S(1)}, bf16[1536,32]{0,1:T(8,128)(2,1)}, u32[]{:S(2)}) copy-start(bf16[1536,32]{0,1:T(8,128)(2,1)} %param.26) | copy-start | bytes 294916
  0.7 19.8 %copy-start.2 = (f32[1536]{0:T(1024)S(1)}, f32[1536]{0:T(1024)}, u32[]{:S(2)}) copy-start(f32[1536]{0:T(1024)} %gain_ref.1) | copy-start | bytes 18436
  7.9 1.8 %collective-permute-start = (bf16[64,1536]{1,0:T(8,128)(2,1)}, bf16[64,1536]{1,0:T(8,128)(2,1)S(1)}, u32[]{:S(2)}, u32[]{:S(2)}) collective-permute-start(bf16[64,1536]{1,0:T(8,128)(2,1)} %get-tuple-element.20), channel_id=1, source_target_pairs={{0,1},{1,0},{2,3},{3,2},{4,5},{5,4},{6,7},{7,6},{8,9},{9,8},{10,11... | collective-permute-start | bytes 589832 | tf_op jit(solution)/shard_map/ppermute | solution.py:620
  10.7 8.1 %collective-permute-start.1 = (bf16[64,1536]{1,0:T(8,128)(2,1)S(1)}, bf16[64,1536]{1,0:T(8,128)(2,1)S(1)}, u32[]{:S(2)}, u32[]{:S(2)}) collective-permute-start(bf16[64,1536]{1,0:T(8,128)(2,1)S(1)} %add_convert_fusion.1), channel_id=1, source_target_pairs={{0,2},{1,3},{2,0},{3,1},{4,6},{5,7},{6,4},{7,5},{8,10},{9,11},{10,... | collective-permute-start | bytes 589832 | tf_op jit(solution)/shard_map/ppermute | solution.py:621
  18.9 1.5 %collective-permute-start.2 = (bf16[64,1536]{1,0:T(8,128)(2,1)S(1)}, bf16[64,1536]{1,0:T(8,128)(2,1)S(1)}, u32[]{:S(2)}, u32[]{:S(2)}) collective-permute-start(bf16[64,1536]{1,0:T(8,128)(2,1)S(1)} %add_convert_fusion.half_ref), channel_id=1, source_target_pairs={{0,1},{1,0},{2,3},{3,2},{4,5},{5,4},{6,7},{7,6},{8,9},{9,8},{10,11... | collective-permute-start | bytes 589832 | tf_op jit(solution)/shard_map/ppermute | solution.py:622
  21.9 8.4 %collective-permute-start.3 = (bf16[32,1536]{1,0:T(8,128)(2,1)S(1)}, bf16[32,1536]{1,0:T(8,128)(2,1)S(1)}, u32[]{:S(2)}, u32[]{:S(2)}) collective-permute-start(bf16[32,1536]{1,0:T(8,128)(2,1)S(1)} %get-tuple-element.22), channel_id=1, source_target_pairs={{0,4},{4,0},{8,12},{12,8},{16,20},{20,16},{24,28},{28,24},{1,5},{5... | collective-permute-start | bytes 294920 | tf_op jit(solution)/shard_map/ppermute | solution.py:629
  24.4 8.8 %collective-permute-start.4 = (bf16[32,1536]{1,0:T(8,128)(2,1)S(1)}, bf16[32,1536]{1,0:T(8,128)(2,1)S(1)}, u32[]{:S(2)}, u32[]{:S(2)}) collective-permute-start(bf16[32,1536]{1,0:T(8,128)(2,1)S(1)} %get-tuple-element.23), channel_id=1, source_target_pairs={{0,8},{4,12},{8,0},{12,4},{16,24},{20,28},{24,16},{28,20},{1,9},{5... | collective-permute-start | bytes 294920 | tf_op jit(solution)/shard_map/ppermute | solution.py:629
  25.3 16.5 %collective-permute-start.5 = (bf16[32,1536]{1,0:T(8,128)(2,1)S(1)}, bf16[32,1536]{1,0:T(8,128)(2,1)S(1)}, u32[]{:S(2)}, u32[]{:S(2)}) collective-permute-start(bf16[32,1536]{1,0:T(8,128)(2,1)S(1)} %get-tuple-element.24), channel_id=1, source_target_pairs={{0,12},{4,8},{8,4},{12,0},{16,28},{20,24},{24,20},{28,16},{1,13},{... | collective-permute-start | bytes 294920 | tf_op jit(solution)/shard_map/ppermute | solution.py:629
  25.9 15.9 %collective-permute-start.6 = (bf16[32,1536]{1,0:T(8,128)(2,1)S(1)}, bf16[32,1536]{1,0:T(8,128)(2,1)S(1)}, u32[]{:S(2)}, u32[]{:S(2)}) collective-permute-start(bf16[32,1536]{1,0:T(8,128)(2,1)S(1)} %get-tuple-element.25), channel_id=1, source_target_pairs={{0,16},{4,20},{8,24},{12,28},{16,0},{20,4},{24,8},{28,12},{1,17},{... | collective-permute-start | bytes 294920 | tf_op jit(solution)/shard_map/ppermute | solution.py:629
  28.9 15.0 %collective-permute-start.7 = (bf16[32,1536]{1,0:T(8,128)(2,1)S(1)}, bf16[32,1536]{1,0:T(8,128)(2,1)S(1)}, u32[]{:S(2)}, u32[]{:S(2)}) collective-permute-start(bf16[32,1536]{1,0:T(8,128)(2,1)S(1)} %get-tuple-element.26), channel_id=1, source_target_pairs={{0,20},{4,16},{8,28},{12,24},{16,4},{20,0},{24,12},{28,8},{1,21},{... | collective-permute-start | bytes 294920 | tf_op jit(solution)/shard_map/ppermute | solution.py:629
  30.2 13.7 %collective-permute-start.8 = (bf16[32,1536]{1,0:T(8,128)(2,1)S(1)}, bf16[32,1536]{1,0:T(8,128)(2,1)S(1)}, u32[]{:S(2)}, u32[]{:S(2)}) collective-permute-start(bf16[32,1536]{1,0:T(8,128)(2,1)S(1)} %get-tuple-element.27), channel_id=1, source_target_pairs={{0,24},{4,28},{8,16},{12,20},{16,8},{20,12},{24,0},{28,4},{1,25},{... | collective-permute-start | bytes 294920 | tf_op jit(solution)/shard_map/ppermute | solution.py:629
  33.1 10.8 %collective-permute-start.9 = (bf16[32,1536]{1,0:T(8,128)(2,1)S(1)}, bf16[32,1536]{1,0:T(8,128)(2,1)S(1)}, u32[]{:S(2)}, u32[]{:S(2)}) collective-permute-start(bf16[32,1536]{1,0:T(8,128)(2,1)S(1)} %get-tuple-element.28), channel_id=1, source_target_pairs={{0,28},{4,24},{8,20},{12,16},{16,12},{20,8},{24,4},{28,0},{1,29},{... | collective-permute-start | bytes 294920 | tf_op jit(solution)/shard_map/ppermute | solution.py:629
  33.7 6.4 %slice-start = ((s8[9437184]{0:T(1024)(128)(4,1)}), s8[4194304]{0:T(1024)(128)(4,1)S(1)}, s32[]{:S(2)}) async-start(s8[9437184]{0:T(1024)(128)(4,1)} %bitcast.25), calls=%async_computation.2 | async-start | bytes 8388608
  33.7 6.4 %slice-start.1 = ((s8[9437184]{0:T(1024)(128)(4,1)}), s8[4194304]{0:T(1024)(128)(4,1)S(1)}, s32[]{:S(2)}) async-start(s8[9437184]{0:T(1024)(128)(4,1)} %bitcast.25), calls=%async_computation.3 | async-start | bytes 8388608
  39.5 1.2 %slice-start.2 = ((s8[9437184]{0:T(1024)(128)(4,1)}), s8[1048576]{0:T(1024)(128)(4,1)S(1)}, s32[]{:S(2)}) async-start(s8[9437184]{0:T(1024)(128)(4,1)} %bitcast.25), calls=%async_computation.4 | async-start | bytes 2097152
  43.9 10.9 %copy-start.5 = (s32[2]{0:T(128)S(1)}, s32[2]{0:T(128)}, u32[]{:S(2)}) copy-start(s32[2]{0:T(128)} %param.31) | copy-start | bytes 28
  44.0 11.1 %copy-start.4 = (s32[2,64]{1,0:T(2,128)S(1)}, s32[2,64]{1,0:T(2,128)}, u32[]{:S(2)}) copy-start(s32[2,64]{1,0:T(2,128)} %param.30) | copy-start | bytes 1540
  48.1 20.3 %all-to-all-start = ((bf16[16,64,384]{2,1,0:T(8,128)(2,1)}), bf16[16,64,384]{2,1,0:T(8,128)(2,1)S(1)}, u32[]{:S(2)}, u32[]{:S(2)}) async-start(bf16[16,64,384]{2,1,0:T(8,128)(2,1)} %bitcast.12), calls=%async_computation | async-start | bytes 1572864 | tf_op jit(solution)/shard_map/all_to_all | solution.py:688
  55.4 9.1 %collective-permute-start.10 = (f32[16,128]{1,0:T(8,128)S(1)}, f32[16,128]{1,0:T(8,128)S(1)}, u32[]{:S(2)}, u32[]{:S(2)}) collective-permute-start(f32[16,128]{1,0:T(8,128)S(1)} %concatenate.9.own_ref), channel_id=1, source_target_pairs={{0,16},{4,20},{8,24},{12,28},{16,0},{20,4},{24,8},{28,12},{1,17},{... | collective-permute-start | bytes 24584 | tf_op jit(solution)/shard_map/ppermute | solution.py:687
  71.4 15.1 %all-to-all-start.1 = ((bf16[8,2,16,384]{3,2,1,0:T(8,128)(2,1)}), bf16[8,2,16,384]{3,2,1,0:T(8,128)(2,1)S(1)}, u32[]{:S(2)}, u32[]{:S(2)}) async-start(bf16[8,2,16,384]{3,2,1,0:T(8,128)(2,1)} %bitcast.16), calls=%async_computation.1 | async-start | bytes 393216 | tf_op jit(solution)/shard_map/all_to_all | solution.py:718
  74.8 11.7 %collective-permute-start.11 = (bf16[128,384]{1,0:T(8,128)(2,1)S(1)}, bf16[128,384]{1,0:T(8,128)(2,1)S(1)}, u32[]{:S(2)}, u32[]{:S(2)}) collective-permute-start(bf16[128,384]{1,0:T(8,128)(2,1)S(1)} %relay.1.relay_ref), channel_id=1, source_target_pairs={{0,16},{4,20},{8,24},{12,28},{16,0},{20,4},{24,8},{28,12},{1,17},{... | collective-permute-start | bytes 294920 | tf_op jit(solution)/shard_map/ppermute | solution.py:697

commit v5 on v4

--- a/solution.py
+++ b/solution.py
@@ -11,6 +11,7 @@
 CAP = 32
 REQ_DEV = 2
 TOPK = 4
+TURNS = (1, 2, 4, 5, 6, 7, 3, 0)
 
 
 EPSILON = 1e-06
@@ -206,19 +207,26 @@
         mixed.append((accum / total).astype(jnp.bfloat16))
 
     copy_o.wait()
+    heads = jnp.concatenate(
+        [
+            jnp.concatenate(
+                [found[head * tree : (head + 1) * tree] for head in range(local_heads)], axis=1
+            )
+            for found in mixed
+        ],
+        axis=0,
+    )
+    part = jnp.dot(heads, wo[...], preferred_element_type=jnp.float32).astype(jnp.bfloat16)
+    part = part.reshape(req_dev, tree, width)
     for request in range(req_dev):
-        heads = jnp.concatenate(
-            [mixed[request][head * tree : (head + 1) * tree] for head in range(local_heads)], axis=1
-        )
-        part = jnp.dot(heads, wo[...], preferred_element_type=jnp.float32).astype(jnp.bfloat16)
 
         @pl.when(first == request)
-        def _(part=part):
-            mine_ref[...] = part
+        def _(request=request):
+            mine_ref[...] = part[request]
 
         @pl.when(first != request)
-        def _(part=part):
-            theirs_ref[...] = part
+        def _(request=request):
+            theirs_ref[...] = part[request]
 
 
 def attention_part(
@@ -352,7 +360,7 @@
 def expert_kernel(place_ref, wi, wo, *rest):
     *row_refs, out_ref, rows = rest
     share = row_refs[0].shape[0]
-    for step, row_ref in enumerate(row_refs):
+    for step, row_ref in zip(TURNS, row_refs):
         start = pl.multiple_of((place_ref[4] ^ step) * share, share)
         rows[pl.ds(start, share)] = row_ref[...]
     taken = rows[...]
@@ -386,7 +394,7 @@
         scratch_shapes=[pltpu.VMEM((groups * share, width), jnp.bfloat16)],
         compiler_params=pltpu.CompilerParams(vmem_limit_bytes=SOME_VMEM),
         name="experts",
-    )(place, w_in_own, w_out_own, *rows)
+    )(place, w_in_own, w_out_own, *[rows[step] for step in TURNS])
 
 
 def combine_kernel(
@@ -448,35 +456,20 @@
     return jnp.dot(matrix.astype(jnp.bfloat16), rows, preferred_element_type=jnp.float32)
 
 
-def relay_kernel(place_ref, rows_ref, partner_ref, relay_ref):
-    relay_ref[...] = mixture(place_ref, rows_ref, partner_ref, 1).astype(jnp.bfloat16)
-
-
-def relayed(place, rows, partner):
-    whole = pl.BlockSpec(memory_space=pltpu.VMEM)
-    scalar = pl.BlockSpec(memory_space=pltpu.SMEM)
-    return pl.pallas_call(
-        relay_kernel,
-        out_shape=jax.ShapeDtypeStruct((partner.shape[1], rows.shape[2]), jnp.bfloat16),
-        in_specs=[scalar] + [whole] * 2,
-        out_specs=whole,
-        compiler_params=pltpu.CompilerParams(vmem_limit_bytes=SOME_VMEM),
-        name="relay",
-    )(place, rows, partner)
-
-
 def gather_kernel(
     place_ref, rows_ref, own_ref, partner_ref, resid_ref, relay_ref, sum_ref, posted_ref
 ):
     requests, keep, quarter = posted_ref.shape
     tokens = own_ref.shape[1]
     tree = tokens // REQ_DEV
+    relay = mixture(place_ref, rows_ref, partner_ref, 1).astype(jnp.bfloat16)
+    relay_ref[...] = relay
     own_sum = resid_ref[...] + mixture(place_ref, rows_ref, own_ref, 0)
     sum_ref[...] = own_sum
     posted = [jnp.zeros((keep, quarter), jnp.float32)] * requests
     for pack_ref, done in (
         (own_ref, own_sum.astype(jnp.bfloat16)),
-        (partner_ref, relay_ref[...]),
+        (partner_ref, relay),
     ):
         slots = pack_ref[2 * TOPK : 2 * TOPK + 1, :].astype(jnp.int32)
         chosen = lax.broadcasted_iota(jnp.int32, (keep, tokens), 0) == slots
@@ -494,21 +487,22 @@
         posted_ref[place] = posted[place].astype(jnp.bfloat16)
 
 
-def gathered(place, rows, own, partner, resid, relay, requests):
+def gathered(place, rows, own, partner, resid, requests):
     tokens, quarter = resid.shape
     whole = pl.BlockSpec(memory_space=pltpu.VMEM)
     scalar = pl.BlockSpec(memory_space=pltpu.SMEM)
     return pl.pallas_call(
         gather_kernel,
         out_shape=[
+            jax.ShapeDtypeStruct((tokens, quarter), jnp.bfloat16),
             jax.ShapeDtypeStruct((tokens, quarter), jnp.float32),
             jax.ShapeDtypeStruct((requests, KEEP, quarter), jnp.bfloat16),
         ],
-        in_specs=[scalar] + [whole] * 5,
-        out_specs=[whole] * 2,
+        in_specs=[scalar] + [whole] * 4,
+        out_specs=[whole] * 3,
         compiler_params=pltpu.CompilerParams(vmem_limit_bytes=SOME_VMEM),
         name="gather",
-    )(place, rows, own, partner, resid, relay)
+    )(place, rows, own, partner, resid)
 
 
 def finish_kernel(sum_ref, other_ref, received_ref, tree_ref, accepted_ref):
@@ -693,11 +687,10 @@
             axis_index_groups=halves,
             tiled=True,
         )
-        relay = relayed(place, returned, partner)
+        relay, own_sum, posted = gathered(
+            place, returned, own, partner, own_resid, req_count * req_dev
+        )
         other_sum = lax.ppermute(relay, "req", across)
-        own_sum, posted = gathered(
-            place, returned, own, partner, own_resid, relay, req_count * req_dev
-        )
     else:
         returned = lax.all_to_all(
             produced.reshape(req_count * tp_count, -1, quarter),

time: 87.6 us -> 85.5 us (0.976)
  starting transfers between devices: 30.3 us -> 28.2 us
    ppermute x7, starting transfers between devices: 11.9 us -> 10.7 us  [on_device(): lax.ppermute(sent[step], 'req', [(i, i ^ step) for i in range(req_count)])]
    pallas_call x1 -> x0, Pallas kernels: 1.06 us -> none  [relayed(): pl.pallas_call(relay_kernel, out_shape=jax.ShapeDtypeStruct((partner.shap...]
  transfers between devices with their start and end apart: 14 -> 14, of which waited for: 7 -> 8; matrix products, arithmetic and copies ran while one was open for 9% -> 9% of each run, Pallas kernels for 1% -> 1%
where the time goes in v5:
time: 85.5 us; the launch traced here: 85.1 us
  waiting for transfers between devices  29.7 us (35%)
  starting transfers between devices  28.2 us (33%)
  Pallas kernels  17.2 us (20%)
  local copies, waits for them, and re-layouts  7.74 us (9%)
  other arithmetic  1.38 us (2%)
  between operations  0.91 us (1%)
    ppermute x7, starting transfers between devices, on_device(): lax.ppermute(sent[step], 'req', [(i, i ^ step) for i in range(req_count)])  10.7 us
    ppermute x1, waiting for transfers between devices, on_device(): other_sum = lax.ppermute(relay, 'req', across)  8.88 us
    pallas_call x1, Pallas kernels, attention_part(): pl.pallas_call(functools.partial(attention_kernel, tp_count), out_shape=[...  7.68 us
    ppermute x1, waiting for transfers between devices, on_device(): partner = lax.ppermute(own, 'req', across)  7.47 us
    all_to_all x1, starting transfers between devices, on_device(): lax.all_to_all(produced.reshape(side * tp_count, -1, quarter), ('req', 't...  6.15 us
    dynamic_slice x1, local copies, waits for them, and re-layouts, on_device(): lax.dynamic_slice_in_dim(w_in, tp_rank * 2, 2, 0).transpose(0, 2, 1, 3)  5.76 us
    ppermute x1, waiting for transfers between devices, on_device(): half = added(chip, lax.ppermute(chip, 'tp', far))  4.83 us
    pallas_call x1, Pallas kernels, expert_rows(): pl.pallas_call(expert_kernel, out_shape=jax.ShapeDtypeStruct((groups // 2...  4.1 us
  transfers between devices with their start and end apart: 14, of which 8 were waited for; matrix products, arithmetic and copies ran while one was open for 9% of the time, Pallas kernels for 1%

profile of v5, /device:TPU:0, one launch (start us, length us, event | category | flops | bytes accessed | tf_op | source)
XLA Modules:
  0.0 85.1 jit_solution(3383369603079694096)
XLA Ops:
  0.7 7.7 %attention.1 = (bf16[64,1536]{1,0:T(8,128)(2,1)}, bf16[64,1536]{1,0:T(8,128)(2,1)}) custom-call(s32[2]{0:T(128)} %lengths_ref.1, f32[1536]{0:T(1024)} %gain_hbm.1, s32[2,64]{1,0:T(2,128)} %depths_hbm.1, s32[2,64,64]{2,1,0:T(8,128)} %mask_hbm.1, bf16[2,64,1536]{2,1,0:T(8,128)(2,1)} %drafts_ref.1, bf16[1536,384]{1,0:T(8,128)(2,1)} %wq_hbm.1, ...), custom_call_target="tpu_custom_call" | custom-call | tf_op jit(solution)/shard_map/attention/pallas_call | solution.py:244
  8.9 1.3 %collective-permute-done = bf16[64,1536]{1,0:T(8,128)(2,1)S(1)} collective-permute-done((bf16[64,1536]{1,0:T(8,128)(2,1)}, bf16[64,1536]{1,0:T(8,128)(2,1)S(1)}, u32[]{:S(2)}, u32[]{:S(2)}) %collective-permute-start) | collective-permute-done | bytes 196640 | tf_op jit(solution)/shard_map/ppermute | solution.py:614
  10.2 1.0 %add_convert_fusion.1 = bf16[64,1536]{1,0:T(8,128)(2,1)S(1)} fusion(bf16[64,1536]{1,0:T(8,128)(2,1)S(1)} %collective-permute-done, bf16[64,1536]{1,0:T(8,128)(2,1)} %get-tuple-element.20), kind=kLoop, calls=%fused_computation.6 | loop fusion | flops 393216 | bytes 589824 | tf_op jit(solution)/shard_map/convert_element_type | solution.py:612
  11.1 2.9 %collective-permute-start.1 = (bf16[64,1536]{1,0:T(8,128)(2,1)S(1)}, bf16[64,1536]{1,0:T(8,128)(2,1)S(1)}, u32[]{:S(2)}, u32[]{:S(2)}) collective-permute-start(bf16[64,1536]{1,0:T(8,128)(2,1)S(1)} %add_convert_fusion.1), channel_id=1, source_target_pairs={{0,2},{1,3},{2,0},{3,1},{4,6},{5,7},{6,4},{7,5},{8,10},{9,11},{10,... | collective-permute-start | bytes 589832 | tf_op jit(solution)/shard_map/ppermute | solution.py:615
  14.4 4.8 %collective-permute-done.1 = bf16[64,1536]{1,0:T(8,128)(2,1)S(1)} collective-permute-done((bf16[64,1536]{1,0:T(8,128)(2,1)S(1)}, bf16[64,1536]{1,0:T(8,128)(2,1)S(1)}, u32[]{:S(2)}, u32[]{:S(2)}) %collective-permute-start.1) | collective-permute-done | bytes 196640 | tf_op jit(solution)/shard_map/ppermute | solution.py:615
  19.6 1.2 %collective-permute-done.2.other_ref = bf16[64,1536]{1,0:T(8,128)(2,1)S(1)} collective-permute-done((bf16[64,1536]{1,0:T(8,128)(2,1)S(1)}, bf16[64,1536]{1,0:T(8,128)(2,1)S(1)}, u32[]{:S(2)}, u32[]{:S(2)}) %collective-permute-start.2) | collective-permute-done | bytes 196640 | tf_op jit(solution)/shard_map/ppermute | solution.py:616
  20.8 1.4 %dispatch.1 = (f32[128,32]{1,0:T(8,128)S(1)}, bf16[32,1536]{1,0:T(8,128)(2,1)S(1)}, bf16[32,1536]{1,0:T(8,128)(2,1)S(1)}, bf16[32,1536]{1,0:T(8,128)(2,1)S(1)}, ...) custom-call(s32[6]{0:T(128)S(1)} %stack.27.place_ref, ...), custom_call_target="tpu_custom_call" | custom-call | tf_op jit(solution)/shard_map/dispatch/pallas_call | solution.py:316
  22.3 1.8 %collective-permute-start.3 = (bf16[32,1536]{1,0:T(8,128)(2,1)S(1)}, bf16[32,1536]{1,0:T(8,128)(2,1)S(1)}, u32[]{:S(2)}, u32[]{:S(2)}) collective-permute-start(bf16[32,1536]{1,0:T(8,128)(2,1)S(1)} %get-tuple-element.22), channel_id=1, source_target_pairs={{0,4},{4,0},{8,12},{12,8},{16,20},{20,16},{24,28},{28,24},{1,5},{5... | collective-permute-start | bytes 294920 | tf_op jit(solution)/shard_map/ppermute | solution.py:623
  24.1 0.9 %collective-permute-start.4 = (bf16[32,1536]{1,0:T(8,128)(2,1)S(1)}, bf16[32,1536]{1,0:T(8,128)(2,1)S(1)}, u32[]{:S(2)}, u32[]{:S(2)}) collective-permute-start(bf16[32,1536]{1,0:T(8,128)(2,1)S(1)} %get-tuple-element.23), channel_id=1, source_target_pairs={{0,8},{4,12},{8,0},{12,4},{16,24},{20,28},{24,16},{28,20},{1,9},{5... | collective-permute-start | bytes 294920 | tf_op jit(solution)/shard_map/ppermute | solution.py:623
  25.0 3.3 %collective-permute-start.5 = (bf16[32,1536]{1,0:T(8,128)(2,1)S(1)}, bf16[32,1536]{1,0:T(8,128)(2,1)S(1)}, u32[]{:S(2)}, u32[]{:S(2)}) collective-permute-start(bf16[32,1536]{1,0:T(8,128)(2,1)S(1)} %get-tuple-element.24), channel_id=1, source_target_pairs={{0,16},{4,20},{8,24},{12,28},{16,0},{20,4},{24,8},{28,12},{1,17},{... | collective-permute-start | bytes 294920 | tf_op jit(solution)/shard_map/ppermute | solution.py:623
  28.3 2.3 %collective-permute-start.7 = (bf16[32,1536]{1,0:T(8,128)(2,1)S(1)}, bf16[32,1536]{1,0:T(8,128)(2,1)S(1)}, u32[]{:S(2)}, u32[]{:S(2)}) collective-permute-start(bf16[32,1536]{1,0:T(8,128)(2,1)S(1)} %get-tuple-element.26), channel_id=1, source_target_pairs={{0,24},{4,28},{8,16},{12,20},{16,8},{20,12},{24,0},{28,4},{1,25},{... | collective-permute-start | bytes 294920 | tf_op jit(solution)/shard_map/ppermute | solution.py:623
  30.6 2.4 %collective-permute-start.8 = (bf16[32,1536]{1,0:T(8,128)(2,1)S(1)}, bf16[32,1536]{1,0:T(8,128)(2,1)S(1)}, u32[]{:S(2)}, u32[]{:S(2)}) collective-permute-start(bf16[32,1536]{1,0:T(8,128)(2,1)S(1)} %get-tuple-element.27), channel_id=1, source_target_pairs={{0,28},{4,24},{8,20},{12,16},{16,12},{20,8},{24,4},{28,0},{1,29},{... | collective-permute-start | bytes 294920 | tf_op jit(solution)/shard_map/ppermute | solution.py:623
  33.0 5.8 %constant_dynamic-slice_fusion.1 = bf16[2,1536,2,384]{3,2,1,0:T(2,128)(2,1)S(1)} fusion(bf16[8,1536,2,384]{3,2,1,0:T(2,128)(2,1)} %param.28, s32[]{:T(128)S(6)} %select_n.57), kind=kLoop, calls=%fused_computation.23 | loop fusion | bytes 9437188 | tf_op jit(solution)/shard_map/dynamic_slice | solution.py:652
  40.0 1.0 %fetch.1 = (bf16[2,2,1536,384]{3,2,1,0:T(8,128)(2,1)S(1)}, bf16[2,384,1536]{2,1,0:T(8,128)(2,1)S(1)}) custom-call(s32[6]{0:T(128)S(1)} %stack.27.place_ref, bf16[2,2,1536,384]{3,2,1,0:T(8,128)(2,1)S(1)} %bitcast.24, bf16[8,384,1536]{2,1,0:T(8,128)(2,1)S(1)} %bitcast.26), custom_call_target="tpu_custom_call" | custom-call | tf_op jit(solution)/shard_map/fetch/pallas_call | solution.py:346
  41.5 1.7 %collective-permute-done.9.rest_6_ = bf16[32,1536]{1,0:T(8,128)(2,1)S(1)} collective-permute-done((bf16[32,1536]{1,0:T(8,128)(2,1)S(1)}, bf16[32,1536]{1,0:T(8,128)(2,1)S(1)}, u32[]{:S(2)}, u32[]{:S(2)}) %collective-permute-start.9) | collective-permute-done | bytes 98336 | tf_op jit(solution)/shard_map/ppermute | solution.py:623
  43.2 4.1 %experts.1 = bf16[4,4,2,32,384]{4,3,2,1,0:T(8,128)(2,1)} custom-call(s32[6]{0:T(128)S(1)} %stack.27.place_ref, bf16[2,2,1536,384]{3,2,1,0:T(8,128)(2,1)S(1)} %get-tuple-element.18.wi, bf16[768,1536]{1,0:T(8,128)(2,1)S(1)} %bitcast.27, bf16[32,1536]{1,0:T(8,128)(2,1)S(1)} %collective-permute-done.3.rest_0_, ...), custom_call_target="tpu_custom_call" | custom-call | tf_op jit(solution)/shard_map/experts/pallas_call | solution.py:387
  47.3 6.2 %all-to-all-start = ((bf16[16,64,384]{2,1,0:T(8,128)(2,1)}), bf16[16,64,384]{2,1,0:T(8,128)(2,1)S(1)}, u32[]{:S(2)}, u32[]{:S(2)}) async-start(bf16[16,64,384]{2,1,0:T(8,128)(2,1)} %bitcast.12), calls=%async_computation | async-start | bytes 1572864 | tf_op jit(solution)/shard_map/all_to_all | solution.py:682
  54.1 1.6 %collective-permute-start.10 = (f32[16,128]{1,0:T(8,128)S(1)}, f32[16,128]{1,0:T(8,128)S(1)}, u32[]{:S(2)}, u32[]{:S(2)}) collective-permute-start(f32[16,128]{1,0:T(8,128)S(1)} %concatenate.9.own_ref), channel_id=1, source_target_pairs={{0,16},{4,20},{8,24},{12,28},{16,0},{20,4},{24,8},{28,12},{1,17},{... | collective-permute-start | bytes 24584 | tf_op jit(solution)/shard_map/ppermute | solution.py:681
  55.6 7.5 %collective-permute-done.10.partner_ref = f32[16,128]{1,0:T(8,128)S(1)} collective-permute-done((f32[16,128]{1,0:T(8,128)S(1)}, f32[16,128]{1,0:T(8,128)S(1)}, u32[]{:S(2)}, u32[]{:S(2)}) %collective-permute-start.10) | collective-permute-done | bytes 8224 | tf_op jit(solution)/shard_map/ppermute | solution.py:681
  63.1 3.9 %all-to-all-done.rows_ref = bf16[16,64,384]{2,1,0:T(8,128)(2,1)S(1)} async-done(((bf16[16,64,384]{2,1,0:T(8,128)(2,1)}), bf16[16,64,384]{2,1,0:T(8,128)(2,1)S(1)}, u32[]{:S(2)}, u32[]{:S(2)}) %all-to-all-start) | async-done | bytes 786464 | tf_op jit(solution)/shard_map/all_to_all | solution.py:682
  67.0 2.3 %gather.1 = (bf16[128,384]{1,0:T(8,128)(2,1)S(1)}, f32[128,384]{1,0:T(8,128)S(1)}, bf16[16,16,384]{2,1,0:T(8,128)(2,1)}) custom-call(s32[6]{0:T(128)S(1)} %stack.27.place_ref, bf16[16,64,384]{2,1,0:T(8,128)(2,1)S(1)} %all-to-all-done.rows_ref, f32[16,128]{1,0:T(8,128)S(1)} %concatenate.9.own_ref, f32[16,128]{1,0:T(8,128)S(1)} %collective-permute-done.10.partner_ref, ...), custom_call_target="tpu_custom_call" | custom-call | tf_op jit(solution)/shard_map/gather/pallas_call | solution.py:494
  69.3 3.4 %all-to-all-start.1 = ((bf16[8,2,16,384]{3,2,1,0:T(8,128)(2,1)}), bf16[8,2,16,384]{3,2,1,0:T(8,128)(2,1)S(1)}, u32[]{:S(2)}, u32[]{:S(2)}) async-start(bf16[8,2,16,384]{3,2,1,0:T(8,128)(2,1)} %bitcast.16), calls=%async_computation.1 | async-start | bytes 393216 | tf_op jit(solution)/shard_map/all_to_all | solution.py:711
  72.7 2.8 %collective-permute-start.11 = (bf16[128,384]{1,0:T(8,128)(2,1)S(1)}, bf16[128,384]{1,0:T(8,128)(2,1)S(1)}, u32[]{:S(2)}, u32[]{:S(2)}) collective-permute-start(bf16[128,384]{1,0:T(8,128)(2,1)S(1)} %get-tuple-element.32), channel_id=1, source_target_pairs={{0,16},{4,20},{8,24},{12,28},{16,0},{20,4},{24,8},{28,12},{1,17},{... | collective-permute-start | bytes 294920 | tf_op jit(solution)/shard_map/ppermute | solution.py:693
  75.5 8.9 %collective-permute-done.11.other_ref = bf16[128,384]{1,0:T(8,128)(2,1)S(1)} collective-permute-done((bf16[128,384]{1,0:T(8,128)(2,1)S(1)}, bf16[128,384]{1,0:T(8,128)(2,1)S(1)}, u32[]{:S(2)}, u32[]{:S(2)}) %collective-permute-start.11) | collective-permute-done | bytes 98336 | tf_op jit(solution)/shard_map/ppermute | solution.py:693
  (57 shorter events, 4.0 us)
Async XLA Ops:
  0.6 20.2 %copy-start = (bf16[2,64,1536]{2,1,0:T(8,128)(2,1)S(1)}, bf16[2,64,1536]{2,1,0:T(8,128)(2,1)}, u32[]{:S(2)}) copy-start(bf16[2,64,1536]{2,1,0:T(8,128)(2,1)} %drafts_ref.1) | copy-start | bytes 1179652
  0.6 13.4 %copy-start.3 = (s32[2,64,4]{1,2,0:T(4,128)S(1)}, s32[2,64,4]{1,2,0:T(4,128)}, u32[]{:S(2)}) copy-start(s32[2,64,4]{1,2,0:T(4,128)} %param.27) | copy-start | bytes 6148
  0.7 20.2 %copy-start.1 = (bf16[1536,32]{0,1:T(8,128)(2,1)S(1)}, bf16[1536,32]{0,1:T(8,128)(2,1)}, u32[]{:S(2)}) copy-start(bf16[1536,32]{0,1:T(8,128)(2,1)} %param.26) | copy-start | bytes 294916
  0.7 20.2 %copy-start.2 = (f32[1536]{0:T(1024)S(1)}, f32[1536]{0:T(1024)}, u32[]{:S(2)}) copy-start(f32[1536]{0:T(1024)} %gain_ref.1) | copy-start | bytes 18436
  8.4 1.8 %collective-permute-start = (bf16[64,1536]{1,0:T(8,128)(2,1)}, bf16[64,1536]{1,0:T(8,128)(2,1)S(1)}, u32[]{:S(2)}, u32[]{:S(2)}) collective-permute-start(bf16[64,1536]{1,0:T(8,128)(2,1)} %get-tuple-element.21), channel_id=1, source_target_pairs={{0,1},{1,0},{2,3},{3,2},{4,5},{5,4},{6,7},{7,6},{8,9},{9,8},{10,11... | collective-permute-start | bytes 589832 | tf_op jit(solution)/shard_map/ppermute | solution.py:614
  11.1 8.1 %collective-permute-start.1 = (bf16[64,1536]{1,0:T(8,128)(2,1)S(1)}, bf16[64,1536]{1,0:T(8,128)(2,1)S(1)}, u32[]{:S(2)}, u32[]{:S(2)}) collective-permute-start(bf16[64,1536]{1,0:T(8,128)(2,1)S(1)} %add_convert_fusion.1), channel_id=1, source_target_pairs={{0,2},{1,3},{2,0},{3,1},{4,6},{5,7},{6,4},{7,5},{8,10},{9,11},{10,... | collective-permute-start | bytes 589832 | tf_op jit(solution)/shard_map/ppermute | solution.py:615
  19.3 1.5 %collective-permute-start.2 = (bf16[64,1536]{1,0:T(8,128)(2,1)S(1)}, bf16[64,1536]{1,0:T(8,128)(2,1)S(1)}, u32[]{:S(2)}, u32[]{:S(2)}) collective-permute-start(bf16[64,1536]{1,0:T(8,128)(2,1)S(1)} %add_convert_fusion.half_ref), channel_id=1, source_target_pairs={{0,1},{1,0},{2,3},{3,2},{4,5},{5,4},{6,7},{7,6},{8,9},{9,8},{10,11... | collective-permute-start | bytes 589832 | tf_op jit(solution)/shard_map/ppermute | solution.py:616
  22.3 8.3 %collective-permute-start.3 = (bf16[32,1536]{1,0:T(8,128)(2,1)S(1)}, bf16[32,1536]{1,0:T(8,128)(2,1)S(1)}, u32[]{:S(2)}, u32[]{:S(2)}) collective-permute-start(bf16[32,1536]{1,0:T(8,128)(2,1)S(1)} %get-tuple-element.22), channel_id=1, source_target_pairs={{0,4},{4,0},{8,12},{12,8},{16,20},{20,16},{24,28},{28,24},{1,5},{5... | collective-permute-start | bytes 294920 | tf_op jit(solution)/shard_map/ppermute | solution.py:623
  24.1 8.9 %collective-permute-start.4 = (bf16[32,1536]{1,0:T(8,128)(2,1)S(1)}, bf16[32,1536]{1,0:T(8,128)(2,1)S(1)}, u32[]{:S(2)}, u32[]{:S(2)}) collective-permute-start(bf16[32,1536]{1,0:T(8,128)(2,1)S(1)} %get-tuple-element.23), channel_id=1, source_target_pairs={{0,8},{4,12},{8,0},{12,4},{16,24},{20,28},{24,16},{28,20},{1,9},{5... | collective-permute-start | bytes 294920 | tf_op jit(solution)/shard_map/ppermute | solution.py:623
  25.0 16.1 %collective-permute-start.5 = (bf16[32,1536]{1,0:T(8,128)(2,1)S(1)}, bf16[32,1536]{1,0:T(8,128)(2,1)S(1)}, u32[]{:S(2)}, u32[]{:S(2)}) collective-permute-start(bf16[32,1536]{1,0:T(8,128)(2,1)S(1)} %get-tuple-element.24), channel_id=1, source_target_pairs={{0,16},{4,20},{8,24},{12,28},{16,0},{20,4},{24,8},{28,12},{1,17},{... | collective-permute-start | bytes 294920 | tf_op jit(solution)/shard_map/ppermute | solution.py:623
  28.3 13.2 %collective-permute-start.6 = (bf16[32,1536]{1,0:T(8,128)(2,1)S(1)}, bf16[32,1536]{1,0:T(8,128)(2,1)S(1)}, u32[]{:S(2)}, u32[]{:S(2)}) collective-permute-start(bf16[32,1536]{1,0:T(8,128)(2,1)S(1)} %get-tuple-element.25), channel_id=1, source_target_pairs={{0,20},{4,16},{8,28},{12,24},{16,4},{20,0},{24,12},{28,8},{1,21},{... | collective-permute-start | bytes 294920 | tf_op jit(solution)/shard_map/ppermute | solution.py:623
  28.3 13.2 %collective-permute-start.7 = (bf16[32,1536]{1,0:T(8,128)(2,1)S(1)}, bf16[32,1536]{1,0:T(8,128)(2,1)S(1)}, u32[]{:S(2)}, u32[]{:S(2)}) collective-permute-start(bf16[32,1536]{1,0:T(8,128)(2,1)S(1)} %get-tuple-element.26), channel_id=1, source_target_pairs={{0,24},{4,28},{8,16},{12,20},{16,8},{20,12},{24,0},{28,4},{1,25},{... | collective-permute-start | bytes 294920 | tf_op jit(solution)/shard_map/ppermute | solution.py:623
  30.6 10.9 %collective-permute-start.8 = (bf16[32,1536]{1,0:T(8,128)(2,1)S(1)}, bf16[32,1536]{1,0:T(8,128)(2,1)S(1)}, u32[]{:S(2)}, u32[]{:S(2)}) collective-permute-start(bf16[32,1536]{1,0:T(8,128)(2,1)S(1)} %get-tuple-element.27), channel_id=1, source_target_pairs={{0,28},{4,24},{8,20},{12,16},{16,12},{20,8},{24,4},{28,0},{1,29},{... | collective-permute-start | bytes 294920 | tf_op jit(solution)/shard_map/ppermute | solution.py:623
  33.0 10.2 %collective-permute-start.9 = (bf16[32,1536]{1,0:T(8,128)(2,1)S(1)}, bf16[32,1536]{1,0:T(8,128)(2,1)S(1)}, u32[]{:S(2)}, u32[]{:S(2)}) collective-permute-start(bf16[32,1536]{1,0:T(8,128)(2,1)S(1)} %get-tuple-element.28), channel_id=1, source_target_pairs={{0,12},{4,8},{8,4},{12,0},{16,28},{20,24},{24,20},{28,16},{1,13},{... | collective-permute-start | bytes 294920 | tf_op jit(solution)/shard_map/ppermute | solution.py:623
  33.0 6.4 %slice-start = ((s8[9437184]{0:T(1024)(128)(4,1)}), s8[4194304]{0:T(1024)(128)(4,1)S(1)}, s32[]{:S(2)}) async-start(s8[9437184]{0:T(1024)(128)(4,1)} %bitcast.25), calls=%async_computation.2 | async-start | bytes 8388608
  33.0 6.4 %slice-start.1 = ((s8[9437184]{0:T(1024)(128)(4,1)}), s8[4194304]{0:T(1024)(128)(4,1)S(1)}, s32[]{:S(2)}) async-start(s8[9437184]{0:T(1024)(128)(4,1)} %bitcast.25), calls=%async_computation.3 | async-start | bytes 8388608
  38.8 1.2 %slice-start.2 = ((s8[9437184]{0:T(1024)(128)(4,1)}), s8[1048576]{0:T(1024)(128)(4,1)S(1)}, s32[]{:S(2)}) async-start(s8[9437184]{0:T(1024)(128)(4,1)} %bitcast.25), calls=%async_computation.4 | async-start | bytes 2097152
  43.2 10.3 %copy-start.5 = (s32[2]{0:T(128)S(1)}, s32[2]{0:T(128)}, u32[]{:S(2)}) copy-start(s32[2]{0:T(128)} %param.31) | copy-start | bytes 28
  43.2 10.5 %copy-start.4 = (s32[2,64]{1,0:T(2,128)S(1)}, s32[2,64]{1,0:T(2,128)}, u32[]{:S(2)}) copy-start(s32[2,64]{1,0:T(2,128)} %param.30) | copy-start | bytes 1540
  47.3 19.7 %all-to-all-start = ((bf16[16,64,384]{2,1,0:T(8,128)(2,1)}), bf16[16,64,384]{2,1,0:T(8,128)(2,1)S(1)}, u32[]{:S(2)}, u32[]{:S(2)}) async-start(bf16[16,64,384]{2,1,0:T(8,128)(2,1)} %bitcast.12), calls=%async_computation | async-start | bytes 1572864 | tf_op jit(solution)/shard_map/all_to_all | solution.py:682
  54.1 9.1 %collective-permute-start.10 = (f32[16,128]{1,0:T(8,128)S(1)}, f32[16,128]{1,0:T(8,128)S(1)}, u32[]{:S(2)}, u32[]{:S(2)}) collective-permute-start(f32[16,128]{1,0:T(8,128)S(1)} %concatenate.9.own_ref), channel_id=1, source_target_pairs={{0,16},{4,20},{8,24},{12,28},{16,0},{20,4},{24,8},{28,12},{1,17},{... | collective-permute-start | bytes 24584 | tf_op jit(solution)/shard_map/ppermute | solution.py:681
  69.3 15.1 %all-to-all-start.1 = ((bf16[8,2,16,384]{3,2,1,0:T(8,128)(2,1)}), bf16[8,2,16,384]{3,2,1,0:T(8,128)(2,1)S(1)}, u32[]{:S(2)}, u32[]{:S(2)}) async-start(bf16[8,2,16,384]{3,2,1,0:T(8,128)(2,1)} %bitcast.16), calls=%async_computation.1 | async-start | bytes 393216 | tf_op jit(solution)/shard_map/all_to_all | solution.py:711
  72.7 11.7 %collective-permute-start.11 = (bf16[128,384]{1,0:T(8,128)(2,1)S(1)}, bf16[128,384]{1,0:T(8,128)(2,1)S(1)}, u32[]{:S(2)}, u32[]{:S(2)}) collective-permute-start(bf16[128,384]{1,0:T(8,128)(2,1)S(1)} %get-tuple-element.32), channel_id=1, source_target_pairs={{0,16},{4,20},{8,24},{12,28},{16,0},{20,4},{24,8},{28,12},{1,17},{... | collective-permute-start | bytes 294920 | tf_op jit(solution)/shard_map/ppermute | solution.py:693

commit v6 on v5

--- a/solution.py
+++ b/solution.py
@@ -442,29 +442,29 @@
     )(order, rows, targets, gates, resid, slots)
 
 
-def mixture(place_ref, rows_ref, pack_ref, side):
+def weighted(rows_ref, matrix_ref, side):
     experts, _, quarter = rows_ref.shape
-    pack = jnp.transpose(pack_ref[...])
-    first = place_ref[5] * (experts * CAP)
-    places = lax.broadcasted_iota(jnp.int32, (pack.shape[0], experts * CAP), 1) + first
-    matrix = jnp.zeros(places.shape, jnp.float32)
-    for pick in range(TOPK):
-        target = pack[:, pick : pick + 1].astype(jnp.int32)
-        gate = pack[:, TOPK + pick : TOPK + pick + 1]
-        matrix = matrix + jnp.where(places == target, gate, 0.0)
     rows = rows_ref[:, side * CAP : (side + 1) * CAP].reshape(experts * CAP, quarter)
-    return jnp.dot(matrix.astype(jnp.bfloat16), rows, preferred_element_type=jnp.float32)
+    return jnp.dot(matrix_ref[...], rows, preferred_element_type=jnp.float32)
 
 
 def gather_kernel(
-    place_ref, rows_ref, own_ref, partner_ref, resid_ref, relay_ref, sum_ref, posted_ref
+    rows_ref,
+    own_ref,
+    partner_ref,
+    own_matrix_ref,
+    partner_matrix_ref,
+    resid_ref,
+    relay_ref,
+    sum_ref,
+    posted_ref,
 ):
     requests, keep, quarter = posted_ref.shape
     tokens = own_ref.shape[1]
     tree = tokens // REQ_DEV
-    relay = mixture(place_ref, rows_ref, partner_ref, 1).astype(jnp.bfloat16)
+    relay = weighted(rows_ref, partner_matrix_ref, 1).astype(jnp.bfloat16)
     relay_ref[...] = relay
-    own_sum = resid_ref[...] + mixture(place_ref, rows_ref, own_ref, 0)
+    own_sum = resid_ref[...] + weighted(rows_ref, own_matrix_ref, 0)
     sum_ref[...] = own_sum
     posted = [jnp.zeros((keep, quarter), jnp.float32)] * requests
     for pack_ref, done in (
@@ -487,10 +487,9 @@
         posted_ref[place] = posted[place].astype(jnp.bfloat16)
 
 
-def gathered(place, rows, own, partner, resid, requests):
+def gathered(rows, own, partner, matrices, resid, requests):
     tokens, quarter = resid.shape
     whole = pl.BlockSpec(memory_space=pltpu.VMEM)
-    scalar = pl.BlockSpec(memory_space=pltpu.SMEM)
     return pl.pallas_call(
         gather_kernel,
         out_shape=[
@@ -498,11 +497,11 @@
             jax.ShapeDtypeStruct((tokens, quarter), jnp.float32),
             jax.ShapeDtypeStruct((requests, KEEP, quarter), jnp.bfloat16),
         ],
-        in_specs=[scalar] + [whole] * 4,
+        in_specs=[whole] * 6,
         out_specs=[whole] * 3,
         compiler_params=pltpu.CompilerParams(vmem_limit_bytes=SOME_VMEM),
         name="gather",
-    )(place, rows, own, partner, resid)
+    )(rows, own, partner, *matrices, resid)
 
 
 def finish_kernel(sum_ref, other_ref, received_ref, tree_ref, accepted_ref):
@@ -649,7 +648,8 @@
     )
 
     if by_expert:
-        own_in = lax.dynamic_slice_in_dim(w_in, tp_rank * 2, 2, 0).transpose(0, 2, 1, 3)
+        begin = lax.optimization_barrier((tp_rank * 2, arrived[1]))[0]
+        own_in = lax.dynamic_slice_in_dim(w_in, begin, 2, 0).transpose(0, 2, 1, 3)
         own_in, own_out = fetched(own_in, w_out, place)
         produced = expert_rows(arrived, own_in, own_out.reshape(-1, width), place, tp_count)
     else:
@@ -679,6 +679,19 @@
             axis=0,
         )
         partner = lax.ppermute(own, "req", across)
+        places = jnp.arange(side * tp_count * CAP) + req_rank // side * (side * tp_count * CAP)
+
+        def combining(pack):
+            hits = [
+                jnp.where(
+                    pack[pick][:, None].astype(jnp.int32) == places[None, :],
+                    pack[TOPK + pick][:, None],
+                    0.0,
+                )
+                for pick in range(TOPK)
+            ]
+            return functools.reduce(jnp.add, hits).astype(jnp.bfloat16)
+
         returned = lax.all_to_all(
             produced.reshape(side * tp_count, -1, quarter),
             ("req", "tp"),
@@ -688,7 +701,12 @@
             tiled=True,
         )
         relay, own_sum, posted = gathered(
-            place, returned, own, partner, own_resid, req_count * req_dev
+            returned,
+            own,
+            partner,
+            [combining(own), combining(partner)],
+            own_resid,
+            req_count * req_dev,
         )
         other_sum = lax.ppermute(relay, "req", across)
     else:

time: 85.5 us -> 84.5 us (0.988)
  Pallas kernels: 17.2 us -> 15.3 us
    pallas_call x1, Pallas kernels: 2.26 us -> 1.17 us  [gathered(): pl.pallas_call(gather_kernel, out_shape=[jax.ShapeDtypeStruct((tokens, qu...]
    ppermute x7, starting transfers between devices: 10.7 us -> 11.8 us  [on_device(): lax.ppermute(sent[step], 'req', [(i, i ^ step) for i in range(req_count)])]
where the time goes in v6:
time: 84.5 us; the launch traced here: 84.1 us
  waiting for transfers between devices  30.1 us (36%)
  starting transfers between devices  28.3 us (33%)
  Pallas kernels  15.3 us (18%)
  local copies, waits for them, and re-layouts  7.75 us (9%)
  other arithmetic  1.73 us (2%)
  between operations  0.93 us (1%)
    ppermute x7, starting transfers between devices, on_device(): lax.ppermute(sent[step], 'req', [(i, i ^ step) for i in range(req_count)])  11.8 us
    ppermute x1, waiting for transfers between devices, on_device(): other_sum = lax.ppermute(relay, 'req', across)  8.88 us
    ppermute x1, waiting for transfers between devices, on_device(): partner = lax.ppermute(own, 'req', across)  7.79 us
    pallas_call x1, Pallas kernels, attention_part(): pl.pallas_call(functools.partial(attention_kernel, tp_count), out_shape=[...  6.98 us
    dynamic_slice x1, local copies, waits for them, and re-layouts, on_device(): own_in = lax.dynamic_slice_in_dim(w_in, begin, 2, 0).transpose(0, 2, 1, 3)  5.76 us
    all_to_all x1, starting transfers between devices, on_device(): lax.all_to_all(produced.reshape(side * tp_count, -1, quarter), ('req', 't...  5.4 us
    ppermute x1, waiting for transfers between devices, on_device(): half = added(chip, lax.ppermute(chip, 'tp', far))  4.83 us
    pallas_call x1, Pallas kernels, expert_rows(): pl.pallas_call(expert_kernel, out_shape=jax.ShapeDtypeStruct((groups // 2...  4.08 us
  transfers between devices with their start and end apart: 14, of which 8 were waited for; matrix products, arithmetic and copies ran while one was open for 9% of the time, Pallas kernels for 1%

profile of v6, /device:TPU:0, one launch (start us, length us, event | category | flops | bytes accessed | tf_op | source)
XLA Modules:
  0.0 84.1 jit_solution(2558556237666581542)
XLA Ops:
  0.7 7.0 %attention.1 = (bf16[64,1536]{1,0:T(8,128)(2,1)}, bf16[64,1536]{1,0:T(8,128)(2,1)}) custom-call(s32[2]{0:T(128)} %lengths_ref.1, f32[1536]{0:T(1024)} %gain_hbm.1, s32[2,64]{1,0:T(2,128)} %depths_hbm.1, s32[2,64,64]{2,1,0:T(8,128)} %mask_hbm.1, bf16[2,64,1536]{2,1,0:T(8,128)(2,1)} %drafts_ref.1, bf16[1536,384]{1,0:T(8,128)(2,1)} %wq_hbm.1, ...), custom_call_target="tpu_custom_call" | custom-call | tf_op jit(solution)/shard_map/attention/pallas_call | solution.py:244
  8.2 1.3 %collective-permute-done = bf16[64,1536]{1,0:T(8,128)(2,1)S(1)} collective-permute-done((bf16[64,1536]{1,0:T(8,128)(2,1)}, bf16[64,1536]{1,0:T(8,128)(2,1)S(1)}, u32[]{:S(2)}, u32[]{:S(2)}) %collective-permute-start) | collective-permute-done | bytes 196640 | tf_op jit(solution)/shard_map/ppermute | solution.py:613
  10.5 2.9 %collective-permute-start.1 = (bf16[64,1536]{1,0:T(8,128)(2,1)S(1)}, bf16[64,1536]{1,0:T(8,128)(2,1)S(1)}, u32[]{:S(2)}, u32[]{:S(2)}) collective-permute-start(bf16[64,1536]{1,0:T(8,128)(2,1)S(1)} %add_convert_fusion.1), channel_id=1, source_target_pairs={{0,2},{1,3},{2,0},{3,1},{4,6},{5,7},{6,4},{7,5},{8,10},{9,11},{10,... | collective-permute-start | bytes 589832 | tf_op jit(solution)/shard_map/ppermute | solution.py:614
  13.8 4.8 %collective-permute-done.1 = bf16[64,1536]{1,0:T(8,128)(2,1)S(1)} collective-permute-done((bf16[64,1536]{1,0:T(8,128)(2,1)S(1)}, bf16[64,1536]{1,0:T(8,128)(2,1)S(1)}, u32[]{:S(2)}, u32[]{:S(2)}) %collective-permute-start.1) | collective-permute-done | bytes 196640 | tf_op jit(solution)/shard_map/ppermute | solution.py:614
  19.0 1.1 %collective-permute-done.2.other_ref = bf16[64,1536]{1,0:T(8,128)(2,1)S(1)} collective-permute-done((bf16[64,1536]{1,0:T(8,128)(2,1)S(1)}, bf16[64,1536]{1,0:T(8,128)(2,1)S(1)}, u32[]{:S(2)}, u32[]{:S(2)}) %collective-permute-start.2) | collective-permute-done | bytes 196640 | tf_op jit(solution)/shard_map/ppermute | solution.py:615
  20.2 1.4 %dispatch.1 = (f32[128,32]{1,0:T(8,128)S(1)}, bf16[32,1536]{1,0:T(8,128)(2,1)S(1)}, bf16[32,1536]{1,0:T(8,128)(2,1)S(1)}, bf16[32,1536]{1,0:T(8,128)(2,1)S(1)}, ...) custom-call(s32[6]{0:T(128)S(1)} %stack.27.place_ref, ...), custom_call_target="tpu_custom_call" | custom-call | tf_op jit(solution)/shard_map/dispatch/pallas_call | solution.py:316
  21.6 2.5 %collective-permute-start.3 = (bf16[32,1536]{1,0:T(8,128)(2,1)S(1)}, bf16[32,1536]{1,0:T(8,128)(2,1)S(1)}, u32[]{:S(2)}, u32[]{:S(2)}) collective-permute-start(bf16[32,1536]{1,0:T(8,128)(2,1)S(1)} %get-tuple-element.21), channel_id=1, source_target_pairs={{0,4},{4,0},{8,12},{12,8},{16,20},{20,16},{24,28},{28,24},{1,5},{5... | collective-permute-start | bytes 294920 | tf_op jit(solution)/shard_map/ppermute | solution.py:622
  24.1 1.6 %collective-permute-start.4 = (bf16[32,1536]{1,0:T(8,128)(2,1)S(1)}, bf16[32,1536]{1,0:T(8,128)(2,1)S(1)}, u32[]{:S(2)}, u32[]{:S(2)}) collective-permute-start(bf16[32,1536]{1,0:T(8,128)(2,1)S(1)} %get-tuple-element.25), channel_id=1, source_target_pairs={{0,8},{4,12},{8,0},{12,4},{16,24},{20,28},{24,16},{28,20},{1,9},{5... | collective-permute-start | bytes 294920 | tf_op jit(solution)/shard_map/ppermute | solution.py:622
  25.7 2.0 %collective-permute-start.5 = (bf16[32,1536]{1,0:T(8,128)(2,1)S(1)}, bf16[32,1536]{1,0:T(8,128)(2,1)S(1)}, u32[]{:S(2)}, u32[]{:S(2)}) collective-permute-start(bf16[32,1536]{1,0:T(8,128)(2,1)S(1)} %get-tuple-element.26), channel_id=1, source_target_pairs={{0,16},{4,20},{8,24},{12,28},{16,0},{20,4},{24,8},{28,12},{1,17},{... | collective-permute-start | bytes 294920 | tf_op jit(solution)/shard_map/ppermute | solution.py:622
  27.7 1.7 %collective-permute-start.6 = (bf16[32,1536]{1,0:T(8,128)(2,1)S(1)}, bf16[32,1536]{1,0:T(8,128)(2,1)S(1)}, u32[]{:S(2)}, u32[]{:S(2)}) collective-permute-start(bf16[32,1536]{1,0:T(8,128)(2,1)S(1)} %get-tuple-element.27), channel_id=1, source_target_pairs={{0,20},{4,16},{8,28},{12,24},{16,4},{20,0},{24,12},{28,8},{1,21},{... | collective-permute-start | bytes 294920 | tf_op jit(solution)/shard_map/ppermute | solution.py:622
  29.3 1.3 %collective-permute-start.7 = (bf16[32,1536]{1,0:T(8,128)(2,1)S(1)}, bf16[32,1536]{1,0:T(8,128)(2,1)S(1)}, u32[]{:S(2)}, u32[]{:S(2)}) collective-permute-start(bf16[32,1536]{1,0:T(8,128)(2,1)S(1)} %get-tuple-element.28), channel_id=1, source_target_pairs={{0,24},{4,28},{8,16},{12,20},{16,8},{20,12},{24,0},{28,4},{1,25},{... | collective-permute-start | bytes 294920 | tf_op jit(solution)/shard_map/ppermute | solution.py:622
  30.7 2.8 %collective-permute-start.8 = (bf16[32,1536]{1,0:T(8,128)(2,1)S(1)}, bf16[32,1536]{1,0:T(8,128)(2,1)S(1)}, u32[]{:S(2)}, u32[]{:S(2)}) collective-permute-start(bf16[32,1536]{1,0:T(8,128)(2,1)S(1)} %get-tuple-element.29), channel_id=1, source_target_pairs={{0,28},{4,24},{8,20},{12,16},{16,12},{20,8},{24,4},{28,0},{1,29},{... | collective-permute-start | bytes 294920 | tf_op jit(solution)/shard_map/ppermute | solution.py:622
  33.4 5.8 %constant_dynamic-slice_fusion = bf16[2,1536,2,384]{3,2,1,0:T(2,128)(2,1)S(1)} fusion(bf16[8,1536,2,384]{3,2,1,0:T(2,128)(2,1)} %param.28, s32[]{:T(128)S(6)} %select_n.86), kind=kLoop, calls=%fused_computation.25 | loop fusion | bytes 9437188 | tf_op jit(solution)/shard_map/dynamic_slice | solution.py:652
  41.5 1.5 %collective-permute-done.6.rest_3_ = bf16[32,1536]{1,0:T(8,128)(2,1)S(1)} collective-permute-done((bf16[32,1536]{1,0:T(8,128)(2,1)S(1)}, bf16[32,1536]{1,0:T(8,128)(2,1)S(1)}, u32[]{:S(2)}, u32[]{:S(2)}) %collective-permute-start.6) | collective-permute-done | bytes 98336 | tf_op jit(solution)/shard_map/ppermute | solution.py:622
  43.0 1.1 %collective-permute-done.9.rest_6_ = bf16[32,1536]{1,0:T(8,128)(2,1)S(1)} collective-permute-done((bf16[32,1536]{1,0:T(8,128)(2,1)S(1)}, bf16[32,1536]{1,0:T(8,128)(2,1)S(1)}, u32[]{:S(2)}, u32[]{:S(2)}) %collective-permute-start.9) | collective-permute-done | bytes 98336 | tf_op jit(solution)/shard_map/ppermute | solution.py:622
  44.1 4.1 %experts.1 = bf16[4,4,2,32,384]{4,3,2,1,0:T(8,128)(2,1)} custom-call(s32[6]{0:T(128)S(1)} %stack.27.place_ref, bf16[2,2,1536,384]{3,2,1,0:T(8,128)(2,1)S(1)} %get-tuple-element.23.wi, bf16[768,1536]{1,0:T(8,128)(2,1)S(1)} %bitcast.59, bf16[32,1536]{1,0:T(8,128)(2,1)S(1)} %collective-permute-done.3.rest_0_, ...), custom_call_target="tpu_custom_call" | custom-call | tf_op jit(solution)/shard_map/experts/pallas_call | solution.py:387
  48.2 5.4 %all-to-all-start = ((bf16[16,64,384]{2,1,0:T(8,128)(2,1)}), bf16[16,64,384]{2,1,0:T(8,128)(2,1)S(1)}, u32[]{:S(2)}, u32[]{:S(2)}) async-start(bf16[16,64,384]{2,1,0:T(8,128)(2,1)} %bitcast.12), calls=%async_computation | async-start | bytes 1572864 | tf_op jit(solution)/shard_map/all_to_all | solution.py:695
  54.1 1.3 %collective-permute-start.10 = (f32[16,128]{1,0:T(8,128)S(1)}, f32[16,128]{1,0:T(8,128)S(1)}, u32[]{:S(2)}, u32[]{:S(2)}) collective-permute-start(f32[16,128]{1,0:T(8,128)S(1)} %concatenate.9.own_ref), channel_id=1, source_target_pairs={{0,16},{4,20},{8,24},{12,28},{16,0},{20,4},{24,8},{28,12},{1,17},{... | collective-permute-start | bytes 24584 | tf_op jit(solution)/shard_map/ppermute | solution.py:681
  55.4 7.8 %collective-permute-done.10.partner_ref = f32[16,128]{1,0:T(8,128)S(1)} collective-permute-done((f32[16,128]{1,0:T(8,128)S(1)}, f32[16,128]{1,0:T(8,128)S(1)}, u32[]{:S(2)}, u32[]{:S(2)}) %collective-permute-start.10) | collective-permute-done | bytes 8224 | tf_op jit(solution)/shard_map/ppermute | solution.py:681
  63.6 3.6 %all-to-all-done.rows_ref = bf16[16,64,384]{2,1,0:T(8,128)(2,1)S(1)} async-done(((bf16[16,64,384]{2,1,0:T(8,128)(2,1)}), bf16[16,64,384]{2,1,0:T(8,128)(2,1)S(1)}, u32[]{:S(2)}, u32[]{:S(2)}) %all-to-all-start) | async-done | bytes 786464 | tf_op jit(solution)/shard_map/all_to_all | solution.py:695
  67.1 1.2 %gather.1 = (bf16[128,384]{1,0:T(8,128)(2,1)S(1)}, f32[128,384]{1,0:T(8,128)S(1)}, bf16[16,16,384]{2,1,0:T(8,128)(2,1)}) custom-call(bf16[16,64,384]{2,1,0:T(8,128)(2,1)S(1)} %all-to-all-done.rows_ref, f32[16,128]{1,0:T(8,128)S(1)} %concatenate.9.own_ref, f32[16,128]{1,0:T(8,128)S(1)} %collective-permute-done.10.partner_ref, ...), custom_call_target="tpu_custom_call" | custom-call | tf_op jit(solution)/shard_map/gather/pallas_call | solution.py:493
  68.3 3.4 %all-to-all-start.1 = ((bf16[8,2,16,384]{3,2,1,0:T(8,128)(2,1)}), bf16[8,2,16,384]{3,2,1,0:T(8,128)(2,1)S(1)}, u32[]{:S(2)}, u32[]{:S(2)}) async-start(bf16[8,2,16,384]{3,2,1,0:T(8,128)(2,1)} %bitcast.32), calls=%async_computation.1 | async-start | bytes 393216 | tf_op jit(solution)/shard_map/all_to_all | solution.py:729
  71.7 2.8 %collective-permute-start.11 = (bf16[128,384]{1,0:T(8,128)(2,1)S(1)}, bf16[128,384]{1,0:T(8,128)(2,1)S(1)}, u32[]{:S(2)}, u32[]{:S(2)}) collective-permute-start(bf16[128,384]{1,0:T(8,128)(2,1)S(1)} %get-tuple-element.34), channel_id=1, source_target_pairs={{0,16},{4,20},{8,24},{12,28},{16,0},{20,4},{24,8},{28,12},{1,17},{... | collective-permute-start | bytes 294920 | tf_op jit(solution)/shard_map/ppermute | solution.py:711
  74.5 8.9 %collective-permute-done.11.other_ref = bf16[128,384]{1,0:T(8,128)(2,1)S(1)} collective-permute-done((bf16[128,384]{1,0:T(8,128)(2,1)S(1)}, bf16[128,384]{1,0:T(8,128)(2,1)S(1)}, u32[]{:S(2)}, u32[]{:S(2)}) %collective-permute-start.11) | collective-permute-done | bytes 98336 | tf_op jit(solution)/shard_map/ppermute | solution.py:711
  (61 shorter events, 6.0 us)
Async XLA Ops:
  0.6 19.5 %copy-start = (bf16[2,64,1536]{2,1,0:T(8,128)(2,1)S(1)}, bf16[2,64,1536]{2,1,0:T(8,128)(2,1)}, u32[]{:S(2)}) copy-start(bf16[2,64,1536]{2,1,0:T(8,128)(2,1)} %drafts_ref.1) | copy-start | bytes 1179652
  0.6 12.7 %copy-start.3 = (s32[2,64,4]{1,2,0:T(4,128)S(1)}, s32[2,64,4]{1,2,0:T(4,128)}, u32[]{:S(2)}) copy-start(s32[2,64,4]{1,2,0:T(4,128)} %param.27) | copy-start | bytes 6148
  0.7 19.5 %copy-start.1 = (bf16[1536,32]{0,1:T(8,128)(2,1)S(1)}, bf16[1536,32]{0,1:T(8,128)(2,1)}, u32[]{:S(2)}) copy-start(bf16[1536,32]{0,1:T(8,128)(2,1)} %param.26) | copy-start | bytes 294916
  0.7 19.5 %copy-start.2 = (f32[1536]{0:T(1024)S(1)}, f32[1536]{0:T(1024)}, u32[]{:S(2)}) copy-start(f32[1536]{0:T(1024)} %gain_ref.1) | copy-start | bytes 18436
  7.7 1.8 %collective-permute-start = (bf16[64,1536]{1,0:T(8,128)(2,1)}, bf16[64,1536]{1,0:T(8,128)(2,1)S(1)}, u32[]{:S(2)}, u32[]{:S(2)}) collective-permute-start(bf16[64,1536]{1,0:T(8,128)(2,1)} %get-tuple-element.20), channel_id=1, source_target_pairs={{0,1},{1,0},{2,3},{3,2},{4,5},{5,4},{6,7},{7,6},{8,9},{9,8},{10,11... | collective-permute-start | bytes 589832 | tf_op jit(solution)/shard_map/ppermute | solution.py:613
  10.5 8.1 %collective-permute-start.1 = (bf16[64,1536]{1,0:T(8,128)(2,1)S(1)}, bf16[64,1536]{1,0:T(8,128)(2,1)S(1)}, u32[]{:S(2)}, u32[]{:S(2)}) collective-permute-start(bf16[64,1536]{1,0:T(8,128)(2,1)S(1)} %add_convert_fusion.1), channel_id=1, source_target_pairs={{0,2},{1,3},{2,0},{3,1},{4,6},{5,7},{6,4},{7,5},{8,10},{9,11},{10,... | collective-permute-start | bytes 589832 | tf_op jit(solution)/shard_map/ppermute | solution.py:614
  18.6 1.5 %collective-permute-start.2 = (bf16[64,1536]{1,0:T(8,128)(2,1)S(1)}, bf16[64,1536]{1,0:T(8,128)(2,1)S(1)}, u32[]{:S(2)}, u32[]{:S(2)}) collective-permute-start(bf16[64,1536]{1,0:T(8,128)(2,1)S(1)} %add_convert_fusion.half_ref), channel_id=1, source_target_pairs={{0,1},{1,0},{2,3},{3,2},{4,5},{5,4},{6,7},{7,6},{8,9},{9,8},{10,11... | collective-permute-start | bytes 589832 | tf_op jit(solution)/shard_map/ppermute | solution.py:615
  21.6 9.1 %collective-permute-start.3 = (bf16[32,1536]{1,0:T(8,128)(2,1)S(1)}, bf16[32,1536]{1,0:T(8,128)(2,1)S(1)}, u32[]{:S(2)}, u32[]{:S(2)}) collective-permute-start(bf16[32,1536]{1,0:T(8,128)(2,1)S(1)} %get-tuple-element.21), channel_id=1, source_target_pairs={{0,4},{4,0},{8,12},{12,8},{16,20},{20,16},{24,28},{28,24},{1,5},{5... | collective-permute-start | bytes 294920 | tf_op jit(solution)/shard_map/ppermute | solution.py:622
  24.1 9.3 %collective-permute-start.4 = (bf16[32,1536]{1,0:T(8,128)(2,1)S(1)}, bf16[32,1536]{1,0:T(8,128)(2,1)S(1)}, u32[]{:S(2)}, u32[]{:S(2)}) collective-permute-start(bf16[32,1536]{1,0:T(8,128)(2,1)S(1)} %get-tuple-element.25), channel_id=1, source_target_pairs={{0,8},{4,12},{8,0},{12,4},{16,24},{20,28},{24,16},{28,20},{1,9},{5... | collective-permute-start | bytes 294920 | tf_op jit(solution)/shard_map/ppermute | solution.py:622
  25.7 15.8 %collective-permute-start.5 = (bf16[32,1536]{1,0:T(8,128)(2,1)S(1)}, bf16[32,1536]{1,0:T(8,128)(2,1)S(1)}, u32[]{:S(2)}, u32[]{:S(2)}) collective-permute-start(bf16[32,1536]{1,0:T(8,128)(2,1)S(1)} %get-tuple-element.26), channel_id=1, source_target_pairs={{0,16},{4,20},{8,24},{12,28},{16,0},{20,4},{24,8},{28,12},{1,17},{... | collective-permute-start | bytes 294920 | tf_op jit(solution)/shard_map/ppermute | solution.py:622
  27.7 15.3 %collective-permute-start.6 = (bf16[32,1536]{1,0:T(8,128)(2,1)S(1)}, bf16[32,1536]{1,0:T(8,128)(2,1)S(1)}, u32[]{:S(2)}, u32[]{:S(2)}) collective-permute-start(bf16[32,1536]{1,0:T(8,128)(2,1)S(1)} %get-tuple-element.27), channel_id=1, source_target_pairs={{0,20},{4,16},{8,28},{12,24},{16,4},{20,0},{24,12},{28,8},{1,21},{... | collective-permute-start | bytes 294920 | tf_op jit(solution)/shard_map/ppermute | solution.py:622
  29.3 13.7 %collective-permute-start.7 = (bf16[32,1536]{1,0:T(8,128)(2,1)S(1)}, bf16[32,1536]{1,0:T(8,128)(2,1)S(1)}, u32[]{:S(2)}, u32[]{:S(2)}) collective-permute-start(bf16[32,1536]{1,0:T(8,128)(2,1)S(1)} %get-tuple-element.28), channel_id=1, source_target_pairs={{0,24},{4,28},{8,16},{12,20},{16,8},{20,12},{24,0},{28,4},{1,25},{... | collective-permute-start | bytes 294920 | tf_op jit(solution)/shard_map/ppermute | solution.py:622
  30.7 12.3 %collective-permute-start.8 = (bf16[32,1536]{1,0:T(8,128)(2,1)S(1)}, bf16[32,1536]{1,0:T(8,128)(2,1)S(1)}, u32[]{:S(2)}, u32[]{:S(2)}) collective-permute-start(bf16[32,1536]{1,0:T(8,128)(2,1)S(1)} %get-tuple-element.29), channel_id=1, source_target_pairs={{0,28},{4,24},{8,20},{12,16},{16,12},{20,8},{24,4},{28,0},{1,29},{... | collective-permute-start | bytes 294920 | tf_op jit(solution)/shard_map/ppermute | solution.py:622
  33.4 10.7 %collective-permute-start.9 = (bf16[32,1536]{1,0:T(8,128)(2,1)S(1)}, bf16[32,1536]{1,0:T(8,128)(2,1)S(1)}, u32[]{:S(2)}, u32[]{:S(2)}) collective-permute-start(bf16[32,1536]{1,0:T(8,128)(2,1)S(1)} %get-tuple-element.30), channel_id=1, source_target_pairs={{0,12},{4,8},{8,4},{12,0},{16,28},{20,24},{24,20},{28,16},{1,13},{... | collective-permute-start | bytes 294920 | tf_op jit(solution)/shard_map/ppermute | solution.py:622
  33.4 6.4 %slice-start = ((s8[9437184]{0:T(1024)(128)(4,1)}), s8[4194304]{0:T(1024)(128)(4,1)S(1)}, s32[]{:S(2)}) async-start(s8[9437184]{0:T(1024)(128)(4,1)} %bitcast.57), calls=%async_computation.2 | async-start | bytes 8388608
  33.4 6.4 %slice-start.1 = ((s8[9437184]{0:T(1024)(128)(4,1)}), s8[4194304]{0:T(1024)(128)(4,1)S(1)}, s32[]{:S(2)}) async-start(s8[9437184]{0:T(1024)(128)(4,1)} %bitcast.57), calls=%async_computation.3 | async-start | bytes 8388608
  39.2 1.2 %slice-start.2 = ((s8[9437184]{0:T(1024)(128)(4,1)}), s8[1048576]{0:T(1024)(128)(4,1)S(1)}, s32[]{:S(2)}) async-start(s8[9437184]{0:T(1024)(128)(4,1)} %bitcast.57), calls=%async_computation.4 | async-start | bytes 2097152
  44.1 9.5 %copy-start.5 = (s32[2]{0:T(128)S(1)}, s32[2]{0:T(128)}, u32[]{:S(2)}) copy-start(s32[2]{0:T(128)} %param.31) | copy-start | bytes 28
  44.1 9.7 %copy-start.4 = (s32[2,64]{1,0:T(2,128)S(1)}, s32[2,64]{1,0:T(2,128)}, u32[]{:S(2)}) copy-start(s32[2,64]{1,0:T(2,128)} %param.30) | copy-start | bytes 1540
  48.2 18.9 %all-to-all-start = ((bf16[16,64,384]{2,1,0:T(8,128)(2,1)}), bf16[16,64,384]{2,1,0:T(8,128)(2,1)S(1)}, u32[]{:S(2)}, u32[]{:S(2)}) async-start(bf16[16,64,384]{2,1,0:T(8,128)(2,1)} %bitcast.12), calls=%async_computation | async-start | bytes 1572864 | tf_op jit(solution)/shard_map/all_to_all | solution.py:695
  54.1 9.1 %collective-permute-start.10 = (f32[16,128]{1,0:T(8,128)S(1)}, f32[16,128]{1,0:T(8,128)S(1)}, u32[]{:S(2)}, u32[]{:S(2)}) collective-permute-start(f32[16,128]{1,0:T(8,128)S(1)} %concatenate.9.own_ref), channel_id=1, source_target_pairs={{0,16},{4,20},{8,24},{12,28},{16,0},{20,4},{24,8},{28,12},{1,17},{... | collective-permute-start | bytes 24584 | tf_op jit(solution)/shard_map/ppermute | solution.py:681
  68.3 15.1 %all-to-all-start.1 = ((bf16[8,2,16,384]{3,2,1,0:T(8,128)(2,1)}), bf16[8,2,16,384]{3,2,1,0:T(8,128)(2,1)S(1)}, u32[]{:S(2)}, u32[]{:S(2)}) async-start(bf16[8,2,16,384]{3,2,1,0:T(8,128)(2,1)} %bitcast.32), calls=%async_computation.1 | async-start | bytes 393216 | tf_op jit(solution)/shard_map/all_to_all | solution.py:729
  71.7 11.7 %collective-permute-start.11 = (bf16[128,384]{1,0:T(8,128)(2,1)S(1)}, bf16[128,384]{1,0:T(8,128)(2,1)S(1)}, u32[]{:S(2)}, u32[]{:S(2)}) collective-permute-start(bf16[128,384]{1,0:T(8,128)(2,1)S(1)} %get-tuple-element.34), channel_id=1, source_target_pairs={{0,16},{4,20},{8,24},{12,28},{16,0},{20,4},{24,8},{28,12},{1,17},{... | collective-permute-start | bytes 294920 | tf_op jit(solution)/shard_map/ppermute | solution.py:711

commit v7 on v6

--- a/solution.py
+++ b/solution.py
@@ -19,7 +19,7 @@
 LOG2E = 1.4426950408889634
 BLOCK = 1536
 WHOLE_VMEM = 60 * 1024 * 1024
-SOME_VMEM = 20 * 1024 * 1024
+SOME_VMEM = 12 * 1024 * 1024
 
 
 def rms_norm(values, gain_vec):

time: 84.5 us -> 84.8 us (level)
  waiting for transfers between devices: 30.1 us -> 28.6 us
  starting transfers between devices: 28.3 us -> 29.5 us
    ppermute x1, starting transfers between devices: 1.31 us -> 2.28 us  [on_device(): partner = lax.ppermute(own, 'req', across)]
    ppermute x1, waiting for transfers between devices: 7.79 us -> 6.81 us  [on_device(): partner = lax.ppermute(own, 'req', across)]
where the time goes in v7:
time: 84.8 us; the launch traced here: 84 us
  starting transfers between devices  29.5 us (35%)
  waiting for transfers between devices  28.6 us (34%)
  Pallas kernels  15.4 us (18%)
  local copies, waits for them, and re-layouts  7.73 us (9%)
  other arithmetic  1.73 us (2%)
  between operations  0.91 us (1%)
    ppermute x7, starting transfers between devices, on_device(): lax.ppermute(sent[step], 'req', [(i, i ^ step) for i in range(req_count)])  11.8 us
    ppermute x1, waiting for transfers between devices, on_device(): other_sum = lax.ppermute(relay, 'req', across)  8.9 us
    pallas_call x1, Pallas kernels, attention_part(): pl.pallas_call(functools.partial(attention_kernel, tp_count), out_shape=[...  6.98 us
    ppermute x1, waiting for transfers between devices, on_device(): partner = lax.ppermute(own, 'req', across)  6.81 us
    dynamic_slice x1, local copies, waits for them, and re-layouts, on_device(): own_in = lax.dynamic_slice_in_dim(w_in, begin, 2, 0).transpose(0, 2, 1, 3)  5.75 us
    all_to_all x1, starting transfers between devices, on_device(): lax.all_to_all(produced.reshape(side * tp_count, -1, quarter), ('req', 't...  5.64 us
    ppermute x1, waiting for transfers between devices, on_device(): half = added(chip, lax.ppermute(chip, 'tp', far))  4.83 us
    pallas_call x1, Pallas kernels, expert_rows(): pl.pallas_call(expert_kernel, out_shape=jax.ShapeDtypeStruct((groups // 2...  4.15 us
  transfers between devices with their start and end apart: 14, of which 8 were waited for; matrix products, arithmetic and copies ran while one was open for 9% of the time, Pallas kernels for 1%

profile of v7, /device:TPU:0, one launch (start us, length us, event | category | flops | bytes accessed | tf_op | source)
XLA Modules:
  0.0 84.0 jit_solution(10178867254636059998)
XLA Ops:
  0.7 7.0 %attention.1 = (bf16[64,1536]{1,0:T(8,128)(2,1)}, bf16[64,1536]{1,0:T(8,128)(2,1)}) custom-call(s32[2]{0:T(128)} %lengths_ref.1, f32[1536]{0:T(1024)} %gain_hbm.1, s32[2,64]{1,0:T(2,128)} %depths_hbm.1, s32[2,64,64]{2,1,0:T(8,128)} %mask_hbm.1, bf16[2,64,1536]{2,1,0:T(8,128)(2,1)} %drafts_ref.1, bf16[1536,384]{1,0:T(8,128)(2,1)} %wq_hbm.1, ...), custom_call_target="tpu_custom_call" | custom-call | tf_op jit(solution)/shard_map/attention/pallas_call | solution.py:244
  8.2 1.3 %collective-permute-done = bf16[64,1536]{1,0:T(8,128)(2,1)S(1)} collective-permute-done((bf16[64,1536]{1,0:T(8,128)(2,1)}, bf16[64,1536]{1,0:T(8,128)(2,1)S(1)}, u32[]{:S(2)}, u32[]{:S(2)}) %collective-permute-start) | collective-permute-done | bytes 196640 | tf_op jit(solution)/shard_map/ppermute | solution.py:613
  10.5 2.9 %collective-permute-start.1 = (bf16[64,1536]{1,0:T(8,128)(2,1)S(1)}, bf16[64,1536]{1,0:T(8,128)(2,1)S(1)}, u32[]{:S(2)}, u32[]{:S(2)}) collective-permute-start(bf16[64,1536]{1,0:T(8,128)(2,1)S(1)} %add_convert_fusion.1), channel_id=1, source_target_pairs={{0,2},{1,3},{2,0},{3,1},{4,6},{5,7},{6,4},{7,5},{8,10},{9,11},{10,... | collective-permute-start | bytes 589832 | tf_op jit(solution)/shard_map/ppermute | solution.py:614
  13.8 4.8 %collective-permute-done.1 = bf16[64,1536]{1,0:T(8,128)(2,1)S(1)} collective-permute-done((bf16[64,1536]{1,0:T(8,128)(2,1)S(1)}, bf16[64,1536]{1,0:T(8,128)(2,1)S(1)}, u32[]{:S(2)}, u32[]{:S(2)}) %collective-permute-start.1) | collective-permute-done | bytes 196640 | tf_op jit(solution)/shard_map/ppermute | solution.py:614
  19.0 1.1 %collective-permute-done.2.other_ref = bf16[64,1536]{1,0:T(8,128)(2,1)S(1)} collective-permute-done((bf16[64,1536]{1,0:T(8,128)(2,1)S(1)}, bf16[64,1536]{1,0:T(8,128)(2,1)S(1)}, u32[]{:S(2)}, u32[]{:S(2)}) %collective-permute-start.2) | collective-permute-done | bytes 196640 | tf_op jit(solution)/shard_map/ppermute | solution.py:615
  20.2 1.4 %dispatch.1 = (f32[128,32]{1,0:T(8,128)S(1)}, bf16[32,1536]{1,0:T(8,128)(2,1)S(1)}, bf16[32,1536]{1,0:T(8,128)(2,1)S(1)}, bf16[32,1536]{1,0:T(8,128)(2,1)S(1)}, ...) custom-call(s32[6]{0:T(128)S(1)} %stack.27.place_ref, ...), custom_call_target="tpu_custom_call" | custom-call | tf_op jit(solution)/shard_map/dispatch/pallas_call | solution.py:316
  21.6 1.8 %collective-permute-start.3 = (bf16[32,1536]{1,0:T(8,128)(2,1)S(1)}, bf16[32,1536]{1,0:T(8,128)(2,1)S(1)}, u32[]{:S(2)}, u32[]{:S(2)}) collective-permute-start(bf16[32,1536]{1,0:T(8,128)(2,1)S(1)} %get-tuple-element.21), channel_id=1, source_target_pairs={{0,4},{4,0},{8,12},{12,8},{16,20},{20,16},{24,28},{28,24},{1,5},{5... | collective-permute-start | bytes 294920 | tf_op jit(solution)/shard_map/ppermute | solution.py:622
  23.4 1.6 %collective-permute-start.4 = (bf16[32,1536]{1,0:T(8,128)(2,1)S(1)}, bf16[32,1536]{1,0:T(8,128)(2,1)S(1)}, u32[]{:S(2)}, u32[]{:S(2)}) collective-permute-start(bf16[32,1536]{1,0:T(8,128)(2,1)S(1)} %get-tuple-element.25), channel_id=1, source_target_pairs={{0,8},{4,12},{8,0},{12,4},{16,24},{20,28},{24,16},{28,20},{1,9},{5... | collective-permute-start | bytes 294920 | tf_op jit(solution)/shard_map/ppermute | solution.py:622
  25.0 2.6 %collective-permute-start.5 = (bf16[32,1536]{1,0:T(8,128)(2,1)S(1)}, bf16[32,1536]{1,0:T(8,128)(2,1)S(1)}, u32[]{:S(2)}, u32[]{:S(2)}) collective-permute-start(bf16[32,1536]{1,0:T(8,128)(2,1)S(1)} %get-tuple-element.26), channel_id=1, source_target_pairs={{0,16},{4,20},{8,24},{12,28},{16,0},{20,4},{24,8},{28,12},{1,17},{... | collective-permute-start | bytes 294920 | tf_op jit(solution)/shard_map/ppermute | solution.py:622
  27.7 1.4 %collective-permute-start.6 = (bf16[32,1536]{1,0:T(8,128)(2,1)S(1)}, bf16[32,1536]{1,0:T(8,128)(2,1)S(1)}, u32[]{:S(2)}, u32[]{:S(2)}) collective-permute-start(bf16[32,1536]{1,0:T(8,128)(2,1)S(1)} %get-tuple-element.27), channel_id=1, source_target_pairs={{0,20},{4,16},{8,28},{12,24},{16,4},{20,0},{24,12},{28,8},{1,21},{... | collective-permute-start | bytes 294920 | tf_op jit(solution)/shard_map/ppermute | solution.py:622
  29.1 2.3 %collective-permute-start.7 = (bf16[32,1536]{1,0:T(8,128)(2,1)S(1)}, bf16[32,1536]{1,0:T(8,128)(2,1)S(1)}, u32[]{:S(2)}, u32[]{:S(2)}) collective-permute-start(bf16[32,1536]{1,0:T(8,128)(2,1)S(1)} %get-tuple-element.28), channel_id=1, source_target_pairs={{0,24},{4,28},{8,16},{12,20},{16,8},{20,12},{24,0},{28,4},{1,25},{... | collective-permute-start | bytes 294920 | tf_op jit(solution)/shard_map/ppermute | solution.py:622
  31.4 1.5 %collective-permute-start.8 = (bf16[32,1536]{1,0:T(8,128)(2,1)S(1)}, bf16[32,1536]{1,0:T(8,128)(2,1)S(1)}, u32[]{:S(2)}, u32[]{:S(2)}) collective-permute-start(bf16[32,1536]{1,0:T(8,128)(2,1)S(1)} %get-tuple-element.29), channel_id=1, source_target_pairs={{0,28},{4,24},{8,20},{12,16},{16,12},{20,8},{24,4},{28,0},{1,29},{... | collective-permute-start | bytes 294920 | tf_op jit(solution)/shard_map/ppermute | solution.py:622
  33.4 5.7 %constant_dynamic-slice_fusion = bf16[2,1536,2,384]{3,2,1,0:T(2,128)(2,1)S(1)} fusion(bf16[8,1536,2,384]{3,2,1,0:T(2,128)(2,1)} %param.28, s32[]{:T(128)S(6)} %select_n.86), kind=kLoop, calls=%fused_computation.25 | loop fusion | bytes 9437188 | tf_op jit(solution)/shard_map/dynamic_slice | solution.py:652
  40.4 1.0 %fetch.1 = (bf16[2,2,1536,384]{3,2,1,0:T(8,128)(2,1)S(1)}, bf16[2,384,1536]{2,1,0:T(8,128)(2,1)S(1)}) custom-call(s32[6]{0:T(128)S(1)} %stack.27.place_ref, bf16[2,2,1536,384]{3,2,1,0:T(8,128)(2,1)S(1)} %bitcast.56, bf16[8,384,1536]{2,1,0:T(8,128)(2,1)S(1)} %bitcast.58), custom_call_target="tpu_custom_call" | custom-call | tf_op jit(solution)/shard_map/fetch/pallas_call | solution.py:346
  41.4 1.2 %collective-permute-done.6.rest_3_ = bf16[32,1536]{1,0:T(8,128)(2,1)S(1)} collective-permute-done((bf16[32,1536]{1,0:T(8,128)(2,1)S(1)}, bf16[32,1536]{1,0:T(8,128)(2,1)S(1)}, u32[]{:S(2)}, u32[]{:S(2)}) %collective-permute-start.6) | collective-permute-done | bytes 98336 | tf_op jit(solution)/shard_map/ppermute | solution.py:622
  43.6 4.2 %experts.1 = bf16[4,4,2,32,384]{4,3,2,1,0:T(8,128)(2,1)} custom-call(s32[6]{0:T(128)S(1)} %stack.27.place_ref, bf16[2,2,1536,384]{3,2,1,0:T(8,128)(2,1)S(1)} %get-tuple-element.23.wi, bf16[768,1536]{1,0:T(8,128)(2,1)S(1)} %bitcast.59, bf16[32,1536]{1,0:T(8,128)(2,1)S(1)} %collective-permute-done.3.rest_0_, ...), custom_call_target="tpu_custom_call" | custom-call | tf_op jit(solution)/shard_map/experts/pallas_call | solution.py:387
  47.7 5.6 %all-to-all-start = ((bf16[16,64,384]{2,1,0:T(8,128)(2,1)}), bf16[16,64,384]{2,1,0:T(8,128)(2,1)S(1)}, u32[]{:S(2)}, u32[]{:S(2)}) async-start(bf16[16,64,384]{2,1,0:T(8,128)(2,1)} %bitcast.12), calls=%async_computation | async-start | bytes 1572864 | tf_op jit(solution)/shard_map/all_to_all | solution.py:695
  53.8 2.3 %collective-permute-start.10 = (f32[16,128]{1,0:T(8,128)S(1)}, f32[16,128]{1,0:T(8,128)S(1)}, u32[]{:S(2)}, u32[]{:S(2)}) collective-permute-start(f32[16,128]{1,0:T(8,128)S(1)} %concatenate.9.own_ref), channel_id=1, source_target_pairs={{0,16},{4,20},{8,24},{12,28},{16,0},{20,4},{24,8},{28,12},{1,17},{... | collective-permute-start | bytes 24584 | tf_op jit(solution)/shard_map/ppermute | solution.py:681
  56.2 6.8 %collective-permute-done.10.partner_ref = f32[16,128]{1,0:T(8,128)S(1)} collective-permute-done((f32[16,128]{1,0:T(8,128)S(1)}, f32[16,128]{1,0:T(8,128)S(1)}, u32[]{:S(2)}, u32[]{:S(2)}) %collective-permute-start.10) | collective-permute-done | bytes 8224 | tf_op jit(solution)/shard_map/ppermute | solution.py:681
  63.3 3.6 %all-to-all-done.rows_ref = bf16[16,64,384]{2,1,0:T(8,128)(2,1)S(1)} async-done(((bf16[16,64,384]{2,1,0:T(8,128)(2,1)}), bf16[16,64,384]{2,1,0:T(8,128)(2,1)S(1)}, u32[]{:S(2)}, u32[]{:S(2)}) %all-to-all-start) | async-done | bytes 786464 | tf_op jit(solution)/shard_map/all_to_all | solution.py:695
  66.9 1.2 %gather.1 = (bf16[128,384]{1,0:T(8,128)(2,1)S(1)}, f32[128,384]{1,0:T(8,128)S(1)}, bf16[16,16,384]{2,1,0:T(8,128)(2,1)}) custom-call(bf16[16,64,384]{2,1,0:T(8,128)(2,1)S(1)} %all-to-all-done.rows_ref, f32[16,128]{1,0:T(8,128)S(1)} %concatenate.9.own_ref, f32[16,128]{1,0:T(8,128)S(1)} %collective-permute-done.10.partner_ref, ...), custom_call_target="tpu_custom_call" | custom-call | tf_op jit(solution)/shard_map/gather/pallas_call | solution.py:493
  68.1 3.4 %all-to-all-start.1 = ((bf16[8,2,16,384]{3,2,1,0:T(8,128)(2,1)}), bf16[8,2,16,384]{3,2,1,0:T(8,128)(2,1)S(1)}, u32[]{:S(2)}, u32[]{:S(2)}) async-start(bf16[8,2,16,384]{3,2,1,0:T(8,128)(2,1)} %bitcast.32), calls=%async_computation.1 | async-start | bytes 393216 | tf_op jit(solution)/shard_map/all_to_all | solution.py:729
  71.5 2.9 %collective-permute-start.11 = (bf16[128,384]{1,0:T(8,128)(2,1)S(1)}, bf16[128,384]{1,0:T(8,128)(2,1)S(1)}, u32[]{:S(2)}, u32[]{:S(2)}) collective-permute-start(bf16[128,384]{1,0:T(8,128)(2,1)S(1)} %get-tuple-element.34), channel_id=1, source_target_pairs={{0,16},{4,20},{8,24},{12,28},{16,0},{20,4},{24,8},{28,12},{1,17},{... | collective-permute-start | bytes 294920 | tf_op jit(solution)/shard_map/ppermute | solution.py:711
  74.4 8.9 %collective-permute-done.11.other_ref = bf16[128,384]{1,0:T(8,128)(2,1)S(1)} collective-permute-done((bf16[128,384]{1,0:T(8,128)(2,1)S(1)}, bf16[128,384]{1,0:T(8,128)(2,1)S(1)}, u32[]{:S(2)}, u32[]{:S(2)}) %collective-permute-start.11) | collective-permute-done | bytes 98336 | tf_op jit(solution)/shard_map/ppermute | solution.py:711
  (61 shorter events, 6.4 us)
Async XLA Ops:
  0.6 19.5 %copy-start = (bf16[2,64,1536]{2,1,0:T(8,128)(2,1)S(1)}, bf16[2,64,1536]{2,1,0:T(8,128)(2,1)}, u32[]{:S(2)}) copy-start(bf16[2,64,1536]{2,1,0:T(8,128)(2,1)} %drafts_ref.1) | copy-start | bytes 1179652
  0.6 12.7 %copy-start.3 = (s32[2,64,4]{1,2,0:T(4,128)S(1)}, s32[2,64,4]{1,2,0:T(4,128)}, u32[]{:S(2)}) copy-start(s32[2,64,4]{1,2,0:T(4,128)} %param.27) | copy-start | bytes 6148
  0.7 19.5 %copy-start.1 = (bf16[1536,32]{0,1:T(8,128)(2,1)S(1)}, bf16[1536,32]{0,1:T(8,128)(2,1)}, u32[]{:S(2)}) copy-start(bf16[1536,32]{0,1:T(8,128)(2,1)} %param.26) | copy-start | bytes 294916
  0.7 19.5 %copy-start.2 = (f32[1536]{0:T(1024)S(1)}, f32[1536]{0:T(1024)}, u32[]{:S(2)}) copy-start(f32[1536]{0:T(1024)} %gain_ref.1) | copy-start | bytes 18436
  7.7 1.8 %collective-permute-start = (bf16[64,1536]{1,0:T(8,128)(2,1)}, bf16[64,1536]{1,0:T(8,128)(2,1)S(1)}, u32[]{:S(2)}, u32[]{:S(2)}) collective-permute-start(bf16[64,1536]{1,0:T(8,128)(2,1)} %get-tuple-element.20), channel_id=1, source_target_pairs={{0,1},{1,0},{2,3},{3,2},{4,5},{5,4},{6,7},{7,6},{8,9},{9,8},{10,11... | collective-permute-start | bytes 589832 | tf_op jit(solution)/shard_map/ppermute | solution.py:613
  10.5 8.1 %collective-permute-start.1 = (bf16[64,1536]{1,0:T(8,128)(2,1)S(1)}, bf16[64,1536]{1,0:T(8,128)(2,1)S(1)}, u32[]{:S(2)}, u32[]{:S(2)}) collective-permute-start(bf16[64,1536]{1,0:T(8,128)(2,1)S(1)} %add_convert_fusion.1), channel_id=1, source_target_pairs={{0,2},{1,3},{2,0},{3,1},{4,6},{5,7},{6,4},{7,5},{8,10},{9,11},{10,... | collective-permute-start | bytes 589832 | tf_op jit(solution)/shard_map/ppermute | solution.py:614
  18.6 1.5 %collective-permute-start.2 = (bf16[64,1536]{1,0:T(8,128)(2,1)S(1)}, bf16[64,1536]{1,0:T(8,128)(2,1)S(1)}, u32[]{:S(2)}, u32[]{:S(2)}) collective-permute-start(bf16[64,1536]{1,0:T(8,128)(2,1)S(1)} %add_convert_fusion.half_ref), channel_id=1, source_target_pairs={{0,1},{1,0},{2,3},{3,2},{4,5},{5,4},{6,7},{7,6},{8,9},{9,8},{10,11... | collective-permute-start | bytes 589832 | tf_op jit(solution)/shard_map/ppermute | solution.py:615
  21.6 9.8 %collective-permute-start.3 = (bf16[32,1536]{1,0:T(8,128)(2,1)S(1)}, bf16[32,1536]{1,0:T(8,128)(2,1)S(1)}, u32[]{:S(2)}, u32[]{:S(2)}) collective-permute-start(bf16[32,1536]{1,0:T(8,128)(2,1)S(1)} %get-tuple-element.21), channel_id=1, source_target_pairs={{0,4},{4,0},{8,12},{12,8},{16,20},{20,16},{24,28},{28,24},{1,5},{5... | collective-permute-start | bytes 294920 | tf_op jit(solution)/shard_map/ppermute | solution.py:622
  23.4 9.4 %collective-permute-start.4 = (bf16[32,1536]{1,0:T(8,128)(2,1)S(1)}, bf16[32,1536]{1,0:T(8,128)(2,1)S(1)}, u32[]{:S(2)}, u32[]{:S(2)}) collective-permute-start(bf16[32,1536]{1,0:T(8,128)(2,1)S(1)} %get-tuple-element.25), channel_id=1, source_target_pairs={{0,8},{4,12},{8,0},{12,4},{16,24},{20,28},{24,16},{28,20},{1,9},{5... | collective-permute-start | bytes 294920 | tf_op jit(solution)/shard_map/ppermute | solution.py:622
  25.0 16.4 %collective-permute-start.5 = (bf16[32,1536]{1,0:T(8,128)(2,1)S(1)}, bf16[32,1536]{1,0:T(8,128)(2,1)S(1)}, u32[]{:S(2)}, u32[]{:S(2)}) collective-permute-start(bf16[32,1536]{1,0:T(8,128)(2,1)S(1)} %get-tuple-element.26), channel_id=1, source_target_pairs={{0,16},{4,20},{8,24},{12,28},{16,0},{20,4},{24,8},{28,12},{1,17},{... | collective-permute-start | bytes 294920 | tf_op jit(solution)/shard_map/ppermute | solution.py:622
  27.7 15.0 %collective-permute-start.6 = (bf16[32,1536]{1,0:T(8,128)(2,1)S(1)}, bf16[32,1536]{1,0:T(8,128)(2,1)S(1)}, u32[]{:S(2)}, u32[]{:S(2)}) collective-permute-start(bf16[32,1536]{1,0:T(8,128)(2,1)S(1)} %get-tuple-element.27), channel_id=1, source_target_pairs={{0,20},{4,16},{8,28},{12,24},{16,4},{20,0},{24,12},{28,8},{1,21},{... | collective-permute-start | bytes 294920 | tf_op jit(solution)/shard_map/ppermute | solution.py:622
  29.1 13.6 %collective-permute-start.7 = (bf16[32,1536]{1,0:T(8,128)(2,1)S(1)}, bf16[32,1536]{1,0:T(8,128)(2,1)S(1)}, u32[]{:S(2)}, u32[]{:S(2)}) collective-permute-start(bf16[32,1536]{1,0:T(8,128)(2,1)S(1)} %get-tuple-element.28), channel_id=1, source_target_pairs={{0,24},{4,28},{8,16},{12,20},{16,8},{20,12},{24,0},{28,4},{1,25},{... | collective-permute-start | bytes 294920 | tf_op jit(solution)/shard_map/ppermute | solution.py:622
  31.4 11.3 %collective-permute-start.8 = (bf16[32,1536]{1,0:T(8,128)(2,1)S(1)}, bf16[32,1536]{1,0:T(8,128)(2,1)S(1)}, u32[]{:S(2)}, u32[]{:S(2)}) collective-permute-start(bf16[32,1536]{1,0:T(8,128)(2,1)S(1)} %get-tuple-element.29), channel_id=1, source_target_pairs={{0,28},{4,24},{8,20},{12,16},{16,12},{20,8},{24,4},{28,0},{1,29},{... | collective-permute-start | bytes 294920 | tf_op jit(solution)/shard_map/ppermute | solution.py:622
  32.8 10.7 %collective-permute-start.9 = (bf16[32,1536]{1,0:T(8,128)(2,1)S(1)}, bf16[32,1536]{1,0:T(8,128)(2,1)S(1)}, u32[]{:S(2)}, u32[]{:S(2)}) collective-permute-start(bf16[32,1536]{1,0:T(8,128)(2,1)S(1)} %get-tuple-element.30), channel_id=1, source_target_pairs={{0,12},{4,8},{8,4},{12,0},{16,28},{20,24},{24,20},{28,16},{1,13},{... | collective-permute-start | bytes 294920 | tf_op jit(solution)/shard_map/ppermute | solution.py:622
  33.4 6.4 %slice-start = ((s8[9437184]{0:T(1024)(128)(4,1)}), s8[4194304]{0:T(1024)(128)(4,1)S(1)}, s32[]{:S(2)}) async-start(s8[9437184]{0:T(1024)(128)(4,1)} %bitcast.57), calls=%async_computation.2 | async-start | bytes 8388608
  33.4 6.4 %slice-start.1 = ((s8[9437184]{0:T(1024)(128)(4,1)}), s8[4194304]{0:T(1024)(128)(4,1)S(1)}, s32[]{:S(2)}) async-start(s8[9437184]{0:T(1024)(128)(4,1)} %bitcast.57), calls=%async_computation.3 | async-start | bytes 8388608
  39.2 1.2 %slice-start.2 = ((s8[9437184]{0:T(1024)(128)(4,1)}), s8[1048576]{0:T(1024)(128)(4,1)S(1)}, s32[]{:S(2)}) async-start(s8[9437184]{0:T(1024)(128)(4,1)} %bitcast.57), calls=%async_computation.4 | async-start | bytes 2097152
  43.6 9.8 %copy-start.5 = (s32[2]{0:T(128)S(1)}, s32[2]{0:T(128)}, u32[]{:S(2)}) copy-start(s32[2]{0:T(128)} %param.31) | copy-start | bytes 28
  43.6 10.0 %copy-start.4 = (s32[2,64]{1,0:T(2,128)S(1)}, s32[2,64]{1,0:T(2,128)}, u32[]{:S(2)}) copy-start(s32[2,64]{1,0:T(2,128)} %param.30) | copy-start | bytes 1540
  47.7 19.2 %all-to-all-start = ((bf16[16,64,384]{2,1,0:T(8,128)(2,1)}), bf16[16,64,384]{2,1,0:T(8,128)(2,1)S(1)}, u32[]{:S(2)}, u32[]{:S(2)}) async-start(bf16[16,64,384]{2,1,0:T(8,128)(2,1)} %bitcast.12), calls=%async_computation | async-start | bytes 1572864 | tf_op jit(solution)/shard_map/all_to_all | solution.py:695
  53.8 9.1 %collective-permute-start.10 = (f32[16,128]{1,0:T(8,128)S(1)}, f32[16,128]{1,0:T(8,128)S(1)}, u32[]{:S(2)}, u32[]{:S(2)}) collective-permute-start(f32[16,128]{1,0:T(8,128)S(1)} %concatenate.9.own_ref), channel_id=1, source_target_pairs={{0,16},{4,20},{8,24},{12,28},{16,0},{20,4},{24,8},{28,12},{1,17},{... | collective-permute-start | bytes 24584 | tf_op jit(solution)/shard_map/ppermute | solution.py:681
  68.1 15.2 %all-to-all-start.1 = ((bf16[8,2,16,384]{3,2,1,0:T(8,128)(2,1)}), bf16[8,2,16,384]{3,2,1,0:T(8,128)(2,1)S(1)}, u32[]{:S(2)}, u32[]{:S(2)}) async-start(bf16[8,2,16,384]{3,2,1,0:T(8,128)(2,1)} %bitcast.32), calls=%async_computation.1 | async-start | bytes 393216 | tf_op jit(solution)/shard_map/all_to_all | solution.py:729
  71.5 11.8 %collective-permute-start.11 = (bf16[128,384]{1,0:T(8,128)(2,1)S(1)}, bf16[128,384]{1,0:T(8,128)(2,1)S(1)}, u32[]{:S(2)}, u32[]{:S(2)}) collective-permute-start(bf16[128,384]{1,0:T(8,128)(2,1)S(1)} %get-tuple-element.34), channel_id=1, source_target_pairs={{0,16},{4,20},{8,24},{12,28},{16,0},{20,4},{24,8},{28,12},{1,17},{... | collective-permute-start | bytes 294920 | tf_op jit(solution)/shard_map/ppermute | solution.py:711
